TPU v7x, 32 devices: a whole 2x2x4 slice. The times are simulated.
32 devices in a mesh: fsdp: 32 (over z, y, x, core).
Axes of the slice: x: 2, y: 2, z: 4, core: 2. Of those that a mesh axis runs over, the one named last changes fastest.
Arguments:
- tokens: bfloat16 [8192, 2048], P('fsdp'), may hold values from -6 to 6
- w_query: bfloat16 [2048, 2048], P('fsdp'), may hold values from -0.125 to 0.125
- w_key: bfloat16 [2048, 2048], P('fsdp'), may hold values from -0.125 to 0.125
- w_value: bfloat16 [2048, 2048], P('fsdp'), may hold values from -0.125 to 0.125
- w_out: bfloat16 [2048, 2048], P('fsdp'), may hold values from -2 to 2
- w_router: bfloat16 [2048, 16], P('fsdp'), may hold values from -0.0625 to 0.0625
- gain_attn: bfloat16 [2048], P('fsdp'), may hold values from 0.5 to 1.5
- gain_moe: bfloat16 [2048], P('fsdp'), may hold values from 0.5 to 1.5
- w_gate: bfloat16 [16384, 2048], P('fsdp'), may hold values from -0.125 to 0.125
- w_up: bfloat16 [16384, 2048], P('fsdp'), may hold values from -0.125 to 0.125
- w_down: bfloat16 [16384, 2048], P('fsdp'), may hold values from -0.75 to 0.75
- routes: int32 [8192, 8], P('fsdp'), may hold values from 0 to 15, all different within a row; in each aligned block of 256 rows (0 to 255, 256 to 511, ...) at most 192 rows name the same one
- doc_lengths: int32 [2, 4], replicated, may hold values from 1 to 2048, 4096 in all within a row
- clip_limit: float32 [16], replicated, may hold values from 3.5 to 7.5
- cotangent: bfloat16 [8192, 2048], P('fsdp'), may hold values from -6 to 6
Outputs:
- mixed: bfloat16 [8192, 2048], P('fsdp')
- grad_tokens: float32 [8192, 2048], P('fsdp')
- grad_query: float32 [2048, 2048], P('fsdp')
- grad_key: float32 [2048, 2048], P('fsdp')
- grad_value: float32 [2048, 2048], P('fsdp')
- grad_out: float32 [2048, 2048], P('fsdp')
- grad_router: float32 [2048, 16], P('fsdp')
- grad_gain_attn: float32 [2048], P('fsdp')
- grad_gain_moe: float32 [2048], P('fsdp')
- grad_gate: float32 [16384, 2048], P('fsdp')
- grad_up: float32 [16384, 2048], P('fsdp')
- grad_down: float32 [16384, 2048], P('fsdp')
- clipped_query: bfloat16 [2048, 2048], P('fsdp')
- clipped_key: bfloat16 [2048, 2048], P('fsdp')
Inputs may be any that keep to these rules, and one draw needn't show every extreme that they name: `routes`: each token names 8 different experts. Among the 256 tokens of one device no expert is named more than 192 times, a bound that some block reaches. `doc_lengths`: each row holds the lengths of the 4 documents of one packed sequence in order; a row sums to 4096 and its largest length is exactly 2048.
All inputs are finite; a program needn't handle non-finite values.
Results may differ from a plain program's by a relative error of at most 0.018.
Values may be sent and summed in bfloat16 or wider, within the bound.
A program may use at most 384 MiB of HBM per device.

v0:
```python
from functools import reduce

import jax
import jax.numpy as jnp
from jax import lax
from jax.sharding import PartitionSpec as P

HALF = 512


epsilon = 1e-05
masked = -1e30
highest = lax.Precision.HIGHEST


def passed_along(x, axis, by):
    length = lax.axis_size(axis)
    pairs = [(i, i + by) for i in range(length) if 0 <= i + by < length]
    return lax.ppermute(x, axis, pairs)


def swapped(block, axis, apart):
    count = lax.axis_size(axis)
    route = []
    for low in range(count):
        high = low | 1 << apart
        if high != low and high < count:
            route += [(low, high), (high, low)]
    return lax.ppermute(block, axis, route)


def rms_scale(source):
    return lax.rsqrt(jnp.mean(source * source, axis=-1, keepdims=True) + epsilon)


def norm_back(grad_normed, source, scale_rows, gain):
    unit_rows = source * scale_rows
    grad_unit = grad_normed * gain
    grad_gain = jnp.sum(grad_normed * unit_rows, axis=0)
    grad_source = scale_rows * (
        grad_unit - unit_rows * jnp.mean(grad_unit * unit_rows, axis=-1, keepdims=True)
    )
    return (grad_source, grad_gain)


def document_of(places, doc_lengths, seq_len):
    doc_ends = jnp.cumsum(doc_lengths, axis=1)
    seq_count = doc_lengths.shape[0]
    doc_count = doc_lengths.shape[1]
    sequence = places // seq_len
    within = places % seq_len
    picked = (sequence[:, None] == jnp.arange(seq_count, dtype=jnp.int32)[None, :]).astype(
        jnp.int32
    )
    ends_of = jnp.dot(picked, doc_ends)
    local_doc = jnp.sum((within[:, None] >= ends_of).astype(jnp.int32), axis=1)
    inside = (places >= 0) & (places < seq_count * seq_len)
    return jnp.where(inside, sequence * doc_count + local_doc, -1)


def contract(left, right, left_dim, right_dim):
    return lax.dot_general(
        left, right, (((left_dim,), (right_dim,)), ((), ())), preferred_element_type=jnp.float32
    )


def per_device(
    tokens,
    w_query,
    w_key,
    w_value,
    w_out,
    w_router,
    gain_attn,
    gain_moe,
    w_gate,
    w_up,
    w_down,
    routes,
    doc_lengths,
    clip_limit,
    cotangent,
):
    devices = lax.axis_size("fsdp")
    device = lax.axis_index("fsdp")
    tok_rows = tokens.shape[0]
    model_width = tokens.shape[1]
    head_count = clip_limit.shape[0]
    head_size = model_width // head_count
    experts = w_router.shape[1]
    top_count = routes.shape[1]
    seq_len = devices * tok_rows // doc_lengths.shape[0]
    score_scale = head_size ** (-0.5)
    gathered = (
        lax.all_gather(w_query, "fsdp", axis=0, tiled=True),
        lax.all_gather(w_key, "fsdp", axis=0, tiled=True),
        lax.all_gather(w_value, "fsdp", axis=0, tiled=True),
        lax.all_gather(w_out, "fsdp", axis=0, tiled=True),
        lax.all_gather(w_router, "fsdp", axis=0, tiled=True),
        lax.all_gather(gain_attn, "fsdp", axis=0, tiled=True),
        lax.all_gather(gain_moe, "fsdp", axis=0, tiled=True),
    )
    query_full, key_full, value_full, out_full, router_full, gain_one, gain_two = gathered
    token_values = tokens.astype(jnp.float32)
    scale_one = rms_scale(token_values)
    attn_gain = gain_one.astype(jnp.float32)
    normed_attn = (token_values * scale_one * attn_gain).astype(jnp.bfloat16)
    queries = jnp.dot(normed_attn, query_full, preferred_element_type=jnp.float32).astype(
        jnp.bfloat16
    )
    kv_own = jnp.concatenate(
        (
            jnp.dot(normed_attn, key_full, preferred_element_type=jnp.float32),
            jnp.dot(normed_attn, value_full, preferred_element_type=jnp.float32),
        ),
        axis=1,
    ).astype(jnp.bfloat16)
    reach_count = (HALF - 2) // tok_rows + 1
    offsets = list(range(reach_count, 0, -1)) + list(range(-1, -reach_count - 1, -1))
    arrived = [passed_along(kv_own, "fsdp", offset) for offset in offsets]
    kv_rows = jnp.concatenate(arrived[:reach_count] + [kv_own] + arrived[reach_count:], axis=0)
    ordered = offsets[:reach_count] + [0] + offsets[reach_count:]
    row_index = jnp.arange(tok_rows, dtype=jnp.int32)
    query_places = device * tok_rows + row_index
    key_places = jnp.concatenate([(device - offset) * tok_rows + row_index for offset in ordered])
    query_docs = document_of(query_places, doc_lengths, seq_len)
    key_docs = document_of(key_places, doc_lengths, seq_len)
    visible = (
        (query_docs[:, None] == key_docs[None, :])
        & (key_docs[None, :] >= 0)
        & (jnp.abs(query_places[:, None] - key_places[None, :]) < HALF)
    )
    key_count = kv_rows.shape[0]
    query_heads = queries.reshape(tok_rows, head_count, head_size)
    key_heads = kv_rows[:, :model_width].reshape(key_count, head_count, head_size)
    value_heads = kv_rows[:, model_width:].reshape(key_count, head_count, head_size)

    def scores_of():
        raw_scores = (
            jnp.einsum("qhd,khd->hqk", query_heads, key_heads, preferred_element_type=jnp.float32)
            * score_scale
        )
        return jnp.where(visible[None], raw_scores, masked)

    scores = scores_of()
    head_top = jnp.max(scores, axis=2, keepdims=True)
    exponents = jnp.exp(scores - head_top)
    totals = jnp.sum(exponents, axis=2, keepdims=True)
    log_total = head_top + jnp.log(totals)
    probs_low = (exponents / totals).astype(jnp.bfloat16)
    head_max = lax.pmax(jnp.max(head_top, axis=(1, 2)), "fsdp")
    context = (
        jnp.einsum("hqk,khd->qhd", probs_low, value_heads, preferred_element_type=jnp.float32)
        .reshape(tok_rows, model_width)
        .astype(jnp.bfloat16)
    )
    attended = token_values + jnp.dot(context, out_full, preferred_element_type=jnp.float32)
    factor = clip_limit / jnp.maximum(head_max, clip_limit)
    columns = jnp.repeat(jnp.sqrt(factor), head_size)
    clipped_query = (w_query.astype(jnp.float32) * columns[None, :]).astype(jnp.bfloat16)
    clipped_key = (w_key.astype(jnp.float32) * columns[None, :]).astype(jnp.bfloat16)
    scale_two = rms_scale(attended)
    moe_gain = gain_two.astype(jnp.float32)
    normed_moe = (attended * scale_two * moe_gain).astype(jnp.bfloat16)
    logits = jnp.dot(normed_moe, router_full, preferred_element_type=jnp.float32)
    matches = routes[:, :, None] == jnp.arange(experts, dtype=jnp.int32)[None, None, :]
    chosen = jnp.sum(jnp.where(matches, logits[:, None, :], 0.0), axis=2)
    gate_share = jax.nn.softmax(chosen, axis=1)
    pair_count = tok_rows * top_count
    capacity = 3 * tok_rows * top_count // devices
    half_cap = capacity // 2
    flat_route = routes.reshape(pair_count)
    one_hot = (flat_route[:, None] == jnp.arange(experts, dtype=jnp.int32)[None, :]).astype(
        jnp.int32
    )
    slot_rank = jnp.sum(jnp.cumsum(one_hot, axis=0) * one_hot, axis=1) - 1
    target_device = 2 * flat_route + slot_rank // half_cap
    target_slot = slot_rank % half_cap
    flat_slot = target_device * half_cap + target_slot
    slot_total = devices * half_cap
    outgoing = (
        jnp.zeros((slot_total, model_width), jnp.bfloat16)
        .at[flat_slot]
        .set(jnp.repeat(normed_moe, top_count, axis=0))
    )
    live_out = jnp.zeros((slot_total,), jnp.int32).at[flat_slot].set(1)
    incoming, live_in = (
        lax.all_to_all(outgoing, "fsdp", split_axis=0, concat_axis=0, tiled=True),
        lax.all_to_all(live_out, "fsdp", split_axis=0, concat_axis=0, tiled=True),
    )
    packed_order = jnp.cumsum(live_in) - 1
    packed_index = jnp.where(live_in > 0, packed_order, slot_total)
    back_index = jnp.clip(packed_order, 0, slot_total - 1)
    live_count = jnp.sum(live_in)
    tile_rows = 128
    tile_count = (live_count + tile_rows - 1) // tile_rows
    packed_rows = (
        jnp.zeros((slot_total + 1, model_width), jnp.bfloat16)
        .at[packed_index]
        .set(incoming)[:slot_total]
    )
    partner_half = swapped((w_gate, w_up, w_down), "fsdp", 0)
    lower = device % 2 == 0

    def joined(own_half, other_half):
        return jnp.where(
            lower, jnp.concatenate((own_half, other_half)), jnp.concatenate((other_half, own_half))
        )

    gate_full = joined(w_gate, partner_half[0])
    up_full = joined(w_up, partner_half[1])
    down_full = joined(w_down, partner_half[2])
    hidden_units = gate_full.shape[0]

    def forward_tile(tile_step, loop_state):
        out_rows, gate_keep, up_keep = loop_state
        tile_start = tile_step * tile_rows
        tile_input = lax.dynamic_slice_in_dim(packed_rows, tile_start, tile_rows, 0)
        gate_pre = contract(tile_input, gate_full, 1, 1)
        up_pre = contract(tile_input, up_full, 1, 1)
        hidden = (jax.nn.silu(gate_pre) * up_pre).astype(jnp.bfloat16)
        result = jnp.dot(hidden, down_full, preferred_element_type=jnp.float32).astype(jnp.bfloat16)
        return (
            lax.dynamic_update_slice_in_dim(out_rows, result, tile_start, 0),
            lax.dynamic_update_slice_in_dim(gate_keep, gate_pre, tile_start, 0),
            lax.dynamic_update_slice_in_dim(up_keep, up_pre, tile_start, 0),
        )

    start_state = (
        jnp.zeros((slot_total, model_width), jnp.bfloat16),
        jnp.zeros((slot_total, hidden_units), jnp.float32),
        jnp.zeros((slot_total, hidden_units), jnp.float32),
    )
    expert_out, gate_keep, up_keep = lax.fori_loop(0, tile_count, forward_tile, start_state)
    returning = jnp.where(live_in[:, None] > 0, expert_out[back_index], jnp.zeros((), jnp.bfloat16))
    came_back = lax.all_to_all(returning, "fsdp", split_axis=0, concat_axis=0, tiled=True)
    pair_out = came_back[flat_slot].reshape(tok_rows, top_count, model_width)
    mixture = jnp.sum(gate_share[:, :, None] * pair_out, axis=1)
    mixed = (attended + mixture).astype(jnp.bfloat16)
    query_back, key_back, value_back, out_back = (
        lax.all_gather(w_query, "fsdp", axis=0, tiled=True),
        lax.all_gather(w_key, "fsdp", axis=0, tiled=True),
        lax.all_gather(w_value, "fsdp", axis=0, tiled=True),
        lax.all_gather(w_out, "fsdp", axis=0, tiled=True),
    )
    grad_mixed = cotangent.astype(jnp.float32)
    grad_share = jnp.sum(grad_mixed[:, None, :] * pair_out, axis=2)
    grad_pair = (
        (gate_share[:, :, None] * grad_mixed[:, None, :])
        .astype(jnp.bfloat16)
        .reshape(pair_count, model_width)
    )
    grad_outgoing = jnp.zeros((slot_total, model_width), jnp.bfloat16).at[flat_slot].set(grad_pair)
    grad_incoming = lax.all_to_all(grad_outgoing, "fsdp", split_axis=0, concat_axis=0, tiled=True)
    grad_packed = (
        jnp.zeros((slot_total + 1, model_width), jnp.bfloat16)
        .at[packed_index]
        .set(grad_incoming)[:slot_total]
    )

    def backward_tile(tile_step, loop_state):
        grad_rows, gate_sum, up_sum, down_sum = loop_state
        tile_start = tile_step * tile_rows
        tile_input = lax.dynamic_slice_in_dim(packed_rows, tile_start, tile_rows, 0)
        tile_grad = lax.dynamic_slice_in_dim(grad_packed, tile_start, tile_rows, 0)
        gate_pre = lax.dynamic_slice_in_dim(gate_keep, tile_start, tile_rows, 0)
        up_pre = lax.dynamic_slice_in_dim(up_keep, tile_start, tile_rows, 0)
        sigmoid_gate = jax.nn.sigmoid(gate_pre)
        silu_gate = gate_pre * sigmoid_gate
        hidden = (silu_gate * up_pre).astype(jnp.bfloat16)
        grad_hidden = contract(tile_grad, down_full, 1, 1)
        grad_gate_pre = (
            grad_hidden * up_pre * sigmoid_gate * (1.0 + gate_pre * (1.0 - sigmoid_gate))
        ).astype(jnp.bfloat16)
        grad_up_pre = (grad_hidden * silu_gate).astype(jnp.bfloat16)
        down_sum = down_sum + contract(hidden, tile_grad, 0, 0)
        gate_sum = gate_sum + contract(grad_gate_pre, tile_input, 0, 0)
        up_sum = up_sum + contract(grad_up_pre, tile_input, 0, 0)
        grad_input = (
            jnp.dot(grad_gate_pre, gate_full, preferred_element_type=jnp.float32)
            + jnp.dot(grad_up_pre, up_full, preferred_element_type=jnp.float32)
        ).astype(jnp.bfloat16)
        return (
            lax.dynamic_update_slice_in_dim(grad_rows, grad_input, tile_start, 0),
            gate_sum,
            up_sum,
            down_sum,
        )

    weight_zero = jnp.zeros((hidden_units, model_width), jnp.float32)
    back_state = (
        jnp.zeros((slot_total, model_width), jnp.bfloat16),
        weight_zero,
        weight_zero,
        weight_zero,
    )
    grad_rows, gate_sum, up_sum, down_sum = lax.fori_loop(0, tile_count, backward_tile, back_state)
    grad_returning = jnp.where(
        live_in[:, None] > 0, grad_rows[back_index], jnp.zeros((), jnp.bfloat16)
    )
    grad_came = lax.all_to_all(grad_returning, "fsdp", split_axis=0, concat_axis=0, tiled=True)
    grad_from_experts = jnp.sum(
        grad_came[flat_slot].reshape(tok_rows, top_count, model_width), axis=1, dtype=jnp.float32
    )
    half_units = w_gate.shape[0]

    def partner_part(grad_sum):
        return jnp.where(lower, grad_sum[half_units:], grad_sum[:half_units])

    def own_part(grad_sum):
        return jnp.where(lower, grad_sum[:half_units], grad_sum[half_units:])

    partner_terms = (
        swapped(partner_part(gate_sum).astype(jnp.bfloat16), "fsdp", 0).astype(jnp.float32),
        swapped(partner_part(up_sum).astype(jnp.bfloat16), "fsdp", 0).astype(jnp.float32),
        swapped(partner_part(down_sum).astype(jnp.bfloat16), "fsdp", 0).astype(jnp.float32),
    )
    grad_gate = own_part(gate_sum) + partner_terms[0]
    grad_up = own_part(up_sum) + partner_terms[1]
    grad_down = own_part(down_sum) + partner_terms[2]
    grad_chosen = gate_share * (
        grad_share - jnp.sum(gate_share * grad_share, axis=1, keepdims=True)
    )
    grad_logits = jnp.sum(jnp.where(matches, grad_chosen[:, :, None], 0.0), axis=1)
    grad_router_part = jnp.dot(normed_moe.astype(jnp.float32).T, grad_logits, precision=highest)
    grad_normed_moe = grad_from_experts + jnp.dot(
        grad_logits, router_full.astype(jnp.float32).T, precision=highest
    )
    grad_from_norm, grad_gain_two = norm_back(grad_normed_moe, attended, scale_two, moe_gain)
    grad_attended = grad_mixed + grad_from_norm
    grad_attended_low = grad_attended.astype(jnp.bfloat16)
    grad_out_part = contract(context, grad_attended_low, 0, 0)
    grad_context = (
        contract(grad_attended_low, out_back, 1, 1)
        .astype(jnp.bfloat16)
        .reshape(tok_rows, head_count, head_size)
    )
    probs = jnp.exp(scores_of() - log_total)
    probs_back = probs.astype(jnp.bfloat16)
    grad_values = jnp.einsum(
        "hqk,qhd->khd", probs_back, grad_context, preferred_element_type=jnp.float32
    )
    grad_probs = jnp.einsum(
        "qhd,khd->hqk", grad_context, value_heads, preferred_element_type=jnp.float32
    )
    grad_scores = (
        probs * (grad_probs - jnp.sum(probs * grad_probs, axis=2, keepdims=True))
    ).astype(jnp.bfloat16)
    grad_queries = (
        (
            jnp.einsum("hqk,khd->qhd", grad_scores, key_heads, preferred_element_type=jnp.float32)
            * score_scale
        )
        .reshape(tok_rows, model_width)
        .astype(jnp.bfloat16)
    )
    grad_keys = (
        jnp.einsum("hqk,qhd->khd", grad_scores, query_heads, preferred_element_type=jnp.float32)
        * score_scale
    )
    grad_kv = jnp.concatenate(
        (grad_keys.reshape(key_count, model_width), grad_values.reshape(key_count, model_width)),
        axis=1,
    )
    grad_blocks = [
        grad_kv[position * tok_rows : (position + 1) * tok_rows] for position in range(len(ordered))
    ]
    own_block = grad_blocks[reach_count]
    remote = grad_blocks[:reach_count] + grad_blocks[reach_count + 1 :]
    returned = [
        passed_along(grad_block.astype(jnp.bfloat16), "fsdp", -offset).astype(grad_block.dtype)
        for grad_block, offset in zip(remote, offsets)
    ]
    grad_kv_low = reduce(jnp.add, returned, own_block).astype(jnp.bfloat16)
    grad_query_part = contract(normed_attn, grad_queries, 0, 0)
    grad_kv_part = contract(normed_attn, grad_kv_low, 0, 0)
    grad_normed_attn = (
        contract(grad_queries, query_back, 1, 1)
        + contract(grad_kv_low[:, :model_width], key_back, 1, 1)
        + contract(grad_kv_low[:, model_width:], value_back, 1, 1)
    )
    grad_from_first, grad_gain_one = norm_back(grad_normed_attn, token_values, scale_one, attn_gain)
    grad_tokens = grad_attended + grad_from_first
    reduced = (
        lax.psum_scatter(grad_query_part, "fsdp", scatter_dimension=0, tiled=True),
        lax.psum_scatter(grad_kv_part[:, :model_width], "fsdp", scatter_dimension=0, tiled=True),
        lax.psum_scatter(grad_kv_part[:, model_width:], "fsdp", scatter_dimension=0, tiled=True),
        lax.psum_scatter(grad_out_part, "fsdp", scatter_dimension=0, tiled=True),
        lax.psum_scatter(grad_router_part, "fsdp", scatter_dimension=0, tiled=True),
        lax.psum_scatter(grad_gain_one, "fsdp", scatter_dimension=0, tiled=True),
        lax.psum_scatter(grad_gain_two, "fsdp", scatter_dimension=0, tiled=True),
    )
    return (
        mixed,
        grad_tokens,
        reduced[0],
        reduced[1],
        reduced[2],
        reduced[3],
        reduced[4],
        reduced[5],
        reduced[6],
        grad_gate,
        grad_up,
        grad_down,
        clipped_query,
        clipped_key,
    )


def solution(mesh):
    placed = (
        P("fsdp", None),
        P("fsdp", None),
        P("fsdp", None),
        P("fsdp", None),
        P("fsdp", None),
        P("fsdp", None),
        P("fsdp"),
        P("fsdp"),
        P("fsdp", None),
        P("fsdp", None),
        P("fsdp", None),
        P("fsdp", None),
        P(),
        P(),
        P("fsdp", None),
    )
    return jax.shard_map(
        per_device,
        mesh=mesh,
        in_specs=placed,
        out_specs=(
            P("fsdp", None),
            P("fsdp", None),
            P("fsdp", None),
            P("fsdp", None),
            P("fsdp", None),
            P("fsdp", None),
            P("fsdp", None),
            P("fsdp"),
            P("fsdp"),
            P("fsdp", None),
            P("fsdp", None),
            P("fsdp", None),
            P("fsdp", None),
            P("fsdp", None),
        ),
        check_vma=False,
    )
```

profile of v0, /device:TPU:16, one launch (start us, length us, event | category | flops | bytes accessed | tf_op | source)
XLA Modules:
  0.0 3650.6 jit_solution(16188282616778618938)
XLA Ops:
  33.9 41.1 %all-reduce.5 = (bf16[2048]{0:T(1024)(128)(2,1)S(1)}, bf16[2048]{0:T(1024)(128)(2,1)S(1)}) all-reduce(bf16[2048]{0:T(1024)(128)(2,1)S(1)} %dynamic-update-slice, bf16[2048]{0:T(1024)(128)(2,1)S(1)} %dynamic-update-slice.1), channel_id=1, replica_groups=mesh['fsdp'=32] {'fsdp'}, use_global_device_ids=true, to_apply=%add | all-reduce | flops 4096 | bytes 16384
  96.6 72.9 %all-gather.6.cloned.1.call-done = bf16[2048,2048]{1,0:T(8,128)(2,1)} async-done(((bf16[64,2048]{1,0:T(8,128)(2,1)}), bf16[2048,2048]{1,0:T(8,128)(2,1)}) %all-gather.6.cloned.1.call-update) | async-done | bytes 8388624 | tf_op jit(solution)/shard_map/all_gather | solution.py:96
  181.0 109.6 %all-gather = bf16[32,64,16]{1,2,0:T(8,128)(2,1)S(1)} all-gather(bf16[1,64,16]{1,2,0:T(8,128)(2,1)S(1)} %bitcast.190), channel_id=1, replica_groups=mesh['fsdp'=32] {'fsdp'}, dimensions={0}, use_global_device_ids=true | all-gather | bytes 67584 | tf_op jit(solution)/shard_map/all_gather | solution.py:99
  339.6 61.4 %collective-permute-done.2 = bf16[256,4096]{1,0:T(8,128)(2,1)} collective-permute-done((bf16[256,4096]{1,0:T(8,128)(2,1)}, bf16[256,4096]{1,0:T(8,128)(2,1)}, u32[]{:S(2)}, u32[]{:S(2)}) %collective-permute-start.2) | collective-permute-done | bytes 2097184 | tf_op jit(solution)/shard_map/ppermute | solution.py:19
  522.5 256.5 %all-to-all-done.3 = bf16[32,96,2048]{2,1,0:T(8,128)(2,1)} async-done(((bf16[32,96,2048]{2,1,0:T(8,128)(2,1)}), bf16[32,96,2048]{2,1,0:T(8,128)(2,1)}, u32[]{:S(2)}, u32[]{:S(2)}) %all-to-all-start.3) | async-done | bytes 12582944 | tf_op jit(solution)/shard_map/all_to_all | solution.py:254
  807.7 26.1 scatter_custom_fusion.4
  844.5 217.4 %all-to-all-done.1 = bf16[32,96,2048]{2,1,0:T(8,128)(2,1)} async-done(((bf16[32,96,2048]{2,1,0:T(8,128)(2,1)}), bf16[32,96,2048]{2,1,0:T(8,128)(2,1)}, u32[]{:S(2)}, u32[]{:S(2)}) %all-to-all-start.1) | async-done | bytes 12582944 | tf_op jit(solution)/shard_map/all_to_all | solution.py:188
  1061.9 25.8 scatter_custom_fusion.2
  1116.9 266.4 %while.30 = (s32[]{:T(128)}, bf16[3072,2048]{1,0:T(8,128)(2,1)}, f32[3072,1024]{1,0:T(8,128)}, f32[3072,1024]{1,0:T(8,128)}, s32[]{:T(128)}, /*index=5*/bf16[307...) while((s32[]{:T(128)}, bf16[3072,2048]{1,0:T(8,128)(2,1)}, ...), condition=%wide.region_20.21_spmd, body=%wide.region_19.20_spmd.sunk | while | flops 1611661312 | bytes 34080968 | solution.py:234
  1402.4 581.0 %while.31 = (s32[]{:T(128)}, bf16[3072,2048]{1,0:T(8,128)(2,1)}, f32[1024,2048]{1,0:T(8,128)}, f32[1024,2048]{1,0:T(8,128)}, f32[1024,2048]{1,0:T(8,128)}, /*ind...) while((s32[]{:T(128)}, bf16[3072,2048]{1,0:T(8,128)(2,1)}, ...), condition=%wide.region_25.26_spmd, body=%wide.region_24.25_spmd.sunk | while | flops 3230531584 | bytes 289409504 | solution.py:297
  1983.5 30.0 gather_fusion.2
  2013.5 30.0 gather_fusion
  2057.0 277.3 %all_to_all.51 = bf16[32,96,2048]{2,1,0:T(8,128)(2,1)} all-to-all(bf16[32,96,2048]{2,1,0:T(8,128)(2,1)S(1)} %get-tuple-element.226), channel_id=1, replica_groups=mesh['fsdp'=32] {'fsdp'}, dimensions={0} | all-to-all | bytes 25165824 | tf_op jit(solution)/shard_map/all_to_all | solution.py:301
  2340.1 22.7 gather_fusion.3
  2374.1 241.6 %all-to-all-done.2 = bf16[32,96,2048]{2,1,0:T(8,128)(2,1)} async-done(((bf16[32,96,2048]{2,1,0:T(8,128)(2,1)}), bf16[32,96,2048]{2,1,0:T(8,128)(2,1)}, u32[]{:S(2)}, u32[]{:S(2)}) %all-to-all-start.2) | async-done | bytes 12582944 | tf_op jit(solution)/shard_map/all_to_all | solution.py:236
  2615.7 22.6 gather_fusion.1
  2780.0 37.4 %collective-permute-done.7 = bf16[256,4096]{0,1:T(8,128)(2,1)S(1)} collective-permute-done((bf16[256,4096]{0,1:T(8,128)(2,1)}, bf16[256,4096]{0,1:T(8,128)(2,1)S(1)}, u32[]{:S(2)}, u32[]{:S(2)}) %collective-permute-start.7) | collective-permute-done | bytes 2097184 | tf_op jit(solution)/shard_map/ppermute | solution.py:19
  2817.4 96.1 %collective-permute-done.10 = bf16[256,4096]{0,1:T(8,128)(2,1)S(1)} collective-permute-done((bf16[256,4096]{0,1:T(8,128)(2,1)}, bf16[256,4096]{0,1:T(8,128)(2,1)S(1)}, u32[]{:S(2)}, u32[]{:S(2)}) %collective-permute-start.10) | collective-permute-done | bytes 2097184 | tf_op jit(solution)/shard_map/ppermute | solution.py:19
  2957.2 58.8 %collective-permute-start.12 = (bf16[512,2048]{1,0:T(8,128)(2,1)}, bf16[512,2048]{1,0:T(8,128)(2,1)}, u32[]{:S(2)}, u32[]{:S(2)}) collective-permute-start(bf16[512,2048]{1,0:T(8,128)(2,1)} %select_convert_fusion.1), channel_id=1, source_target_pairs={{0,1},{1,0},{2,3},{3,2},{4,5},{5,4},{6,7},{7,6},{8,9},{9,8},{10,11... | collective-permute-start | bytes 6291464 | tf_op jit(solution)/shard_map/ppermute | solution.py:29
  3048.1 52.0 %pmax.7 = f32[16]{0:T(128)S(1)} all-reduce(f32[16]{0:T(128)S(1)} %get-tuple-element.142), channel_id=1, replica_groups=mesh['fsdp'=32] {'fsdp'}, use_global_device_ids=true, to_apply=%region_43.44 | all-reduce | flops 16 | bytes 128 | tf_op jit(solution)/shard_map/pmax | solution.py:151
  3124.5 44.1 %all-reduce.4 = (f32[2048]{0:T(1024)S(1)}, f32[2048]{0:T(1024)S(1)}) all-reduce(f32[2048]{0:T(1024)S(1)} %get-tuple-element.148, f32[2048]{0:T(1024)S(1)} %copy-done.49), channel_id=7, replica_groups=mesh['fsdp'=32] {'fsdp'}, use_global_device_ids=true, to_apply=%region_39.40.clone | all-reduce | flops 4096 | bytes 32768
  3173.8 95.8 %reduce-scatter.8.cloned.1.call-done = f32[64,2048]{1,0:T(8,128)} async-done(((f32[2048,2048]{1,0:T(8,128)}), f32[64,2048]{1,0:T(8,128)}) %reduce-scatter.8.cloned.1.call-update) | async-done | bytes 524304 | tf_op jit(solution)/shard_map/reduce_scatter | solution.py:385
  3269.7 186.7 %reduce-scatter.12.cloned.1.call-done = f32[64,2048]{1,0:T(8,128)} async-done(((f32[2048,2048]{1,0:T(8,128)}), f32[64,2048]{1,0:T(8,128)}) %reduce-scatter.12.cloned.1.call-update) | async-done | bytes 524304 | tf_op jit(solution)/shard_map/reduce_scatter | solution.py:387
  3456.4 187.5 %reduce-scatter.10.cloned.1.call-done = f32[64,2048]{1,0:T(8,128)} async-done(((f32[2048,2048]{1,0:T(8,128)}), f32[64,2048]{1,0:T(8,128)}) %reduce-scatter.10.cloned.1.call-update) | async-done | bytes 524304 | tf_op jit(solution)/shard_map/reduce_scatter | solution.py:386
  (1118 shorter events, 1437.9 us)
Async XLA Ops:
  7.2 83.2 %all-gather.8.cloned.1.call-start = ((), (), s32[]{:S(2)}) async-start(), calls=%async_computation.11 | async-start | bytes 8650752 | tf_op jit(solution)/shard_map/all_gather | solution.py:97
  7.9 161.6 %all-gather.6.cloned.1.call-start = ((), (), s32[]{:S(2)}) async-start(), calls=%async_computation.10 | async-start | bytes 8650752 | tf_op jit(solution)/shard_map/all_gather | solution.py:96
  8.7 296.9 %all-gather.10.cloned.1.call-start = ((), (), s32[]{:S(2)}) async-start(), calls=%async_computation.12 | async-start | bytes 8650752 | tf_op jit(solution)/shard_map/all_gather | solution.py:95
  9.4 444.5 %all-gather.12.cloned.1.call-start = ((), (), s32[]{:S(2)}) async-start(), calls=%async_computation.13 | async-start | bytes 8650752 | tf_op jit(solution)/shard_map/all_gather | solution.py:98
  26.2 457.1 %all-to-all-start = ((s32[32,96,1]{1,2,0:T(1,128)}), s32[32,96,1]{1,2,0:T(1,128)S(1)}, u32[]{:S(2)}, u32[]{:S(2)}) async-start(s32[32,96,1]{1,2,0:T(1,128)} %all_to_all.34), calls=%async_computation | async-start | bytes 32768 | tf_op jit(solution)/shard_map/all_to_all | solution.py:189
  177.7 135.1 %collective-permute-start = (bf16[256,4096]{1,0:T(8,128)(2,1)}, bf16[256,4096]{1,0:T(8,128)(2,1)}, u32[]{:S(2)}, u32[]{:S(2)}) collective-permute-start(bf16[256,4096]{1,0:T(8,128)(2,1)} %pad_maximum_fusion.1), channel_id=1, source_target_pairs={{0,2},{1,3},{2,4},{3,5},{4,6},{5,7},{6,8},{7,9},{8,10},{9,11},{10,... | collective-permute-start | bytes 6291464 | tf_op jit(solution)/shard_map/ppermute | solution.py:19
  294.2 40.7 %collective-permute-start.1 = (bf16[256,4096]{1,0:T(8,128)(2,1)}, bf16[256,4096]{1,0:T(8,128)(2,1)}, u32[]{:S(2)}, u32[]{:S(2)}) collective-permute-start(bf16[256,4096]{1,0:T(8,128)(2,1)} %pad_maximum_fusion.1), channel_id=1, source_target_pairs={{0,1},{1,2},{2,3},{3,4},{4,5},{5,6},{6,7},{7,8},{8,9},{9,10},{10,1... | collective-permute-start | bytes 6291464 | tf_op jit(solution)/shard_map/ppermute | solution.py:19
  297.6 106.5 %collective-permute-start.3 = (bf16[256,4096]{1,0:T(8,128)(2,1)}, bf16[256,4096]{1,0:T(8,128)(2,1)}, u32[]{:S(2)}, u32[]{:S(2)}) collective-permute-start(bf16[256,4096]{1,0:T(8,128)(2,1)} %pad_maximum_fusion.1), channel_id=1, source_target_pairs={{2,0},{3,1},{4,2},{5,3},{6,4},{7,5},{8,6},{9,7},{10,8},{11,9},{12,... | collective-permute-start | bytes 6291464 | tf_op jit(solution)/shard_map/ppermute | solution.py:19
  302.3 98.7 %collective-permute-start.2 = (bf16[256,4096]{1,0:T(8,128)(2,1)}, bf16[256,4096]{1,0:T(8,128)(2,1)}, u32[]{:S(2)}, u32[]{:S(2)}) collective-permute-start(bf16[256,4096]{1,0:T(8,128)(2,1)} %pad_maximum_fusion.1), channel_id=1, source_target_pairs={{1,0},{2,1},{3,2},{4,3},{5,4},{6,5},{7,6},{8,7},{9,8},{10,9},{11,1... | collective-permute-start | bytes 6291464 | tf_op jit(solution)/shard_map/ppermute | solution.py:19
  483.4 295.6 %all-to-all-start.3 = ((bf16[32,96,2048]{2,1,0:T(8,128)(2,1)}), bf16[32,96,2048]{2,1,0:T(8,128)(2,1)}, u32[]{:S(2)}, u32[]{:S(2)}) async-start(bf16[32,96,2048]{2,1,0:T(8,128)(2,1)} %bitcast.165), calls=%async_computation.3 | async-start | bytes 25165824 | tf_op jit(solution)/shard_map/all_to_all | solution.py:254
  779.0 282.9 %all-to-all-start.1 = ((bf16[32,96,2048]{2,1,0:T(8,128)(2,1)}), bf16[32,96,2048]{2,1,0:T(8,128)(2,1)}, u32[]{:S(2)}, u32[]{:S(2)}) async-start(bf16[32,96,2048]{2,1,0:T(8,128)(2,1)} %bitcast.164), calls=%async_computation.1 | async-start | bytes 25165824 | tf_op jit(solution)/shard_map/all_to_all | solution.py:188
  786.9 15.7 collective-permute-start.6
  2334.3 281.4 %all-to-all-start.2 = ((bf16[32,96,2048]{2,1,0:T(8,128)(2,1)}), bf16[32,96,2048]{2,1,0:T(8,128)(2,1)}, u32[]{:S(2)}, u32[]{:S(2)}) async-start(bf16[32,96,2048]{2,1,0:T(8,128)(2,1)} %get-tuple-element.227), calls=%async_computation.2 | async-start | bytes 25165824 | tf_op jit(solution)/shard_map/all_to_all | solution.py:236
  2340.0 768.3 %reduce-scatter.16.cloned.1.call-start = ((), (), s32[]{:S(2)}) async-start(), calls=%async_computation.18 | async-start | bytes 1081344
  2655.9 517.9 %reduce-scatter.14.cloned.1.call-start = ((), (), s32[]{:S(2)}) async-start(), calls=%async_computation.17 | async-start | bytes 17301504 | tf_op jit(solution)/shard_map/reduce_scatter | solution.py:388
  2669.7 600.0 %reduce-scatter.8.cloned.1.call-start = ((), (), s32[]{:S(2)}) async-start(), calls=%async_computation.14 | async-start | bytes 17301504 | tf_op jit(solution)/shard_map/reduce_scatter | solution.py:385
  2731.9 724.5 %reduce-scatter.12.cloned.1.call-start = ((), (), s32[]{:S(2)}) async-start(), calls=%async_computation.16 | async-start | bytes 17301504 | tf_op jit(solution)/shard_map/reduce_scatter | solution.py:387
  2766.5 50.9 %collective-permute-start.7 = (bf16[256,4096]{0,1:T(8,128)(2,1)}, bf16[256,4096]{0,1:T(8,128)(2,1)S(1)}, u32[]{:S(2)}, u32[]{:S(2)}) collective-permute-start(bf16[256,4096]{0,1:T(8,128)(2,1)} %get-tuple-element.210), channel_id=1, source_target_pairs={{2,0},{3,1},{4,2},{5,3},{6,4},{7,5},{8,6},{9,7},{10,8},{11,9},{12,... | collective-permute-start | bytes 6291464 | tf_op jit(solution)/shard_map/ppermute | solution.py:19
  2768.8 144.7 %collective-permute-start.10 = (bf16[256,4096]{0,1:T(8,128)(2,1)}, bf16[256,4096]{0,1:T(8,128)(2,1)S(1)}, u32[]{:S(2)}, u32[]{:S(2)}) collective-permute-start(bf16[256,4096]{0,1:T(8,128)(2,1)} %get-tuple-element.211), channel_id=1, source_target_pairs={{0,2},{1,3},{2,4},{3,5},{4,6},{5,7},{6,8},{7,9},{8,10},{9,11},{10,... | collective-permute-start | bytes 6291464 | tf_op jit(solution)/shard_map/ppermute | solution.py:19
  2772.6 140.9 %collective-permute-start.9 = (bf16[256,4096]{0,1:T(8,128)(2,1)S(1)}, bf16[256,4096]{0,1:T(8,128)(2,1)S(1)}, u32[]{:S(2)}, u32[]{:S(2)}) collective-permute-start(bf16[256,4096]{0,1:T(8,128)(2,1)S(1)} %get-tuple-element.212), channel_id=1, source_target_pairs={{0,1},{1,2},{2,3},{3,4},{4,5},{5,6},{6,7},{7,8},{8,9},{9,10},{10,1... | collective-permute-start | bytes 6291464 | tf_op jit(solution)/shard_map/ppermute | solution.py:19
  2774.5 138.9 %collective-permute-start.8 = (bf16[256,4096]{0,1:T(8,128)(2,1)S(1)}, bf16[256,4096]{0,1:T(8,128)(2,1)}, u32[]{:S(2)}, u32[]{:S(2)}) collective-permute-start(bf16[256,4096]{0,1:T(8,128)(2,1)S(1)} %get-tuple-element.213), channel_id=1, source_target_pairs={{1,0},{2,1},{3,2},{4,3},{5,4},{6,5},{7,6},{8,7},{9,8},{10,9},{11,1... | collective-permute-start | bytes 6291464 | tf_op jit(solution)/shard_map/ppermute | solution.py:19
  2951.3 692.6 %reduce-scatter.10.cloned.1.call-start = ((), (), s32[]{:S(2)}) async-start(), calls=%async_computation.15 | async-start | bytes 17301504 | tf_op jit(solution)/shard_map/reduce_scatter | solution.py:386
  2957.2 69.8 %collective-permute-start.12 = (bf16[512,2048]{1,0:T(8,128)(2,1)}, bf16[512,2048]{1,0:T(8,128)(2,1)}, u32[]{:S(2)}, u32[]{:S(2)}) collective-permute-start(bf16[512,2048]{1,0:T(8,128)(2,1)} %select_convert_fusion.1), channel_id=1, source_target_pairs={{0,1},{1,0},{2,3},{3,2},{4,5},{5,4},{6,7},{7,6},{8,9},{9,8},{10,11... | collective-permute-start | bytes 6291464 | tf_op jit(solution)/shard_map/ppermute | solution.py:29
  3026.6 16.2 collective-permute-start.13
  (332 other events, 4962.3 us)
Sparse Core Ops, SparseCore 0:
  10.9 79.5 all-gather.7
  93.3 76.1 all-gather.5
  172.3 95.7 all-gather.9
  270.9 125.7 all-gather.11
  2656.0 103.8 reduce-scatter.15
  2762.7 318.5 reduce-scatter.13
  3084.3 185.2 reduce-scatter.7
  3272.6 183.7 reduce-scatter.11
  3459.4 184.4 reduce-scatter.9
where the time goes:
time: 3660 us; the launch traced here: 3650 us
  waiting for transfers between devices  1490 us (41%)
  matrix products  846 us (23%)
  blocking collectives  524 us (14%)
  local copies, waits for them, and re-layouts  476 us (13%)
  other arithmetic  169 us (5%)
  starting transfers between devices  126 us (3%)
    dot_general x151, matrix products, contract(): lax.dot_general(left, right, (((left_dim,), (right_dim,)), ((), ())), pre...  645 us
    all_to_all x1, blocking collectives, per_device(): lax.all_to_all(grad_returning, 'fsdp', split_axis=0, concat_axis=0, tiled...  277 us
    all_to_all x1, waiting for transfers between devices, per_device(): lax.all_to_all(grad_outgoing, 'fsdp', split_axis=0, concat_axis=0, tiled=...  257 us
    all_to_all x1, waiting for transfers between devices, per_device(): lax.all_to_all(returning, 'fsdp', split_axis=0, concat_axis=0, tiled=True)  242 us
    all_to_all x1, waiting for transfers between devices, per_device(): lax.all_to_all(outgoing, 'fsdp', split_axis=0, concat_axis=0, tiled=True)  217 us
    ppermute x8, waiting for transfers between devices, passed_along(): return lax.ppermute(x, axis, pairs)  214 us
    reduce_scatter x1, waiting for transfers between devices, per_device(): lax.psum_scatter(grad_kv_part[:, :model_width], 'fsdp', scatter_dimension...  187 us
    reduce_scatter x1, waiting for transfers between devices, per_device(): lax.psum_scatter(grad_kv_part[:, model_width:], 'fsdp', scatter_dimension...  187 us
  transfers between devices with their start and end apart: 27, of which 13 were waited for; matrix products, arithmetic and copies ran while one was open for 12% of the time, Pallas kernels for 0%

commit v1 on v0

--- a/solution.py
+++ b/solution.py
@@ -1,8 +1,11 @@
+import functools
 from functools import reduce
 
 import jax
 import jax.numpy as jnp
 from jax import lax
+from jax.experimental import pallas as pl
+from jax.experimental.pallas import tpu as pltpu
 from jax.sharding import PartitionSpec as P
 
 HALF = 512
@@ -64,7 +67,7 @@
     )
 
 
-def per_device(
+def routed_layer(
     tokens,
     w_query,
     w_key,
@@ -408,6 +411,878 @@
     )
 
 
+MESH = pl.DeviceIdType.MESH
+f32 = jnp.float32
+bf = jnp.bfloat16
+
+def place():
+    me = lax.axis_index("fsdp")
+    core = lax.rem(me, 2)
+    x = lax.rem(lax.div(me, 2), 2)
+    y = lax.rem(lax.div(me, 4), 2)
+    z = lax.div(me, 8)
+    return z, y, x, core
+
+def index_of(z, y, x, core):
+    return ((z * 2 + y) * 2 + x) * 2 + core
+
+def remote(src, dst, send, recv, device):
+    return pltpu.make_async_remote_copy(
+        src_ref=src, dst_ref=dst, send_sem=send, recv_sem=recv, device_id=(device,), device_id_type=MESH)
+
+def greet(devices, conditions):
+    barrier = pltpu.get_barrier_semaphore()
+    for device, condition in zip(devices, conditions):
+        if condition is None:
+            pl.semaphore_signal(barrier, inc=1, device_id=(device,), device_id_type=MESH)
+        else:
+            @pl.when(condition)
+            def _(device=device):
+                pl.semaphore_signal(barrier, inc=1, device_id=(device,), device_id_type=MESH)
+    count = 0
+    for condition in conditions:
+        count = count + (1 if condition is None else jnp.where(condition, 1, 0))
+    pl.semaphore_wait(barrier, count)
+
+def line_items(z):
+    low = z < 2
+    near = z + 1 - 2 * lax.rem(z, 2)
+    return [z, near, jnp.where(low, 2, 1), jnp.where(low, 3, 0)]
+
+def gather_plane(ins, outs, ssem, rsem, lsem):
+    count = len(ins)
+    z, y, x, core = place()
+    mid = (z == 1) | (z == 2)
+    up, down = z < 3, z > 0
+    y_dev = index_of(z, 1 - y, x, core)
+    up_dev = index_of(jnp.minimum(z + 1, 3), y, x, core)
+    down_dev = index_of(jnp.maximum(z - 1, 0), y, x, core)
+    greet([y_dev, up_dev, down_dev], [None, up, down])
+    own = [pltpu.make_async_copy(ins[a], outs[a].at[z * 2 + y], lsem.at[a]) for a in range(count)]
+    for copy in own:
+        copy.start()
+    pending = []
+
+    def go(kind, a, o, src, device, condition=None):
+        def make():
+            return remote(src, outs[a].at[o * 2 + y], ssem.at[kind, o, a], rsem.at[kind, o, a], device)
+        if condition is None:
+            make().start()
+        else:
+            pl.when(condition)(lambda: make().start())
+        pending.append((make, condition))
+
+    for i, o in enumerate(line_items(z)):
+        for a in range(count):
+            src = ins[a] if i == 0 else outs[a].at[o * 2 + y]
+            if i == 0:
+                go(0, a, o, src, up_dev, up)
+                go(1, a, o, src, down_dev, down)
+            else:
+                from_below = o < z
+                for kind, condition in ((0, from_below), (1, jnp.logical_not(from_below))):
+                    @pl.when(condition)
+                    def _(kind=kind, a=a, o=o, src=src):
+                        remote(src, src, ssem.at[kind, o, a], rsem.at[kind, o, a], y_dev).wait_recv()
+                go(0, a, o, src, up_dev, mid & from_below)
+                go(1, a, o, src, down_dev, mid & jnp.logical_not(from_below))
+            go(2, a, o, src, y_dev)
+    for i, o in enumerate(line_items(z)):
+        for a in range(count):
+            land = outs[a].at[o * 2 + 1 - y]
+            remote(land, land, ssem.at[2, o, a], rsem.at[2, o, a], y_dev).wait_recv()
+    for make, condition in pending:
+        if condition is None:
+            make().wait_send()
+        else:
+            pl.when(condition)(lambda make=make: make().wait_send())
+    for copy in own:
+        copy.wait()
+
+def plane_gather(arrays, cid):
+    count = len(arrays)
+    anys = pl.BlockSpec(memory_space=pl.ANY)
+    def body(*refs):
+        gather_plane(refs[:count], refs[count:2 * count], *refs[2 * count:])
+    return pl.pallas_call(
+        body, in_specs=[anys] * count, out_specs=[anys] * count,
+        out_shape=[jax.ShapeDtypeStruct((8,) + a.shape, a.dtype) for a in arrays],
+        scratch_shapes=[pltpu.SemaphoreType.DMA((3, 4, count)), pltpu.SemaphoreType.DMA((3, 4, count)),
+                        pltpu.SemaphoreType.DMA((count,))],
+        compiler_params=pltpu.CompilerParams(collective_id=cid, has_side_effects=True),
+        name="plane_gather")(*arrays)
+
+def gather_all(ins, outs, ssem, rsem, lsem):
+    count = len(ins)
+    z, y, x, core = place()
+    mid = (z == 1) | (z == 2)
+    up, down = z < 3, z > 0
+    x_dev = index_of(z, y, 1 - x, core)
+    y_dev = index_of(z, 1 - y, x, core)
+    c_dev = index_of(z, y, x, 1 - core)
+    up_dev = index_of(jnp.minimum(z + 1, 3), y, x, core)
+    down_dev = index_of(jnp.maximum(z - 1, 0), y, x, core)
+    greet([x_dev, y_dev, c_dev, up_dev, down_dev], [None, None, None, up, down])
+    own = [pltpu.make_async_copy(ins[a], outs[a].at[index_of(z, y, x, core)], lsem.at[a]) for a in range(count)]
+    for copy in own:
+        copy.start()
+    pending = []
+
+    def go(kind, a, o, src, dst, device, condition=None):
+        def make():
+            return remote(src, dst, ssem.at[kind, o, a], rsem.at[kind, o, a], device)
+        if condition is None:
+            make().start()
+        else:
+            pl.when(condition)(lambda: make().start())
+        pending.append((make, condition))
+
+    def arrived(kind, a, o, land):
+        remote(land, land, ssem.at[kind, o, a], rsem.at[kind, o, a], c_dev).wait_recv()
+
+    items = line_items(z)
+
+    def first(i):
+        o = items[i]
+        for a in range(count):
+            slot = index_of(o, y, x, core)
+            dst = outs[a].at[slot]
+            src = ins[a] if i == 0 else dst
+            if i == 0:
+                go(0, a, o, src, dst, up_dev, up)
+                go(1, a, o, src, dst, down_dev, down)
+            else:
+                from_below = o < z
+                for kind, condition in ((0, from_below), (1, jnp.logical_not(from_below))):
+                    pl.when(condition)(lambda kind=kind, a=a, o=o, dst=dst: arrived(kind, a, o, dst))
+                go(0, a, o, src, dst, up_dev, mid & from_below)
+                go(1, a, o, src, dst, down_dev, mid & jnp.logical_not(from_below))
+            go(2, a, o, src, dst, x_dev)
+            go(3, a, o, src, dst, y_dev)
+            go(6, a, o, src, dst, c_dev)
+
+    def second(i):
+        o = items[i]
+        for a in range(count):
+            half = ins[a].shape[0] // 2
+            from_x = outs[a].at[index_of(o, y, 1 - x, core)]
+            arrived(2, a, o, from_x)
+            go(5, a, o, from_x.at[pl.ds(0, half)], from_x.at[pl.ds(0, half)], y_dev)
+            from_y = outs[a].at[index_of(o, 1 - y, x, core)]
+            arrived(3, a, o, from_y)
+            go(4, a, o, from_y.at[pl.ds(half, half)], from_y.at[pl.ds(half, half)], x_dev)
+            go(7, a, o, from_x, from_x, c_dev)
+            go(8, a, o, from_y, from_y, c_dev)
+
+    def third(i):
+        o = items[i]
+        for a in range(count):
+            half = ins[a].shape[0] // 2
+            corner = outs[a].at[index_of(o, 1 - y, 1 - x, core)]
+            arrived(5, a, o, corner.at[pl.ds(0, half)])
+            arrived(4, a, o, corner.at[pl.ds(half, half)])
+            go(9, a, o, corner, corner, c_dev)
+
+    first(0); first(1); second(0); first(2); second(1); third(0); first(3); second(2); third(1); second(3); third(2); third(3)
+    for i in range(4):
+        o = items[i]
+        for a in range(count):
+            for kind, (yy, xx) in ((6, (y, x)), (7, (y, 1 - x)), (8, (1 - y, x)), (9, (1 - y, 1 - x))):
+                arrived(kind, a, o, outs[a].at[index_of(o, yy, xx, 1 - core)])
+    for make, condition in pending:
+        if condition is None:
+            make().wait_send()
+        else:
+            pl.when(condition)(lambda make=make: make().wait_send())
+    for copy in own:
+        copy.wait()
+
+def full_gather(arrays, cid):
+    count = len(arrays)
+    anys = pl.BlockSpec(memory_space=pl.ANY)
+    def body(*refs):
+        gather_all(refs[:count], refs[count:2 * count], *refs[2 * count:])
+    return pl.pallas_call(
+        body, in_specs=[anys] * count, out_specs=[anys] * count,
+        out_shape=[jax.ShapeDtypeStruct((32,) + a.shape, a.dtype) for a in arrays],
+        scratch_shapes=[pltpu.SemaphoreType.DMA((10, 4, count)), pltpu.SemaphoreType.DMA((10, 4, count)),
+                        pltpu.SemaphoreType.DMA((count,))],
+        compiler_params=pltpu.CompilerParams(collective_id=cid, has_side_effects=True),
+        name="full_gather")(*arrays)
+
+def add_into(target, *terms, rows=16):
+    total = target.shape[0]
+    step = min(rows, total)
+    def one(r, carry):
+        part = pl.ds(pl.multiple_of(r * step, step), step)
+        value = target[part, :].astype(f32)
+        for term in terms:
+            value = value + term[part, :].astype(f32)
+        target[part, :] = value.astype(target.dtype)
+        return carry
+    lax.fori_loop(0, total // step, one, 0)
+
+def reduce_plane(parts, outs, accs, yrecvs, zrecvs, ssem, rsem, lsem, osem, ahead=3):
+    count = len(parts)
+    z, y, x, core = place()
+    mid = (z == 1) | (z == 2)
+    up, down = z < 3, z > 0
+    y_dev = index_of(z, 1 - y, x, core)
+    up_dev = index_of(jnp.minimum(z + 1, 3), y, x, core)
+    down_dev = index_of(jnp.maximum(z - 1, 0), y, x, core)
+    greet([y_dev, up_dev, down_dev], [None, up, down])
+    items = line_items(z)[::-1]
+    order = [(a, i) for a in range(count) for i in range(4)]
+    loads = {}
+    for a, i in order:
+        o = items[i]
+        copy = pltpu.make_async_copy(parts[a].at[o * 2 + y], accs[a].at[o], lsem.at[o, a])
+        copy.start()
+        loads[a, i] = copy
+    pending = []
+
+    def y_copy(a, i):
+        o = items[i]
+        return remote(parts[a].at[o * 2 + 1 - y], yrecvs[a].at[o], ssem.at[0, o, a], rsem.at[0, o, a], y_dev)
+
+    for a, i in order[:ahead]:
+        y_copy(a, i).start()
+    for k, (a, i) in enumerate(order):
+        o = items[i]
+        y_copy(a, i).wait_recv()
+        if k + ahead < len(order):
+            y_copy(*order[k + ahead]).start()
+        loads[a, i].wait()
+        acc = accs[a].at[o]
+        if i < 3:
+            @pl.when(mid)
+            def _(a=a, o=o, acc=acc):
+                land = zrecvs[a].at[o]
+                remote(land, land, ssem.at[1, o, a], rsem.at[1, o, a], y_dev).wait_recv()
+                add_into(acc, yrecvs[a].at[o], land)
+            @pl.when(jnp.logical_not(mid))
+            def _(a=a, o=o, acc=acc):
+                add_into(acc, yrecvs[a].at[o])
+            rising = o > z
+            for sign, dev in ((1, up_dev), (-1, down_dev)):
+                condition = rising if sign > 0 else jnp.logical_not(rising)
+                def make(a=a, o=o, acc=acc, sign=sign, dev=dev):
+                    slot = o if sign > 0 else jnp.where(z - 1 == o, 4, o)
+                    return remote(acc, zrecvs[a].at[slot], ssem.at[1, o, a], rsem.at[1, slot, a], dev)
+                pl.when(condition)(lambda make=make: make().start())
+                pending.append((make, condition))
+        else:
+            for condition, slots in ((z == 0, (4,)), (z == 3, (3,)), (mid, (None, 4))):
+                @pl.when(condition)
+                def _(a=a, o=o, acc=acc, slots=slots):
+                    terms = [yrecvs[a].at[o]]
+                    for slot in slots:
+                        slot = o if slot is None else slot
+                        land = zrecvs[a].at[slot]
+                        remote(land, land, ssem.at[1, o, a], rsem.at[1, slot, a], y_dev).wait_recv()
+                        terms.append(land)
+                    add_into(acc, *terms)
+            out = pltpu.make_async_copy(acc, outs[a], osem.at[a])
+            out.start()
+            pending.append((lambda out=out: out, "local"))
+    for a, i in order:
+        y_copy(a, i).wait_send()
+    for make, condition in pending:
+        if condition == "local" if isinstance(condition, str) else False:
+            make().wait()
+        else:
+            pl.when(condition)(lambda make=make: make().wait_send())
+
+def plane_reduce(parts, cid):
+    count = len(parts)
+    anys = pl.BlockSpec(memory_space=pl.ANY)
+    def body(*refs):
+        it = iter(refs)
+        take = lambda n: [next(it) for _ in range(n)]
+        ins, outs, accs, yr, zr = take(count), take(count), take(count), take(count), take(count)
+        reduce_plane(ins, outs, accs, yr, zr, *it)
+    shape = [p.shape[1:] for p in parts]
+    sem = pltpu.SemaphoreType.DMA
+    return pl.pallas_call(
+        body, in_specs=[anys] * count, out_specs=[anys] * count,
+        out_shape=[jax.ShapeDtypeStruct(s, p.dtype) for s, p in zip(shape, parts)],
+        scratch_shapes=[pltpu.VMEM((n,) + s, p.dtype) for n in (4, 4, 5) for s, p in zip(shape, parts)]
+        + [sem((2, 5, count)), sem((2, 5, count)), sem((4, count)), sem((count,))],
+        compiler_params=pltpu.CompilerParams(collective_id=cid, has_side_effects=True, vmem_limit_bytes=56 * 2**20),
+        name="plane_reduce")(*parts)
+
+def reduce_all(parts, outs, accs, crecvs, dxs, dys, xrecvs, yrecvs, zrecvs, ssem, rsem, lsem, osem):
+    count = len(parts)
+    z, y, x, core = place()
+    mid = (z == 1) | (z == 2)
+    up, down = z < 3, z > 0
+    x_dev = index_of(z, y, 1 - x, core)
+    y_dev = index_of(z, 1 - y, x, core)
+    c_dev = index_of(z, y, x, 1 - core)
+    up_dev = index_of(jnp.minimum(z + 1, 3), y, x, core)
+    down_dev = index_of(jnp.maximum(z - 1, 0), y, x, core)
+    greet([x_dev, y_dev, c_dev, up_dev, down_dev], [None, None, None, up, down])
+    items = line_items(z)[::-1]
+    mine, xp, yp, dp = y * 2 + x, y * 2 + 1 - x, (1 - y) * 2 + x, (1 - y) * 2 + 1 - x
+    pending = []
+
+    def go(make, condition=None):
+        if condition is None:
+            make().start()
+        else:
+            pl.when(condition)(lambda: make().start())
+        pending.append((make, condition))
+
+    def arrived(kind, a, o, land):
+        remote(land, land, ssem.at[kind, 0, a], rsem.at[kind, o, a], c_dev).wait_recv()
+
+    loads = {}
+    for i, o in enumerate(items):
+        for a in range(count):
+            go(lambda o=o, a=a: remote(parts[a].at[pl.ds(o * 4, 4), 1 - core], crecvs[a].at[o],
+                                       ssem.at[0, o, a], rsem.at[0, o, a], c_dev))
+            loads[i, a] = pltpu.make_async_copy(parts[a].at[pl.ds(o * 4, 4), core], accs[a].at[o], lsem.at[o, a])
+            loads[i, a].start()
+
+    def first(i):
+        o = items[i]
+        for a in range(count):
+            half = parts[a].shape[2] // 2
+            arrived(0, a, o, crecvs[a].at[o])
+            loads[i, a].wait()
+            for p in (dp, xp, yp, mine):
+                add_into(accs[a].at[o, p], crecvs[a].at[o, p])
+                if p is dp:
+                    go(lambda a=a, half=half: remote(accs[a].at[o, dp, pl.ds(0, half)], dxs[a].at[o], ssem.at[1, o, a], rsem.at[1, o, a], x_dev))
+                    go(lambda a=a, half=half: remote(accs[a].at[o, dp, pl.ds(half, half)], dys[a].at[o], ssem.at[2, o, a], rsem.at[2, o, a], y_dev))
+
+    def second(i):
+        o = items[i]
+        for a in range(count):
+            half = parts[a].shape[2] // 2
+            arrived(1, a, o, dxs[a].at[o])
+            add_into(accs[a].at[o, yp, pl.ds(0, half)], dxs[a].at[o])
+            go(lambda a=a, half=half: remote(accs[a].at[o, yp], yrecvs[a].at[o], ssem.at[4, o, a], rsem.at[4, o, a], y_dev))
+            arrived(2, a, o, dys[a].at[o])
+            add_into(accs[a].at[o, xp, pl.ds(half, half)], dys[a].at[o])
+            go(lambda a=a, half=half: remote(accs[a].at[o, xp], xrecvs[a].at[o], ssem.at[3, o, a], rsem.at[3, o, a], x_dev))
+
+    def third(i):
+        o = items[i]
+        for a in range(count):
+            acc = accs[a].at[o, mine]
+            arrived(3, a, o, xrecvs[a].at[o])
+            arrived(4, a, o, yrecvs[a].at[o])
+            if i < 3:
+                @pl.when(mid)
+                def _():
+                    arrived(5, a, o, zrecvs[a].at[o])
+                    add_into(acc, xrecvs[a].at[o], yrecvs[a].at[o], zrecvs[a].at[o])
+                @pl.when(jnp.logical_not(mid))
+                def _():
+                    add_into(acc, xrecvs[a].at[o], yrecvs[a].at[o])
+                rising = o > z
+                go(lambda o=o, a=a, acc=acc: remote(acc, zrecvs[a].at[o], ssem.at[5, o, a], rsem.at[5, o, a], up_dev), rising)
+                def lower(o=o, a=a, acc=acc):
+                    slot = jnp.where(z - 1 == o, 4, o)
+                    return remote(acc, zrecvs[a].at[slot], ssem.at[5, o, a], rsem.at[5, slot, a], down_dev)
+                go(lower, jnp.logical_not(rising))
+            else:
+                for condition, slots in ((z == 0, (4,)), (z == 3, (3,)), (mid, (None, 4))):
+                    @pl.when(condition)
+                    def _(slots=slots):
+                        terms = [xrecvs[a].at[o], yrecvs[a].at[o]]
+                        for slot in slots:
+                            slot = o if slot is None else slot
+                            arrived(5, a, slot, zrecvs[a].at[slot])
+                            terms.append(zrecvs[a].at[slot])
+                        rows, step = outs[a].shape[0], 16
+                        def one(r, carry):
+                            part = pl.ds(pl.multiple_of(r * step, step), step)
+                            value = acc[part, :].astype(f32)
+                            for term in terms:
+                                value = value + term[part, :].astype(f32)
+                            outs[a][part, :] = value
+                            return carry
+                        lax.fori_loop(0, rows // step, one, 0)
+
+    first(0); first(1); second(0); first(2); second(1); third(0); first(3); second(2); third(1); second(3); third(2); third(3)
+    for make, condition in pending:
+        if condition is None:
+            make().wait_send()
+        else:
+            pl.when(condition)(lambda make=make: make().wait_send())
+
+def full_reduce(parts, cid):
+    count = len(parts)
+    anys = pl.BlockSpec(memory_space=pl.ANY)
+    def body(*refs):
+        it = iter(refs)
+        take = lambda n: [next(it) for _ in range(n)]
+        reduce_all(*[take(count) for _ in range(9)], *it)
+    sem = pltpu.SemaphoreType.DMA
+    scratch = []
+    for lead, cut in (((4, 4), 1), ((4, 4), 1), ((4,), 2), ((4,), 2), ((4,), 1), ((4,), 1), ((5,), 1)):
+        scratch += [pltpu.VMEM(lead + (p.shape[2] // cut, p.shape[3]), p.dtype) for p in parts]
+    return pl.pallas_call(
+        body, in_specs=[anys] * count, out_specs=[pl.BlockSpec(memory_space=pltpu.VMEM)] * count,
+        out_shape=[jax.ShapeDtypeStruct(p.shape[2:], f32) for p in parts],
+        scratch_shapes=scratch + [sem((6, 5, count)), sem((6, 5, count)), sem((4, count)), sem((count,))],
+        compiler_params=pltpu.CompilerParams(collective_id=cid, has_side_effects=True, vmem_limit_bytes=62 * 2**20),
+        name="full_reduce")(*parts)
+def nt(left, right):
+    return lax.dot_general(left, right, (((1,), (1,)), ((), ())), preferred_element_type=f32)
+
+
+def tn(left, right):
+    return lax.dot_general(left, right, (((0,), (0,)), ((), ())), preferred_element_type=f32)
+
+
+def nn(left, right):
+    return lax.dot_general(left, right, (((1,), (0,)), ((), ())), preferred_element_type=f32)
+
+
+def expert_body(rows, width, half, tile, block, cut, *refs):
+    it = iter(refs)
+    take = lambda n: [next(it) for _ in range(n)]
+    x_hbm, c_hbm, s_hbm = take(3)
+    weights = [[take(2) for _ in range(3)] for _ in range(2)]
+    mix, gx, gs = take(3)
+    grads = [take(2) for _ in range(2)]
+    xv, cv, sv, wv, acc, hid_s, gate_s, up_s, gst, ostage, prev, stage = take(12)
+    wsem, insem, osem, psem, dsem, gsem = take(6)
+    hidden = 2 * half
+    shard = s_hbm.shape[1] - 8
+    per_tile = tile // shard
+    tiles = rows // tile
+    cuts = width // cut
+    steps = tiles * cuts
+    chip = lax.div(lax.axis_index("fsdp"), 2)
+    experts = (chip, chip + 1 - 2 * lax.rem(chip, 2))
+    lane = lax.broadcasted_iota(jnp.int32, (1, 128), 1)
+
+    def incoming(t, slot):
+        copies = []
+        for r in range(per_tile):
+            part = pl.ds(r * shard, shard)
+            copies += [
+                pltpu.make_async_copy(x_hbm.at[t * per_tile + r], xv.at[slot, part], insem.at[0, r, slot]),
+                pltpu.make_async_copy(c_hbm.at[t * per_tile + r], cv.at[slot, part], insem.at[1, r, slot]),
+                pltpu.make_async_copy(
+                    s_hbm.at[t * per_tile + r, pl.ds(0, shard)], sv.at[slot, part], insem.at[2, r, slot]
+                ),
+            ]
+        return copies
+
+    def spot(k):
+        t, n = lax.div(k, cuts), lax.rem(k, cuts)
+        return pl.ds(pl.multiple_of(t * tile, tile), tile), pl.ds(pl.multiple_of(n * cut, cut), cut)
+
+    def outgoing(k, slot):
+        r, c = spot(k)
+        return [
+            pltpu.make_async_copy(ostage.at[slot, i], ref.at[r, c], osem.at[i, slot])
+            for i, ref in enumerate((mix, gx))
+        ]
+
+    def earlier(k, slot):
+        r, c = spot(k)
+        return [
+            pltpu.make_async_copy(ref.at[r, c], prev.at[slot, i], psem.at[i, slot])
+            for i, ref in enumerate((mix, gx))
+        ]
+
+    for number in range(2):
+        loads = [
+            pltpu.make_async_copy(weights[number][i][h], wv.at[i, pl.ds(h * half, half)], wsem.at[i, h])
+            for i in range(3)
+            for h in range(2)
+        ]
+        for copy in loads:
+            copy.start()
+        for copy in incoming(0, 0):
+            copy.start()
+        if number:
+            for copy in earlier(0, 0):
+                copy.start()
+        acc[...] = jnp.zeros_like(acc)
+        for copy in loads:
+            copy.wait()
+        pick = (lane == experts[number]).astype(f32)
+
+        def one_tile(t, carry, number=number, pick=pick):
+            slot = lax.rem(t, 2)
+
+            @pl.when(t + 1 < tiles)
+            def _():
+                for copy in incoming(t + 1, 1 - slot):
+                    copy.start()
+
+            for copy in incoming(t, slot):
+                copy.wait()
+            share = jnp.sum(sv[slot] * pick, axis=1, keepdims=True)
+
+            def hidden_block(j, dots):
+                part = pl.ds(pl.multiple_of(j * block, block), block)
+                x, c = xv[slot], cv[slot]
+                gate_pre = nt(x, wv[0, part, :])
+                up_pre = nt(x, wv[1, part, :])
+                grad_raw = nt(c, wv[2, part, :])
+                sig = jax.nn.sigmoid(gate_pre)
+                silu = gate_pre * sig
+                hid = silu * up_pre
+                low = hid.astype(bf).astype(f32)
+                dots = dots + jnp.sum(low * grad_raw, axis=1, keepdims=True)
+                grad_hid = grad_raw * share
+                grad_gate = (grad_hid * up_pre * sig * (1.0 + gate_pre * (1.0 - sig))).astype(bf)
+                grad_up = (grad_hid * silu).astype(bf)
+                shared = (low * share).astype(bf)
+                hid_s[:, part] = shared
+                gate_s[:, part] = grad_gate
+                up_s[:, part] = grad_up
+                acc[0, part, :] += tn(grad_gate, x)
+                acc[1, part, :] += tn(grad_up, x)
+                acc[2, part, :] += tn(shared, c)
+                return dots
+
+            dots = lax.fori_loop(0, hidden // block, hidden_block, jnp.zeros((tile, 1), f32))
+            both = dots * pick
+            for r in range(per_tile):
+                turned = jnp.transpose(both[r * shard : (r + 1) * shard, :])[: gst.shape[1], :]
+                spot_now = t * per_tile + r
+                gst[spot_now] = gst[spot_now] + turned if number else turned
+
+            def column_block(n, inner):
+                k = t * cuts + n
+                place_now = lax.rem(k, 2)
+                columns = pl.ds(pl.multiple_of(n * cut, cut), cut)
+
+                @pl.when(k >= 2)
+                def _():
+                    for copy in outgoing(k - 2, place_now):
+                        copy.wait()
+
+                out = nn(hid_s[...], wv[2, :, columns])
+                back = nn(gate_s[...], wv[0, :, columns]) + nn(up_s[...], wv[1, :, columns])
+                if number:
+                    @pl.when(k + 1 < steps)
+                    def _():
+                        for copy in earlier(k + 1, 1 - place_now):
+                            copy.start()
+
+                    for copy in earlier(k, place_now):
+                        copy.wait()
+                    out = out + prev[place_now, 0].astype(f32)
+                    back = back + prev[place_now, 1].astype(f32)
+                ostage[place_now, 0] = out.astype(bf)
+                ostage[place_now, 1] = back.astype(bf)
+                for copy in outgoing(k, place_now):
+                    copy.start()
+                return inner
+
+            lax.fori_loop(0, cuts, column_block, 0)
+            return carry
+
+        lax.fori_loop(0, tiles, one_tile, 0)
+        for k in (steps - 2, steps - 1):
+            for copy in outgoing(k, k % 2):
+                copy.wait()
+        chunk = stage.shape[1]
+        per_half = half // chunk
+        spots = [(i, h, r) for i in range(3) for h in range(2) for r in range(per_half)]
+
+        def flush(k, number=number):
+            i, h, r = spots[k]
+            return pltpu.make_async_copy(
+                stage.at[k % 2], grads[number][h].at[i, pl.ds(r * chunk, chunk)], dsem.at[k % 2]
+            )
+
+        for k, (i, h, r) in enumerate(spots):
+            if k >= 2:
+                flush(k - 2).wait()
+            first = h * half + r * chunk
+            stage[k % 2] = acc[i, first : first + chunk, :].astype(bf)
+            flush(k).start()
+        for k in (len(spots) - 2, len(spots) - 1):
+            flush(k).wait()
+    last = pltpu.make_async_copy(gst, gs, gsem)
+    last.start()
+    last.wait()
+
+
+def expert_pass(x_all, c_all, s_all, weights, gs_rows):
+    blocks, shard, width = x_all.shape
+    rows = blocks * shard
+    half = weights[0][0][0].shape[0]
+    hidden = 2 * half
+    tile, block, cut = 2 * shard, half, 512
+    anys = pl.BlockSpec(memory_space=pl.ANY)
+    sem = pltpu.SemaphoreType.DMA
+    flat = [w for one in weights for pair in one for w in pair]
+    shapes = [
+        jax.ShapeDtypeStruct((rows, width), bf),
+        jax.ShapeDtypeStruct((rows, width), bf),
+        jax.ShapeDtypeStruct((blocks, gs_rows, shard), f32),
+    ] + [jax.ShapeDtypeStruct((3, half, width), bf)] * 4
+    return pl.pallas_call(
+        functools.partial(expert_body, rows, width, half, tile, block, cut),
+        in_specs=[anys] * (3 + len(flat)),
+        out_specs=[anys] * 7,
+        out_shape=shapes,
+        scratch_shapes=[
+            pltpu.VMEM((2, tile, width), bf),
+            pltpu.VMEM((2, tile, width), bf),
+            pltpu.VMEM((2, tile, 128), f32),
+            pltpu.VMEM((3, hidden, width), bf),
+            pltpu.VMEM((3, hidden, width), f32),
+            pltpu.VMEM((tile, hidden), bf),
+            pltpu.VMEM((tile, hidden), bf),
+            pltpu.VMEM((tile, hidden), bf),
+            pltpu.VMEM((blocks, gs_rows, shard), f32),
+            pltpu.VMEM((2, 2, tile, cut), bf),
+            pltpu.VMEM((2, 2, tile, cut), bf),
+            pltpu.VMEM((2, 64, width), bf),
+            sem((3, 2)),
+            sem((3, 2, 2)),
+            sem((2, 2)),
+            sem((2, 2)),
+            sem((2,)),
+            sem,
+        ],
+        compiler_params=pltpu.CompilerParams(vmem_limit_bytes=63 * 2**20),
+        name="expert_pass",
+    )(x_all, c_all, s_all, *flat)
+def dense_layer(
+    tokens,
+    w_query,
+    w_key,
+    w_value,
+    w_out,
+    w_router,
+    gain_attn,
+    gain_moe,
+    w_gate,
+    w_up,
+    w_down,
+    routes,
+    doc_lengths,
+    clip_limit,
+    cotangent,
+):
+    devices = lax.axis_size("fsdp")
+    device = lax.axis_index("fsdp")
+    tok_rows = tokens.shape[0]
+    model_width = tokens.shape[1]
+    weight_rows = w_query.shape[0]
+    head_count = clip_limit.shape[0]
+    head_size = model_width // head_count
+    experts = w_router.shape[1]
+    seq_len = devices * tok_rows // doc_lengths.shape[0]
+    score_scale = head_size ** (-0.5)
+    wide_width = 3 * model_width
+    extra = jnp.pad(
+        jnp.concatenate((w_router, gain_attn[:, None], gain_moe[:, None]), axis=1),
+        ((0, 0), (0, 128 - experts - 2)),
+    )
+    wide_own = jnp.concatenate((w_query, w_key, w_value, extra), axis=1)
+    wide_full, out_full = full_gather([wide_own, w_out], 2)
+    wide_full = wide_full.reshape(model_width, wide_width + 128)
+    out_full = out_full.reshape(model_width, model_width)
+    later = lax.optimization_barrier((out_full, cotangent, w_gate, w_up, w_down))
+    out_full, cot_own, gate_own, up_own, down_own = later
+    planes = [
+        [index_of(z, y, x, core) for z in range(4) for y in range(2)] for x in range(2) for core in range(2)
+    ]
+    c_all = lax.all_gather(cot_own, "fsdp", axis_index_groups=planes)
+    x_weights = [swapped(w, "fsdp", 1) for w in (gate_own, up_own, down_own)]
+    core_weights = [swapped(w, "fsdp", 0) for w in (gate_own, up_own, down_own)]
+    corner_weights = [swapped(w, "fsdp", 0) for w in x_weights]
+    expert_weights = [
+        list(zip((gate_own, up_own, down_own), core_weights)),
+        list(zip(x_weights, corner_weights)),
+    ]
+    router_full = wide_full[:, wide_width : wide_width + experts]
+    gain_one = wide_full[:, wide_width + experts]
+    gain_two = wide_full[:, wide_width + experts + 1]
+    token_values = tokens.astype(f32)
+    scale_one = rms_scale(token_values)
+    attn_gain = gain_one.astype(f32)
+    normed_attn = (token_values * scale_one * attn_gain).astype(bf)
+    qkv = jnp.dot(normed_attn, wide_full, preferred_element_type=f32).astype(bf)
+    queries = qkv[:, :model_width]
+    kv_own = qkv[:, model_width:wide_width]
+    reach_count = (HALF - 2) // tok_rows + 1
+    offsets = list(range(reach_count, 0, -1)) + list(range(-1, -reach_count - 1, -1))
+    arrived = [passed_along(kv_own, "fsdp", offset) for offset in offsets]
+    kv_rows = jnp.concatenate(arrived[:reach_count] + [kv_own] + arrived[reach_count:], axis=0)
+    ordered = offsets[:reach_count] + [0] + offsets[reach_count:]
+    row_index = jnp.arange(tok_rows, dtype=jnp.int32)
+    query_places = device * tok_rows + row_index
+    key_places = jnp.concatenate([(device - offset) * tok_rows + row_index for offset in ordered])
+    query_docs = document_of(query_places, doc_lengths, seq_len)
+    key_docs = document_of(key_places, doc_lengths, seq_len)
+    visible = (
+        (query_docs[:, None] == key_docs[None, :])
+        & (key_docs[None, :] >= 0)
+        & (jnp.abs(query_places[:, None] - key_places[None, :]) < HALF)
+    )
+    key_count = kv_rows.shape[0]
+    query_heads = queries.reshape(tok_rows, head_count, head_size)
+    key_heads = kv_rows[:, :model_width].reshape(key_count, head_count, head_size)
+    value_heads = kv_rows[:, model_width:].reshape(key_count, head_count, head_size)
+
+    def scores_of():
+        raw_scores = (
+            jnp.einsum("qhd,khd->hqk", query_heads, key_heads, preferred_element_type=f32)
+            * score_scale
+        )
+        return jnp.where(visible[None], raw_scores, masked)
+
+    scores = scores_of()
+    head_top = jnp.max(scores, axis=2, keepdims=True)
+    exponents = jnp.exp(scores - head_top)
+    totals = jnp.sum(exponents, axis=2, keepdims=True)
+    log_total = head_top + jnp.log(totals)
+    probs_low = (exponents / totals).astype(bf)
+    own_top = jnp.max(head_top, axis=(1, 2))
+    context = (
+        jnp.einsum("hqk,khd->qhd", probs_low, value_heads, preferred_element_type=f32)
+        .reshape(tok_rows, model_width)
+        .astype(bf)
+    )
+    attended = token_values + jnp.dot(context, out_full, preferred_element_type=f32)
+    scale_two = rms_scale(attended)
+    moe_gain = gain_two.astype(f32)
+    normed_moe = (attended * scale_two * moe_gain).astype(bf)
+    logits = jnp.dot(normed_moe, router_full, preferred_element_type=f32)
+    named = jnp.any(routes[:, :, None] == jnp.arange(experts, dtype=jnp.int32)[None, None, :], axis=1)
+    chosen = jnp.where(named, logits, masked)
+    lifted = jnp.where(named, jnp.exp(logits - jnp.max(chosen, axis=1, keepdims=True)), 0.0)
+    gate_share = lifted / jnp.sum(lifted, axis=1, keepdims=True)
+    share_rows = jnp.concatenate(
+        (
+            jnp.pad(gate_share, ((0, 0), (0, 128 - experts))),
+            jnp.pad(own_top[None, :], ((0, 7), (0, 128 - head_count))),
+        ),
+        axis=0,
+    )
+    x_all, s_all = plane_gather([normed_moe, share_rows], 0)
+    head_max = jnp.max(s_all[:, tok_rows, :head_count], axis=0)
+    head_max = jnp.maximum(head_max, swapped(head_max, "fsdp", 0))
+    head_max = jnp.maximum(head_max, swapped(head_max, "fsdp", 1))
+    factor = clip_limit / jnp.maximum(head_max, clip_limit)
+    columns = jnp.repeat(jnp.sqrt(factor), head_size)
+    clipped_query = (w_query.astype(f32) * columns[None, :]).astype(bf)
+    clipped_key = (w_key.astype(f32) * columns[None, :]).astype(bf)
+    mix_part, gx_part, gs_part, own_grads, core_grads, x_grads, corner_grads = expert_pass(
+        x_all, c_all, s_all, expert_weights, experts
+    )
+    plane_shape = x_all.shape
+    grad_from_experts, grad_share, mixture = plane_reduce(
+        [gx_part.reshape(plane_shape), gs_part, mix_part.reshape(plane_shape)], 1
+    )
+    mixed = (attended + mixture.astype(f32)).astype(bf)
+    grad_share = jnp.transpose(grad_share)
+    core_terms, corner_terms = swapped((core_grads, corner_grads), "fsdp", 0)
+    own_sum = own_grads.astype(f32) + core_terms.astype(f32)
+    x_sum = (x_grads.astype(f32) + corner_terms.astype(f32)).astype(bf)
+    x_terms = swapped(x_sum, "fsdp", 1)
+    expert_grads = own_sum + x_terms.astype(f32)
+    grad_gate, grad_up, grad_down = expert_grads[0], expert_grads[1], expert_grads[2]
+    grad_mixed = cotangent.astype(f32)
+    grad_logits = gate_share * (grad_share - jnp.sum(gate_share * grad_share, axis=1, keepdims=True))
+    grad_router_part = jnp.dot(normed_moe.astype(f32).T, grad_logits, precision=highest)
+    grad_normed_moe = grad_from_experts.astype(f32) + jnp.dot(
+        grad_logits, router_full.astype(f32).T, precision=highest
+    )
+    grad_from_norm, grad_gain_two = norm_back(grad_normed_moe, attended, scale_two, moe_gain)
+    grad_attended = grad_mixed + grad_from_norm
+    grad_attended_low = grad_attended.astype(bf)
+    grad_out_part = contract(context, grad_attended_low, 0, 0).astype(bf)
+    grad_context = (
+        contract(grad_attended_low, out_full, 1, 1)
+        .astype(bf)
+        .reshape(tok_rows, head_count, head_size)
+    )
+    probs = jnp.exp(scores_of() - log_total)
+    probs_back = probs.astype(bf)
+    grad_values = jnp.einsum("hqk,qhd->khd", probs_back, grad_context, preferred_element_type=f32)
+    grad_probs = jnp.einsum("qhd,khd->hqk", grad_context, value_heads, preferred_element_type=f32)
+    grad_scores = (
+        probs * (grad_probs - jnp.sum(probs * grad_probs, axis=2, keepdims=True))
+    ).astype(bf)
+    grad_queries = (
+        (
+            jnp.einsum("hqk,khd->qhd", grad_scores, key_heads, preferred_element_type=f32)
+            * score_scale
+        )
+        .reshape(tok_rows, model_width)
+        .astype(bf)
+    )
+    grad_keys = (
+        jnp.einsum("hqk,qhd->khd", grad_scores, query_heads, preferred_element_type=f32)
+        * score_scale
+    )
+    grad_kv = jnp.concatenate(
+        (grad_keys.reshape(key_count, model_width), grad_values.reshape(key_count, model_width)),
+        axis=1,
+    )
+    grad_blocks = [
+        grad_kv[position * tok_rows : (position + 1) * tok_rows] for position in range(len(ordered))
+    ]
+    own_block = grad_blocks[reach_count]
+    remote_blocks = grad_blocks[:reach_count] + grad_blocks[reach_count + 1 :]
+    returned = [
+        passed_along(grad_block.astype(bf), "fsdp", -offset).astype(grad_block.dtype)
+        for grad_block, offset in zip(remote_blocks, offsets)
+    ]
+    grad_kv_low = reduce(jnp.add, returned, own_block).astype(bf)
+    grad_qkv = jnp.concatenate((grad_queries, grad_kv_low), axis=1)
+    grad_qkv_part = contract(normed_attn, grad_qkv, 0, 0).astype(bf)
+    grad_normed_attn = contract(jnp.pad(grad_qkv, ((0, 0), (0, 128))), wide_full, 1, 1)
+    grad_from_first, grad_gain_one = norm_back(grad_normed_attn, token_values, scale_one, attn_gain)
+    grad_tokens = grad_attended + grad_from_first
+    extra_part = jnp.pad(
+        jnp.concatenate((grad_router_part, grad_gain_one[:, None], grad_gain_two[:, None]), axis=1),
+        ((0, 0), (0, 128 - experts - 2)),
+    )
+    owners = (devices // 2, 2, weight_rows)
+    qkv_sum, out_sum, extra_sum = full_reduce(
+        [
+            grad_qkv_part.reshape(owners + (wide_width,)),
+            grad_out_part.reshape(owners + (model_width,)),
+            extra_part.reshape(owners + (128,)),
+        ],
+        3,
+    )
+    return (
+        mixed,
+        grad_tokens,
+        qkv_sum[:, :model_width],
+        qkv_sum[:, model_width : 2 * model_width],
+        qkv_sum[:, 2 * model_width :],
+        out_sum,
+        extra_sum[:, :experts],
+        extra_sum[:, experts],
+        extra_sum[:, experts + 1],
+        grad_gate,
+        grad_up,
+        grad_down,
+        clipped_query,
+        clipped_key,
+    )
+
+
+def chosen_layer(mesh):
+    def layer(*arrays):
+        experts, top_count = arrays[5].shape[1], arrays[11].shape[1]
+        if mesh.shape["fsdp"] == 32 and 2 * top_count >= experts:
+            return dense_layer(*arrays)
+        return routed_layer(*arrays)
+
+    return layer
+
+
 def solution(mesh):
     placed = (
         P("fsdp", None),
@@ -427,7 +1302,7 @@
         P("fsdp", None),
     )
     return jax.shard_map(
-        per_device,
+        chosen_layer(mesh),
         mesh=mesh,
         in_specs=placed,
         out_specs=(

time: 3660 us -> 1510 us (0.41)
  waiting for transfers between devices: 1490 us -> 244 us
  Pallas kernels: 0 us -> 920 us
  matrix products: 846 us -> 116 us
  blocking collectives: 524 us -> 0 us
  local copies, waits for them, and re-layouts: 476 us -> 75.1 us
  other arithmetic: 169 us -> 81.3 us
  starting transfers between devices: 126 us -> 51.9 us
    pallas_call x0 -> x5, Pallas kernels: none -> 920 us  [the longest x1 246 us: full_reduce(): pl.pallas_call(body, in_specs=[anys] * count, out_specs=[pl.BlockSpec(mem...]
    all_to_all x4 -> x0, waiting for transfers between devices: 716 us -> none  [the longest x1 257 us: per_device(): lax.all_to_all(grad_outgoing, 'fsdp', split_axis=0, concat_axis=0, tiled=...]
    dot_general x151 -> x4, matrix products: 645 us -> 36.1 us  [contract(): lax.dot_general(left, right, (((left_dim,), (right_dim,)), ((), ())), pre...]
    reduce_scatter x4 -> x0, waiting for transfers between devices: 470 us -> none  [the longest x1 187 us: per_device(): lax.psum_scatter(grad_kv_part[:, :model_width], 'fsdp', scatter_dimension...]
    all_to_all x1 -> x0, blocking collectives: 277 us -> none  [per_device(): lax.all_to_all(grad_returning, 'fsdp', split_axis=0, concat_axis=0, tiled...]
    while x528 -> x0, local copies, waits for them, and re-layouts: 155 us -> none
    dot_general x83 -> x10, matrix products: 191 us -> 72 us  [the longest x1 15.4 us: dense_layer(): jnp.einsum('qhd,khd->hqk', grad_context, value_heads, preferred_element_t...]
    all_gather x1 -> x0, blocking collectives: 110 us -> none  [per_device(): lax.all_gather(w_router, 'fsdp', axis=0, tiled=True)]
  transfers between devices with their start and end apart: 27 -> 23, of which waited for: 13 -> 11; matrix products, arithmetic and copies ran while one was open for 12% -> 12% of each run, Pallas kernels for 0% -> 23%
where the time goes in v1:
time: 1510 us; the launch traced here: 1500 us
  Pallas kernels  920 us (61%)
  waiting for transfers between devices  244 us (16%)
  matrix products  116 us (8%)
  other arithmetic  81.3 us (5%)
  local copies, waits for them, and re-layouts  75.1 us (5%)
  starting transfers between devices  51.9 us (3%)
    pallas_call x1, Pallas kernels, full_reduce(): pl.pallas_call(body, in_specs=[anys] * count, out_specs=[pl.BlockSpec(mem...  246 us
    pallas_call x1, Pallas kernels, expert_pass(): pl.pallas_call(functools.partial(expert_body, rows, width, half, tile, bl...  236 us
    ppermute x8, waiting for transfers between devices, passed_along(): return lax.ppermute(x, axis, pairs)  227 us
    pallas_call x1, Pallas kernels, plane_reduce(): pl.pallas_call(body, in_specs=[anys] * count, out_specs=[anys] * count, o...  190 us
    pallas_call x1, Pallas kernels, full_gather(): pl.pallas_call(body, in_specs=[anys] * count, out_specs=[anys] * count, o...  144 us
    pallas_call x1, Pallas kernels, plane_gather(): pl.pallas_call(body, in_specs=[anys] * count, out_specs=[anys] * count, o...  104 us
    dot_general x4, matrix products, contract(): lax.dot_general(left, right, (((left_dim,), (right_dim,)), ((), ())), pre...  36.1 us
    unnamed x84, local copies, waits for them, and re-layouts  34 us
  transfers between devices with their start and end apart: 23, of which 11 were waited for; matrix products, arithmetic and copies ran while one was open for 12% of the time, Pallas kernels for 23%

profile of v1, /device:TPU:16, one launch (start us, length us, event | category | flops | bytes accessed | tf_op | source)
XLA Modules:
  0.0 1502.5 jit_solution(12963677530968727923)
XLA Ops:
  10.2 143.8 %full_gather.1 = (bf16[32,64,6272]{2,1,0:T(8,128)(2,1)}, bf16[32,64,2048]{2,1,0:T(8,128)(2,1)}) custom-call(bf16[64,6272]{1,0:T(8,128)(2,1)} %fusion.40.refs_0_, bf16[64,2048]{1,0:T(8,128)(2,1)} %refs_1_.1), custom_call_target="tpu_custom_call" | custom-call | tf_op jit(solution)/shard_map/full_gather/pallas_call | solution.py:605
  156.3 12.3 convolution_convert_fusion.1
  191.6 83.3 %collective-permute-done = bf16[256,4096]{1,0:T(8,128)(2,1)} collective-permute-done((bf16[256,4096]{1,0:T(8,128)(2,1)}, bf16[256,4096]{1,0:T(8,128)(2,1)}, u32[]{:S(2)}, u32[]{:S(2)}) %collective-permute-start) | collective-permute-done | bytes 2097184 | tf_op jit(solution)/shard_map/ppermute | solution.py:22
  280.9 32.3 %collective-permute-done.1 = bf16[256,4096]{1,0:T(8,128)(2,1)} collective-permute-done((bf16[256,4096]{1,0:T(8,128)(2,1)}, bf16[256,4096]{1,0:T(8,128)(2,1)}, u32[]{:S(2)}, u32[]{:S(2)}) %collective-permute-start.1) | collective-permute-done | bytes 2097184 | tf_op jit(solution)/shard_map/ppermute | solution.py:22
  313.2 19.7 %collective-permute-start.9 = (bf16[512,2048]{1,0:T(8,128)(2,1)}, bf16[512,2048]{1,0:T(8,128)(2,1)}, u32[]{:S(2)}, u32[]{:S(2)}) collective-permute-start(bf16[512,2048]{1,0:T(8,128)(2,1)} %refs_5_), channel_id=1, source_target_pairs={{0,2},{2,0},{1,3},{3,1},{4,6},{6,4},{5,7},{7,5},{8,10},{10,8},{9,1... | collective-permute-start | bytes 6291464 | tf_op jit(solution)/shard_map/ppermute | solution.py:32
  344.1 11.3 slice_bitcast_fusion
  355.4 7.8 copy.98
  377.9 12.0 fusion.33
  400.4 104.0 %plane_gather.1 = (bf16[8,256,2048]{2,1,0:T(8,128)(2,1)}, f32[8,264,128]{2,1,0:T(8,128)}) custom-call(bf16[256,2048]{1,0:T(8,128)(2,1)} %copy-done.11, f32[264,128]{1,0:T(8,128)} %copy.86.refs_1_), custom_call_target="tpu_custom_call" | custom-call | tf_op jit(solution)/shard_map/plane_gather/pallas_call | solution.py:507
  522.9 235.5 %expert_pass.1 = (bf16[2048,2048]{1,0:T(8,128)(2,1)}, bf16[2048,2048]{1,0:T(8,128)(2,1)}, f32[8,16,256]{2,1,0:T(8,128)}, bf16[3,512,2048]{2,1,0:T(8,128)(2,1)}, ...) custom-call(bf16[8,256,2048]{2,1,0:T(8,128)(2,1)} %get-tuple-element.39.refs_0_, ...), custom_call_target="tpu_custom_call" | custom-call | tf_op jit(solution)/shard_map/expert_pass/pallas_call | solution.py:1027
  758.4 189.9 %plane_reduce.1 = (bf16[256,2048]{1,0:T(8,128)(2,1)}, f32[16,256]{1,0:T(8,128)}, bf16[256,2048]{1,0:T(8,128)(2,1)}) custom-call(bf16[8,256,2048]{2,1,0:T(8,128)(2,1)} %bitcast.100, f32[8,16,256]{2,1,0:T(8,128)} %get-tuple-element.46.refs_1_, bf16[8,256,2048]{2,1,0:T(8,128)(2,1)} %bitcast.99), custom_call_target="tpu_custom_call" | custom-call | tf_op jit(solution)/shard_map/plane_reduce/pallas_call | solution.py:706
  960.0 15.4 %multiply_reduce_fusion = (f32[16,256]{1,0:T(8,128)S(1)}, f32[16,256,1280]{2,1,0:T(8,128)}) fusion(f32[16,256,1280]{2,1,0:T(8,128)} %copy-done, f32[16,256]{1,0:T(8,128)S(1)} %log_add_fusion, bf16[256,16,128]{0,2,1:T(8,128)(2,1)S(1)} %bitcast.95, bf16[160,16,8,128]{3,2,1,0:T(8,128)(2,1)} %get-tuple-element.133), kind=kOutput, calls=%fused_computation.6 | convolution fusion | flops 1357901824 | bytes 48267264 | tf_op jit(solution)/shard_map/qhd,khd->hqk/dot_general | solution.py:1210
  975.4 11.3 fusion.3
  986.7 14.1 multiply_convert_fusion
  1004.7 12.7 fusion
  1045.1 7.5 multiply_convert_fusion.1
  1052.5 87.7 %collective-permute-done.16 = bf16[256,4096]{0,1:T(8,128)(2,1)} collective-permute-done((bf16[256,4096]{0,1:T(8,128)(2,1)}, bf16[256,4096]{0,1:T(8,128)(2,1)}, u32[]{:S(2)}, u32[]{:S(2)}) %collective-permute-start.16) | collective-permute-done | bytes 2097184 | tf_op jit(solution)/shard_map/ppermute | solution.py:22
  1140.3 23.8 %collective-permute-done.13 = bf16[256,4096]{0,1:T(8,128)(2,1)} collective-permute-done((bf16[256,4096]{0,1:T(8,128)(2,1)}, bf16[256,4096]{0,1:T(8,128)(2,1)}, u32[]{:S(2)}, u32[]{:S(2)}) %collective-permute-start.13) | collective-permute-done | bytes 2097184 | tf_op jit(solution)/shard_map/ppermute | solution.py:22
  1169.5 10.9 add_convert_fusion
  1183.0 13.9 fusion.30
  1200.6 13.2 convolution_convert_fusion
  1213.8 246.3 %full_reduce.1 = (f32[64,6144]{1,0:T(8,128)}, f32[64,2048]{1,0:T(8,128)}, f32[64,128]{1,0:T(8,128)}) custom-call(bf16[16,2,64,6144]{3,2,1,0:T(8,128)(2,1)} %bitcast.81, bf16[16,2,64,2048]{3,2,1,0:T(8,128)(2,1)} %bitcast.88, f32[16,2,64,128]{3,2,1,0:T(8,128)} %bitcast.104), custom_call_target="tpu_custom_call" | custom-call | tf_op jit(solution)/shard_map/full_reduce/pallas_call | solution.py:827
  1469.2 15.5 %convert_add_fusion = f32[3,512,2048]{2,1,0:T(8,128)} fusion(bf16[3,512,2048]{2,1,0:T(8,128)(2,1)} %collective-permute-done.19, bf16[3,512,2048]{2,1,0:T(8,128)(2,1)} %collective-permute-done.17, bf16[3,512,2048]{2,1,0:T(8,128)(2,1)} %get-tuple-element.54), kind=kLoop, calls=%fused_computation.13 | loop fusion | flops 15728640 | bytes 31457280 | tf_op jit(solution)/shard_map/add | solution.py:1190
  1484.8 9.9 slice_bitcast_fusion.1
  (187 shorter events, 153.2 us)
Async XLA Ops:
  7.2 515.7 %all-gather.3.cloned.1.call-start = ((), (), s32[]{:S(2)}) async-start(), calls=%async_computation | async-start | bytes 9437184 | tf_op jit(solution)/shard_map/all_gather | solution.py:1096
  171.8 103.1 %collective-permute-start = (bf16[256,4096]{1,0:T(8,128)(2,1)}, bf16[256,4096]{1,0:T(8,128)(2,1)}, u32[]{:S(2)}, u32[]{:S(2)}) collective-permute-start(bf16[256,4096]{1,0:T(8,128)(2,1)} %slice.93), channel_id=1, source_target_pairs={{0,2},{1,3},{2,4},{3,5},{4,6},{5,7},{6,8},{7,9},{8,10},{9,11},{10,... | collective-permute-start | bytes 6291464 | tf_op jit(solution)/shard_map/ppermute | solution.py:22
  175.4 137.9 %collective-permute-start.1 = (bf16[256,4096]{1,0:T(8,128)(2,1)}, bf16[256,4096]{1,0:T(8,128)(2,1)}, u32[]{:S(2)}, u32[]{:S(2)}) collective-permute-start(bf16[256,4096]{1,0:T(8,128)(2,1)} %slice.93), channel_id=1, source_target_pairs={{0,1},{1,2},{2,3},{3,4},{4,5},{5,6},{6,7},{7,8},{8,9},{9,10},{10,1... | collective-permute-start | bytes 6291464 | tf_op jit(solution)/shard_map/ppermute | solution.py:22
  177.5 160.3 %collective-permute-start.2 = (bf16[256,4096]{1,0:T(8,128)(2,1)}, bf16[256,4096]{1,0:T(8,128)(2,1)}, u32[]{:S(2)}, u32[]{:S(2)}) collective-permute-start(bf16[256,4096]{1,0:T(8,128)(2,1)} %slice.93), channel_id=1, source_target_pairs={{1,0},{2,1},{3,2},{4,3},{5,4},{6,5},{7,6},{8,7},{9,8},{10,9},{11,1... | collective-permute-start | bytes 6291464 | tf_op jit(solution)/shard_map/ppermute | solution.py:22
  182.8 158.2 %collective-permute-start.3 = (bf16[256,4096]{1,0:T(8,128)(2,1)}, bf16[256,4096]{1,0:T(8,128)(2,1)}, u32[]{:S(2)}, u32[]{:S(2)}) collective-permute-start(bf16[256,4096]{1,0:T(8,128)(2,1)} %slice.93), channel_id=1, source_target_pairs={{2,0},{3,1},{4,2},{5,3},{6,4},{7,5},{8,6},{9,7},{10,8},{11,9},{12,... | collective-permute-start | bytes 6291464 | tf_op jit(solution)/shard_map/ppermute | solution.py:22
  185.4 321.2 %collective-permute-start.4 = (bf16[512,2048]{1,0:T(8,128)(2,1)}, bf16[512,2048]{1,0:T(8,128)(2,1)}, u32[]{:S(2)}, u32[]{:S(2)}) collective-permute-start(bf16[512,2048]{1,0:T(8,128)(2,1)} %refs_3_), channel_id=1, source_target_pairs={{0,1},{1,0},{2,3},{3,2},{4,5},{5,4},{6,7},{7,6},{8,9},{9,8},{10,11... | collective-permute-start | bytes 6291464 | tf_op jit(solution)/shard_map/ppermute | solution.py:32
  275.0 231.9 %collective-permute-start.7 = (bf16[512,2048]{1,0:T(8,128)(2,1)}, bf16[512,2048]{1,0:T(8,128)(2,1)}, u32[]{:S(2)}, u32[]{:S(2)}) collective-permute-start(bf16[512,2048]{1,0:T(8,128)(2,1)} %refs_3_), channel_id=1, source_target_pairs={{0,2},{2,0},{1,3},{3,1},{4,6},{6,4},{5,7},{7,5},{8,10},{10,8},{9,1... | collective-permute-start | bytes 6291464 | tf_op jit(solution)/shard_map/ppermute | solution.py:32
  313.2 193.9 %collective-permute-start.9 = (bf16[512,2048]{1,0:T(8,128)(2,1)}, bf16[512,2048]{1,0:T(8,128)(2,1)}, u32[]{:S(2)}, u32[]{:S(2)}) collective-permute-start(bf16[512,2048]{1,0:T(8,128)(2,1)} %refs_5_), channel_id=1, source_target_pairs={{0,2},{2,0},{1,3},{3,1},{4,6},{6,4},{5,7},{7,5},{8,10},{10,8},{9,1... | collective-permute-start | bytes 6291464 | tf_op jit(solution)/shard_map/ppermute | solution.py:32
  337.8 169.7 %collective-permute-start.11 = (bf16[512,2048]{1,0:T(8,128)(2,1)}, bf16[512,2048]{1,0:T(8,128)(2,1)}, u32[]{:S(2)}, u32[]{:S(2)}) collective-permute-start(bf16[512,2048]{1,0:T(8,128)(2,1)} %refs_7_), channel_id=1, source_target_pairs={{0,2},{2,0},{1,3},{3,1},{4,6},{6,4},{5,7},{7,5},{8,10},{10,8},{9,1... | collective-permute-start | bytes 6291464 | tf_op jit(solution)/shard_map/ppermute | solution.py:32
  505.2 1.2 collective-permute-start.20
  506.4 4.5 collective-permute-start.5
  506.6 7.3 collective-permute-start.6
  506.9 10.0 collective-permute-start.8
  507.1 3.5 collective-permute-start.21
  507.5 12.4 collective-permute-start.10
  510.7 12.2 collective-permute-start.12
  758.4 190.9 %copy-start.4 = (f32[256,2048]{1,0:T(8,128)S(1)}, f32[256,2048]{1,0:T(8,128)}, u32[]{:S(2)}) copy-start(f32[256,2048]{1,0:T(8,128)} %copy-done.3) | copy-start | bytes 6291460
  986.7 182.7 %collective-permute-start.18 = (bf16[3,512,2048]{2,1,0:T(8,128)(2,1)}, bf16[3,512,2048]{2,1,0:T(8,128)(2,1)}, u32[]{:S(2)}, u32[]{:S(2)}) collective-permute-start(bf16[3,512,2048]{2,1,0:T(8,128)(2,1)} %get-tuple-element.57), channel_id=1, source_target_pairs={{0,1},{1,0},{2,3},{3,2},{4,5},{5,4},{6,7},{7,6},{8,9},{9,8},{10,11... | collective-permute-start | bytes 18874376 | tf_op jit(solution)/shard_map/ppermute | solution.py:32
  1024.1 116.2 %collective-permute-start.16 = (bf16[256,4096]{0,1:T(8,128)(2,1)}, bf16[256,4096]{0,1:T(8,128)(2,1)}, u32[]{:S(2)}, u32[]{:S(2)}) collective-permute-start(bf16[256,4096]{0,1:T(8,128)(2,1)} %get-tuple-element.130), channel_id=1, source_target_pairs={{0,2},{1,3},{2,4},{3,5},{4,6},{5,7},{6,8},{7,9},{8,10},{9,11},{10,... | collective-permute-start | bytes 6291464 | tf_op jit(solution)/shard_map/ppermute | solution.py:22
  1026.6 113.7 %collective-permute-start.15 = (bf16[256,4096]{0,1:T(8,128)(2,1)}, bf16[256,4096]{0,1:T(8,128)(2,1)}, u32[]{:S(2)}, u32[]{:S(2)}) collective-permute-start(bf16[256,4096]{0,1:T(8,128)(2,1)} %get-tuple-element.131), channel_id=1, source_target_pairs={{0,1},{1,2},{2,3},{3,4},{4,5},{5,6},{6,7},{7,8},{8,9},{9,10},{10,1... | collective-permute-start | bytes 6291464 | tf_op jit(solution)/shard_map/ppermute | solution.py:22
  1028.8 111.5 %collective-permute-start.14 = (bf16[256,4096]{0,1:T(8,128)(2,1)}, bf16[256,4096]{0,1:T(8,128)(2,1)}, u32[]{:S(2)}, u32[]{:S(2)}) collective-permute-start(bf16[256,4096]{0,1:T(8,128)(2,1)} %get-tuple-element.132), channel_id=1, source_target_pairs={{1,0},{2,1},{3,2},{4,3},{5,4},{6,5},{7,6},{8,7},{9,8},{10,9},{11,1... | collective-permute-start | bytes 6291464 | tf_op jit(solution)/shard_map/ppermute | solution.py:22
  1034.0 130.0 %collective-permute-start.13 = (bf16[256,4096]{0,1:T(8,128)(2,1)}, bf16[256,4096]{0,1:T(8,128)(2,1)}, u32[]{:S(2)}, u32[]{:S(2)}) collective-permute-start(bf16[256,4096]{0,1:T(8,128)(2,1)} %get-tuple-element.129), channel_id=1, source_target_pairs={{2,0},{3,1},{4,2},{5,3},{6,4},{7,5},{8,6},{9,7},{10,8},{11,9},{12,... | collective-permute-start | bytes 6291464 | tf_op jit(solution)/shard_map/ppermute | solution.py:22
  1140.3 328.9 %collective-permute-start.17 = (bf16[3,512,2048]{2,1,0:T(8,128)(2,1)}, bf16[3,512,2048]{2,1,0:T(8,128)(2,1)}, u32[]{:S(2)}, u32[]{:S(2)}) collective-permute-start(bf16[3,512,2048]{2,1,0:T(8,128)(2,1)} %get-tuple-element.55), channel_id=1, source_target_pairs={{0,1},{1,0},{2,3},{3,2},{4,5},{5,4},{6,7},{7,6},{8,9},{9,8},{10,11... | collective-permute-start | bytes 18874376 | tf_op jit(solution)/shard_map/ppermute | solution.py:32
  1180.4 288.9 %collective-permute-start.19 = (bf16[3,512,2048]{2,1,0:T(8,128)(2,1)}, bf16[3,512,2048]{2,1,0:T(8,128)(2,1)}, u32[]{:S(2)}, u32[]{:S(2)}) collective-permute-start(bf16[3,512,2048]{2,1,0:T(8,128)(2,1)} %add_convert_fusion), channel_id=1, source_target_pairs={{0,2},{2,0},{1,3},{3,1},{4,6},{6,4},{5,7},{7,5},{8,10},{10,8},{9,1... | collective-permute-start | bytes 18874376 | tf_op jit(solution)/shard_map/ppermute | solution.py:32
  (36 other events, 939.6 us)
Sparse Core Ops, SparseCore 0:
  185.5 169.1 all-gather.2

commit v2 on v1

--- a/solution.py
+++ b/solution.py
@@ -449,70 +449,7 @@
     near = z + 1 - 2 * lax.rem(z, 2)
     return [z, near, jnp.where(low, 2, 1), jnp.where(low, 3, 0)]
 
-def gather_plane(ins, outs, ssem, rsem, lsem):
-    count = len(ins)
-    z, y, x, core = place()
-    mid = (z == 1) | (z == 2)
-    up, down = z < 3, z > 0
-    y_dev = index_of(z, 1 - y, x, core)
-    up_dev = index_of(jnp.minimum(z + 1, 3), y, x, core)
-    down_dev = index_of(jnp.maximum(z - 1, 0), y, x, core)
-    greet([y_dev, up_dev, down_dev], [None, up, down])
-    own = [pltpu.make_async_copy(ins[a], outs[a].at[z * 2 + y], lsem.at[a]) for a in range(count)]
-    for copy in own:
-        copy.start()
-    pending = []
-
-    def go(kind, a, o, src, device, condition=None):
-        def make():
-            return remote(src, outs[a].at[o * 2 + y], ssem.at[kind, o, a], rsem.at[kind, o, a], device)
-        if condition is None:
-            make().start()
-        else:
-            pl.when(condition)(lambda: make().start())
-        pending.append((make, condition))
-
-    for i, o in enumerate(line_items(z)):
-        for a in range(count):
-            src = ins[a] if i == 0 else outs[a].at[o * 2 + y]
-            if i == 0:
-                go(0, a, o, src, up_dev, up)
-                go(1, a, o, src, down_dev, down)
-            else:
-                from_below = o < z
-                for kind, condition in ((0, from_below), (1, jnp.logical_not(from_below))):
-                    @pl.when(condition)
-                    def _(kind=kind, a=a, o=o, src=src):
-                        remote(src, src, ssem.at[kind, o, a], rsem.at[kind, o, a], y_dev).wait_recv()
-                go(0, a, o, src, up_dev, mid & from_below)
-                go(1, a, o, src, down_dev, mid & jnp.logical_not(from_below))
-            go(2, a, o, src, y_dev)
-    for i, o in enumerate(line_items(z)):
-        for a in range(count):
-            land = outs[a].at[o * 2 + 1 - y]
-            remote(land, land, ssem.at[2, o, a], rsem.at[2, o, a], y_dev).wait_recv()
-    for make, condition in pending:
-        if condition is None:
-            make().wait_send()
-        else:
-            pl.when(condition)(lambda make=make: make().wait_send())
-    for copy in own:
-        copy.wait()
-
-def plane_gather(arrays, cid):
-    count = len(arrays)
-    anys = pl.BlockSpec(memory_space=pl.ANY)
-    def body(*refs):
-        gather_plane(refs[:count], refs[count:2 * count], *refs[2 * count:])
-    return pl.pallas_call(
-        body, in_specs=[anys] * count, out_specs=[anys] * count,
-        out_shape=[jax.ShapeDtypeStruct((8,) + a.shape, a.dtype) for a in arrays],
-        scratch_shapes=[pltpu.SemaphoreType.DMA((3, 4, count)), pltpu.SemaphoreType.DMA((3, 4, count)),
-                        pltpu.SemaphoreType.DMA((count,))],
-        compiler_params=pltpu.CompilerParams(collective_id=cid, has_side_effects=True),
-        name="plane_gather")(*arrays)
-
-def gather_all(ins, outs, ssem, rsem, lsem):
+def gather_all(per_seq, ins, near_in, outs, near_out, ssem, rsem, lsem, nsend, nrecv):
     count = len(ins)
     z, y, x, core = place()
     mid = (z == 1) | (z == 2)
@@ -522,10 +459,27 @@
     c_dev = index_of(z, y, x, 1 - core)
     up_dev = index_of(jnp.minimum(z + 1, 3), y, x, core)
     down_dev = index_of(jnp.maximum(z - 1, 0), y, x, core)
-    greet([x_dev, y_dev, c_dev, up_dev, down_dev], [None, None, None, up, down])
+    previous, following, before, after = chain(z, y, x, core, per_seq)
+    greet([x_dev, y_dev, c_dev, up_dev, down_dev, previous, following], [None, None, None, up, down, before, after])
     own = [pltpu.make_async_copy(ins[a], outs[a].at[index_of(z, y, x, core)], lsem.at[a]) for a in range(count)]
+    own.append(pltpu.make_async_copy(near_in, near_out.at[2], lsem.at[count]))
     for copy in own:
         copy.start()
+    passes = jnp.where(core == 0, after, before)
+    pass_slot = 4 * (1 - core)
+
+    def near(kind):
+        src, slot, device = (
+            (near_in, 0, following),
+            (near_in, 4, previous),
+            (near_in, 1 + 2 * core, c_dev),
+            (near_out.at[pass_slot], 3 - 2 * core, c_dev),
+        )[kind]
+        return remote(src, near_out.at[slot], nsend.at[kind], nrecv.at[kind], device)
+
+    pl.when(after)(lambda: near(0).start())
+    pl.when(before)(lambda: near(1).start())
+    near(2).start()
     pending = []
 
     def go(kind, a, o, src, dst, device, condition=None):
@@ -584,6 +538,15 @@
             go(9, a, o, corner, corner, c_dev)
 
     first(0); first(1); second(0); first(2); second(1); third(0); first(3); second(2); third(1); second(3); third(2); third(3)
+    pl.when(before)(lambda: near(0).wait_recv())
+    pl.when(after)(lambda: near(1).wait_recv())
+    pl.when(passes)(lambda: near(3).start())
+    near(2).wait_recv()
+    pl.when(jnp.where(core == 0, before, after))(lambda: near(3).wait_recv())
+    pl.when(after)(lambda: near(0).wait_send())
+    pl.when(before)(lambda: near(1).wait_send())
+    near(2).wait_send()
+    pl.when(passes)(lambda: near(3).wait_send())
     for i in range(4):
         o = items[i]
         for a in range(count):
@@ -597,18 +560,21 @@
     for copy in own:
         copy.wait()
 
-def full_gather(arrays, cid):
+def full_gather(arrays, near_rows, per_seq, cid):
     count = len(arrays)
     anys = pl.BlockSpec(memory_space=pl.ANY)
     def body(*refs):
-        gather_all(refs[:count], refs[count:2 * count], *refs[2 * count:])
+        ins, near_in = refs[:count], refs[count]
+        outs, near_out = refs[count + 1:2 * count + 1], refs[2 * count + 1]
+        gather_all(per_seq, ins, near_in, outs, near_out, *refs[2 * count + 2:])
+    sem = pltpu.SemaphoreType.DMA
     return pl.pallas_call(
-        body, in_specs=[anys] * count, out_specs=[anys] * count,
-        out_shape=[jax.ShapeDtypeStruct((32,) + a.shape, a.dtype) for a in arrays],
-        scratch_shapes=[pltpu.SemaphoreType.DMA((10, 4, count)), pltpu.SemaphoreType.DMA((10, 4, count)),
-                        pltpu.SemaphoreType.DMA((count,))],
+        body, in_specs=[anys] * (count + 1), out_specs=[anys] * (count + 1),
+        out_shape=[jax.ShapeDtypeStruct((32,) + a.shape, a.dtype) for a in arrays]
+        + [jax.ShapeDtypeStruct((5,) + near_rows.shape, near_rows.dtype)],
+        scratch_shapes=[sem((10, 4, count)), sem((10, 4, count)), sem((count + 1,)), sem((4,)), sem((4,))],
         compiler_params=pltpu.CompilerParams(collective_id=cid, has_side_effects=True),
-        name="full_gather")(*arrays)
+        name="full_gather")(*arrays, near_rows)
 
 def add_into(target, *terms, rows=16):
     total = target.shape[0]
@@ -621,95 +587,6 @@
         target[part, :] = value.astype(target.dtype)
         return carry
     lax.fori_loop(0, total // step, one, 0)
-
-def reduce_plane(parts, outs, accs, yrecvs, zrecvs, ssem, rsem, lsem, osem, ahead=3):
-    count = len(parts)
-    z, y, x, core = place()
-    mid = (z == 1) | (z == 2)
-    up, down = z < 3, z > 0
-    y_dev = index_of(z, 1 - y, x, core)
-    up_dev = index_of(jnp.minimum(z + 1, 3), y, x, core)
-    down_dev = index_of(jnp.maximum(z - 1, 0), y, x, core)
-    greet([y_dev, up_dev, down_dev], [None, up, down])
-    items = line_items(z)[::-1]
-    order = [(a, i) for a in range(count) for i in range(4)]
-    loads = {}
-    for a, i in order:
-        o = items[i]
-        copy = pltpu.make_async_copy(parts[a].at[o * 2 + y], accs[a].at[o], lsem.at[o, a])
-        copy.start()
-        loads[a, i] = copy
-    pending = []
-
-    def y_copy(a, i):
-        o = items[i]
-        return remote(parts[a].at[o * 2 + 1 - y], yrecvs[a].at[o], ssem.at[0, o, a], rsem.at[0, o, a], y_dev)
-
-    for a, i in order[:ahead]:
-        y_copy(a, i).start()
-    for k, (a, i) in enumerate(order):
-        o = items[i]
-        y_copy(a, i).wait_recv()
-        if k + ahead < len(order):
-            y_copy(*order[k + ahead]).start()
-        loads[a, i].wait()
-        acc = accs[a].at[o]
-        if i < 3:
-            @pl.when(mid)
-            def _(a=a, o=o, acc=acc):
-                land = zrecvs[a].at[o]
-                remote(land, land, ssem.at[1, o, a], rsem.at[1, o, a], y_dev).wait_recv()
-                add_into(acc, yrecvs[a].at[o], land)
-            @pl.when(jnp.logical_not(mid))
-            def _(a=a, o=o, acc=acc):
-                add_into(acc, yrecvs[a].at[o])
-            rising = o > z
-            for sign, dev in ((1, up_dev), (-1, down_dev)):
-                condition = rising if sign > 0 else jnp.logical_not(rising)
-                def make(a=a, o=o, acc=acc, sign=sign, dev=dev):
-                    slot = o if sign > 0 else jnp.where(z - 1 == o, 4, o)
-                    return remote(acc, zrecvs[a].at[slot], ssem.at[1, o, a], rsem.at[1, slot, a], dev)
-                pl.when(condition)(lambda make=make: make().start())
-                pending.append((make, condition))
-        else:
-            for condition, slots in ((z == 0, (4,)), (z == 3, (3,)), (mid, (None, 4))):
-                @pl.when(condition)
-                def _(a=a, o=o, acc=acc, slots=slots):
-                    terms = [yrecvs[a].at[o]]
-                    for slot in slots:
-                        slot = o if slot is None else slot
-                        land = zrecvs[a].at[slot]
-                        remote(land, land, ssem.at[1, o, a], rsem.at[1, slot, a], y_dev).wait_recv()
-                        terms.append(land)
-                    add_into(acc, *terms)
-            out = pltpu.make_async_copy(acc, outs[a], osem.at[a])
-            out.start()
-            pending.append((lambda out=out: out, "local"))
-    for a, i in order:
-        y_copy(a, i).wait_send()
-    for make, condition in pending:
-        if condition == "local" if isinstance(condition, str) else False:
-            make().wait()
-        else:
-            pl.when(condition)(lambda make=make: make().wait_send())
-
-def plane_reduce(parts, cid):
-    count = len(parts)
-    anys = pl.BlockSpec(memory_space=pl.ANY)
-    def body(*refs):
-        it = iter(refs)
-        take = lambda n: [next(it) for _ in range(n)]
-        ins, outs, accs, yr, zr = take(count), take(count), take(count), take(count), take(count)
-        reduce_plane(ins, outs, accs, yr, zr, *it)
-    shape = [p.shape[1:] for p in parts]
-    sem = pltpu.SemaphoreType.DMA
-    return pl.pallas_call(
-        body, in_specs=[anys] * count, out_specs=[anys] * count,
-        out_shape=[jax.ShapeDtypeStruct(s, p.dtype) for s, p in zip(shape, parts)],
-        scratch_shapes=[pltpu.VMEM((n,) + s, p.dtype) for n in (4, 4, 5) for s, p in zip(shape, parts)]
-        + [sem((2, 5, count)), sem((2, 5, count)), sem((4, count)), sem((count,))],
-        compiler_params=pltpu.CompilerParams(collective_id=cid, has_side_effects=True, vmem_limit_bytes=56 * 2**20),
-        name="plane_reduce")(*parts)
 
 def reduce_all(parts, outs, accs, crecvs, dxs, dys, xrecvs, yrecvs, zrecvs, ssem, rsem, lsem, osem):
     count = len(parts)
@@ -842,176 +719,471 @@
     return lax.dot_general(left, right, (((1,), (0,)), ((), ())), preferred_element_type=f32)
 
 
-def expert_body(rows, width, half, tile, block, cut, *refs):
+def expert_body(shard, width, half, block, cut, *refs):
     it = iter(refs)
     take = lambda n: [next(it) for _ in range(n)]
-    x_hbm, c_hbm, s_hbm = take(3)
+    x_own, s_own, c_all = take(3)
     weights = [[take(2) for _ in range(3)] for _ in range(2)]
-    mix, gx, gs = take(3)
-    grads = [take(2) for _ in range(2)]
-    xv, cv, sv, wv, acc, hid_s, gate_s, up_s, gst, ostage, prev, stage = take(12)
-    wsem, insem, osem, psem, dsem, gsem = take(6)
+    x_all, s_all, mix, gx, gx_sum, gs_sum, y_land, z_land = take(8)
+    core_land = take(2)
+    grad_sum = take(2)
+    x_land = next(it)
+    xv, cv, sv, wv, acc, hid_s, gate_s, up_s, gst, gs_y, gs_z, ostage, prev = take(13)
+    gsend, grecv, lsem, rsend, rrecv, csend, crecv, xsend, xrecv = take(9)
+    wsem, insem, osem, psem, dsem, hsem, tsem = take(7)
     hidden = 2 * half
-    shard = s_hbm.shape[1] - 8
-    per_tile = tile // shard
-    tiles = rows // tile
+    tile = 2 * shard
     cuts = width // cut
-    steps = tiles * cuts
-    chip = lax.div(lax.axis_index("fsdp"), 2)
-    experts = (chip, chip + 1 - 2 * lax.rem(chip, 2))
+    tiles = 4
+    z, y, x, core = place()
+    mid = (z == 1) | (z == 2)
+    up, down = z < 3, z > 0
+    x_dev = index_of(z, y, 1 - x, core)
+    y_dev = index_of(z, 1 - y, x, core)
+    c_dev = index_of(z, y, x, 1 - core)
+    up_dev = index_of(jnp.minimum(z + 1, 3), y, x, core)
+    down_dev = index_of(jnp.maximum(z - 1, 0), y, x, core)
+    chip = (z * 2 + y) * 2 + x
+    experts = ((z * 2 + y) * 2 + 1 - x, chip)
     lane = lax.broadcasted_iota(jnp.int32, (1, 128), 1)
-
-    def incoming(t, slot):
+    items = line_items(z)
+
+    def nearest(k):
+        return jnp.where(k == 0, items[0], jnp.where(k == 1, items[1], jnp.where(k == 2, items[2], items[3])))
+
+    def farthest(k):
+        return nearest(3 - k)
+
+    sources, landings = (x_own, s_own), (x_all, s_all)
+    own_rows = xv.at[0, pl.ds(pl.multiple_of(y * shard, shard), shard)]
+    own_in = [
+        pltpu.make_async_copy(x_own, own_rows, lsem.at[0]),
+        pltpu.make_async_copy(s_own, s_all.at[z * 2 + y], lsem.at[1]),
+    ]
+    own_out = pltpu.make_async_copy(own_rows, x_all.at[z * 2 + y], lsem.at[0])
+
+    def hop(kind, a, o, src, device):
+        return remote(src, landings[a].at[o * 2 + y], gsend.at[kind, o, a], grecv.at[kind, o, a], device)
+
+    def gather_first():
+        for copy in own_in:
+            copy.start()
+        for a in range(2):
+            hop(2, a, z, sources[a], y_dev).start()
+            pl.when(up)(lambda a=a: hop(0, a, z, sources[a], up_dev).start())
+            pl.when(down)(lambda a=a: hop(1, a, z, sources[a], down_dev).start())
+
+    def gather_next(k):
+        o = nearest(k)
+        from_below = o < z
+        for a in range(2):
+            land = landings[a].at[o * 2 + y]
+
+            @pl.when(from_below)
+            def _():
+                hop(0, a, o, land, up_dev).wait_recv()
+                pl.when(mid)(lambda: hop(0, a, o, land, up_dev).start())
+
+            @pl.when(jnp.logical_not(from_below))
+            def _():
+                hop(1, a, o, land, down_dev).wait_recv()
+                pl.when(mid)(lambda: hop(1, a, o, land, down_dev).start())
+
+            hop(2, a, o, land, y_dev).start()
+
+    def gather_landed(o):
+        for a in range(2):
+            land = landings[a].at[o * 2 + 1 - y]
+            remote(land, land, gsend.at[2, o, a], grecv.at[2, o, a], y_dev).wait_recv()
+
+    def gather_sent():
+        for a in range(2):
+            pl.when(up)(lambda a=a: hop(0, a, z, sources[a], up_dev).wait_send())
+            pl.when(down)(lambda a=a: hop(1, a, z, sources[a], down_dev).wait_send())
+            for k in range(4):
+                hop(2, a, items[k], sources[a], y_dev).wait_send()
+            for k in range(1, 4):
+                o = items[k]
+                pl.when(mid & (o < z))(lambda a=a, o=o: hop(0, a, o, sources[a], up_dev).wait_send())
+                pl.when(mid & (o > z))(lambda a=a, o=o: hop(1, a, o, sources[a], down_dev).wait_send())
+
+    def lines(block_index):
+        return pl.ds(pl.multiple_of(block_index * shard, shard), shard)
+
+    def y_copies(o):
+        other = o * 2 + 1 - y
+        return [
+            remote(gx.at[lines(other)], y_land.at[o], rsend.at[0, o, 0], rrecv.at[0, o, 0], y_dev),
+            remote(gst.at[other], gs_y.at[o], rsend.at[0, o, 1], rrecv.at[0, o, 1], y_dev),
+        ]
+
+    def z_copies(o, slot, device):
+        own = o * 2 + y
+        return [
+            remote(gx.at[lines(own)], z_land.at[slot], rsend.at[1, o, 0], rrecv.at[1, slot, 0], device),
+            remote(gst.at[own], gs_z.at[slot], rsend.at[1, o, 1], rrecv.at[1, slot, 1], device),
+        ]
+
+    def z_go(o, act):
+        rising = o > z
+        slot = jnp.where(z - 1 == o, 4, o)
+
+        @pl.when(rising)
+        def _():
+            for copy in z_copies(o, o, up_dev):
+                act(copy)
+
+        @pl.when(jnp.logical_not(rising))
+        def _():
+            for copy in z_copies(o, slot, down_dev):
+                act(copy)
+
+    wide = width // 2
+
+    def halves(hbm, vmem, slot, out=False):
         copies = []
-        for r in range(per_tile):
+        for h in range(2):
+            far, near = hbm.at[:, pl.ds(h * wide, wide)], vmem.at[pl.ds(h * shard, shard)]
+            if out:
+                copies.append(pltpu.make_async_copy(near, far, tsem.at[slot, h]))
+            else:
+                copies.append(pltpu.make_async_copy(far, near, tsem.at[slot, h]))
+        return copies
+
+    def z_wait(slot):
+        for copy in z_copies(z, slot, y_dev):
+            copy.wait_recv()
+
+    def add_up(terms):
+        def some(r, carry):
+            part = pl.ds(pl.multiple_of(r * 32, 32), 32)
+            value = hid_s[part, :].astype(f32)
+            for term in terms:
+                value = value + term[part, :].astype(f32)
+            hid_s[part, :] = value.astype(bf)
+            return carry
+
+        lax.fori_loop(0, tile // 32, some, 0)
+
+    def pump(o, final):
+        own = o * 2 + y
+        load = halves(gx.at[lines(own)], hid_s, 0)
+        for copy in load:
+            copy.start()
+        for copy in y_copies(o):
+            copy.wait_recv()
+        load_y = halves(y_land.at[o], gate_s, 1)
+        for copy in load_y:
+            copy.start()
+        slot = jnp.where(z == 0, 4, o) if final else o
+
+        def with_z():
+            z_wait(slot)
+            load_z = halves(z_land.at[slot], up_s, 2)
+            for copy in load_z:
+                copy.start()
+            for copy in load + load_y + load_z:
+                copy.wait()
+            add_up([gate_s, up_s])
+            gst[own] = gst[own] + gs_y[o] + gs_z[slot]
+
+        if final:
+            with_z()
+
+            @pl.when(mid)
+            def _():
+                z_wait(4)
+                load_z = halves(z_land.at[4], up_s, 2)
+                for copy in load_z:
+                    copy.start()
+                for copy in load_z:
+                    copy.wait()
+                add_up([up_s])
+                gst[own] = gst[own] + gs_z[4]
+
+            store = halves(gx_sum, hid_s, 0, True)
+            store.append(pltpu.make_async_copy(gst.at[own], gs_sum, tsem.at[1, 0]))
+            for copy in store:
+                copy.start()
+            for copy in store:
+                copy.wait()
+        else:
+            pl.when(mid)(with_z)
+
+            @pl.when(jnp.logical_not(mid))
+            def _():
+                for copy in load + load_y:
+                    copy.wait()
+                add_up([gate_s])
+                gst[own] = gst[own] + gs_y[o]
+
+            store = halves(gx.at[lines(own)], hid_s, 0, True)
+            for copy in store:
+                copy.start()
+            for copy in store:
+                copy.wait()
+            z_go(o, lambda copy: copy.start())
+
+    tall = shard
+    per_half = (half // tall) * (width // cut)
+    pieces = 3 * per_half
+
+    def piece(q):
+        i, rest = lax.div(q, per_half), lax.rem(q, per_half)
+        r, c = lax.div(rest, width // cut), lax.rem(rest, width // cut)
+        return i, pl.multiple_of(r * tall, tall), pl.ds(pl.multiple_of(c * cut, cut), cut)
+
+    slots = 8
+
+    def eighth(ref, slot):
+        low = pl.multiple_of(lax.rem(slot, 2) * tall, tall)
+        return ref.at[lax.div(slot, 4), lax.rem(lax.div(slot, 2), 2), pl.ds(low, tall)]
+
+    def stage(slot):
+        return eighth(ostage, slot)
+
+    def held(slot):
+        return eighth(prev, slot)
+
+    def flush(number):
+        def across(q, slot):
+            i, r, c = piece(q)
+            land = core_land[number].at[i, pl.ds(r, tall), c]
+            return remote(stage(slot), land, csend.at[number, slot], crecv.at[number], c_dev)
+
+        def give(q, carry):
+            slot = lax.rem(q, slots)
+            pl.when(q >= slots)(lambda: across(q - slots, slot).wait_send())
+            i, r, c = piece(q)
+            stage(slot)[...] = acc[i, pl.ds(pl.multiple_of(half + r, tall), tall), c].astype(bf)
+            across(q, slot).start()
+            return carry
+
+        lax.fori_loop(0, pieces, give, 0)
+
+        def given(q, carry):
+            across(q, lax.rem(q, slots)).wait_send()
+            return carry
+
+        lax.fori_loop(pieces - slots, pieces, given, 0)
+        remote(core_land[number], core_land[number], csend.at[number, 0], crecv.at[number], c_dev).wait_recv()
+
+        def bring(q, slot):
+            i, r, c = piece(q)
+            return pltpu.make_async_copy(core_land[number].at[i, pl.ds(r, tall), c], held(slot), hsem.at[slot])
+
+        def store(q, slot):
+            i, r, c = piece(q)
+            return pltpu.make_async_copy(stage(slot), grad_sum[number].at[i, pl.ds(r, tall), c], dsem.at[slot])
+
+        for q in range(slots - 1):
+            bring(q, q).start()
+
+        def keep(q, carry):
+            slot = lax.rem(q, slots)
+            coming = q + slots - 1
+            pl.when(coming < pieces)(lambda: bring(coming, lax.rem(coming, slots)).start())
+            pl.when(q >= slots)(lambda: store(q - slots, slot).wait())
+            bring(q, slot).wait()
+            i, r, c = piece(q)
+            stage(slot)[...] = (acc[i, pl.ds(r, tall), c] + held(slot)[...].astype(f32)).astype(bf)
+            store(q, slot).start()
+            return carry
+
+        lax.fori_loop(0, pieces, keep, 0)
+
+        def kept(q, carry):
+            store(q, lax.rem(q, slots)).wait()
+            return carry
+
+        lax.fori_loop(pieces - slots, pieces, kept, 0)
+
+    def x_copy():
+        return remote(grad_sum[0], x_land, xsend, xrecv, x_dev)
+
+    def c_loads(o, slot):
+        return [
+            pltpu.make_async_copy(c_all.at[o * 2 + r], cv.at[slot, pl.ds(r * shard, shard)], insem.at[1, r, slot])
+            for r in range(2)
+        ]
+
+    def x_loads(o, slot):
+        copies = []
+        for r in range(2):
             part = pl.ds(r * shard, shard)
             copies += [
-                pltpu.make_async_copy(x_hbm.at[t * per_tile + r], xv.at[slot, part], insem.at[0, r, slot]),
-                pltpu.make_async_copy(c_hbm.at[t * per_tile + r], cv.at[slot, part], insem.at[1, r, slot]),
-                pltpu.make_async_copy(
-                    s_hbm.at[t * per_tile + r, pl.ds(0, shard)], sv.at[slot, part], insem.at[2, r, slot]
-                ),
+                pltpu.make_async_copy(x_all.at[o * 2 + r], xv.at[slot, part], insem.at[0, r, slot]),
+                pltpu.make_async_copy(s_all.at[o * 2 + r, pl.ds(0, shard)], sv.at[slot, part], insem.at[2, r, slot]),
             ]
         return copies
 
-    def spot(k):
-        t, n = lax.div(k, cuts), lax.rem(k, cuts)
-        return pl.ds(pl.multiple_of(t * tile, tile), tile), pl.ds(pl.multiple_of(n * cut, cut), cut)
-
-    def outgoing(k, slot):
-        r, c = spot(k)
+    def spot(o, n):
+        return pl.ds(pl.multiple_of(o * tile, tile), tile), pl.ds(pl.multiple_of(n * cut, cut), cut)
+
+    def outgoing(o, n, slot):
+        r, c = spot(o, n)
         return [
             pltpu.make_async_copy(ostage.at[slot, i], ref.at[r, c], osem.at[i, slot])
             for i, ref in enumerate((mix, gx))
         ]
 
-    def earlier(k, slot):
-        r, c = spot(k)
+    def earlier(o, n, slot):
+        r, c = spot(o, n)
         return [
             pltpu.make_async_copy(ref.at[r, c], prev.at[slot, i], psem.at[i, slot])
             for i, ref in enumerate((mix, gx))
         ]
 
-    for number in range(2):
-        loads = [
+    def weight_loads(number):
+        return [
             pltpu.make_async_copy(weights[number][i][h], wv.at[i, pl.ds(h * half, half)], wsem.at[i, h])
             for i in range(3)
             for h in range(2)
         ]
-        for copy in loads:
+
+    def run_tile(number, o, slot):
+        if number:
+            for copy in earlier(o, 0, 0):
+                copy.start()
+        pick = (lane == experts[number]).astype(f32)
+        share = jnp.sum(sv[slot] * pick, axis=1, keepdims=True)
+
+        def hidden_block(j, dots):
+            part = pl.ds(pl.multiple_of(j * block, block), block)
+            rows_in, cots = xv[slot], cv[slot]
+            gate_pre = nt(rows_in, wv[0, part, :])
+            up_pre = nt(rows_in, wv[1, part, :])
+            grad_raw = nt(cots, wv[2, part, :])
+            sig = jax.nn.sigmoid(gate_pre)
+            silu = gate_pre * sig
+            low = (silu * up_pre).astype(bf).astype(f32)
+            dots = dots + jnp.sum(low * grad_raw, axis=1, keepdims=True)
+            grad_hid = grad_raw * share
+            grad_gate = (grad_hid * up_pre * sig * (1.0 + gate_pre * (1.0 - sig))).astype(bf)
+            grad_up = (grad_hid * silu).astype(bf)
+            shared = (low * share).astype(bf)
+            hid_s[:, part] = shared
+            gate_s[:, part] = grad_gate
+            up_s[:, part] = grad_up
+            acc[0, part, :] += tn(grad_gate, rows_in)
+            acc[1, part, :] += tn(grad_up, rows_in)
+            acc[2, part, :] += tn(shared, cots)
+            return dots
+
+        dots = lax.fori_loop(0, hidden // block, hidden_block, jnp.zeros((tile, 1), f32))
+        both = dots * pick
+        for r in range(2):
+            turned = jnp.transpose(both[r * shard : (r + 1) * shard, :])[: gst.shape[1], :]
+            gst[o * 2 + r] = gst[o * 2 + r] + turned if number else turned
+
+        def column_block(n, inner):
+            now = lax.rem(n, 2)
+            columns = pl.ds(pl.multiple_of(n * cut, cut), cut)
+
+            @pl.when(n >= 2)
+            def _():
+                for copy in outgoing(o, n - 2, now):
+                    copy.wait()
+
+            out = nn(hid_s[...], wv[2, :, columns])
+            back = nn(gate_s[...], wv[0, :, columns]) + nn(up_s[...], wv[1, :, columns])
+            if number:
+                @pl.when(n + 1 < cuts)
+                def _():
+                    for copy in earlier(o, n + 1, 1 - now):
+                        copy.start()
+
+                for copy in earlier(o, n, now):
+                    copy.wait()
+                out = out + prev[now, 0].astype(f32)
+                back = back + prev[now, 1].astype(f32)
+            ostage[now, 0] = out.astype(bf)
+            ostage[now, 1] = back.astype(bf)
+            for copy in outgoing(o, n, now):
+                copy.start()
+            return inner
+
+        lax.fori_loop(0, cuts, column_block, 0)
+        for n in (cuts - 2, cuts - 1):
+            for copy in outgoing(o, n, n % 2):
+                copy.wait()
+
+    greet([x_dev, y_dev, c_dev, up_dev, down_dev], [None, None, None, up, down])
+    gather_first()
+    loads = weight_loads(0) + c_loads(items[0], 0)
+    for copy in loads:
+        copy.start()
+    acc[...] = jnp.zeros_like(acc)
+    own_in[0].wait()
+    own_out.start()
+    for copy in loads[:-2]:
+        copy.wait()
+    own_out.wait()
+    own_in[1].wait()
+
+    def first_pass(t, carry):
+        slot = lax.rem(t, 2)
+        o = nearest(t)
+
+        @pl.when(t + 1 < tiles)
+        def _():
+            gather_next(t + 1)
+            for copy in c_loads(nearest(t + 1), 1 - slot):
+                copy.start()
+
+        gather_landed(o)
+        now = x_loads(o, slot)
+        for copy in now:
             copy.start()
-        for copy in incoming(0, 0):
+        for copy in now + c_loads(o, slot):
+            copy.wait()
+        run_tile(0, o, slot)
+        return carry
+
+    lax.fori_loop(0, tiles, first_pass, 0)
+    loads = weight_loads(1)
+    begin = c_loads(items[3], 0) + x_loads(items[3], 0)
+    for copy in loads + begin:
+        copy.start()
+    flush(0)
+    x_copy().start()
+    acc[...] = jnp.zeros_like(acc)
+    for copy in loads:
+        copy.wait()
+
+    def second_pass(t, carry):
+        slot = lax.rem(t, 2)
+        o = farthest(t)
+
+        @pl.when(t + 1 < tiles)
+        def _():
+            for copy in c_loads(farthest(t + 1), 1 - slot) + x_loads(farthest(t + 1), 1 - slot):
+                copy.start()
+
+        for copy in c_loads(o, slot) + x_loads(o, slot):
+            copy.wait()
+        run_tile(1, o, slot)
+        for copy in y_copies(o):
             copy.start()
-        if number:
-            for copy in earlier(0, 0):
-                copy.start()
-        acc[...] = jnp.zeros_like(acc)
-        for copy in loads:
-            copy.wait()
-        pick = (lane == experts[number]).astype(f32)
-
-        def one_tile(t, carry, number=number, pick=pick):
-            slot = lax.rem(t, 2)
-
-            @pl.when(t + 1 < tiles)
-            def _():
-                for copy in incoming(t + 1, 1 - slot):
-                    copy.start()
-
-            for copy in incoming(t, slot):
-                copy.wait()
-            share = jnp.sum(sv[slot] * pick, axis=1, keepdims=True)
-
-            def hidden_block(j, dots):
-                part = pl.ds(pl.multiple_of(j * block, block), block)
-                x, c = xv[slot], cv[slot]
-                gate_pre = nt(x, wv[0, part, :])
-                up_pre = nt(x, wv[1, part, :])
-                grad_raw = nt(c, wv[2, part, :])
-                sig = jax.nn.sigmoid(gate_pre)
-                silu = gate_pre * sig
-                hid = silu * up_pre
-                low = hid.astype(bf).astype(f32)
-                dots = dots + jnp.sum(low * grad_raw, axis=1, keepdims=True)
-                grad_hid = grad_raw * share
-                grad_gate = (grad_hid * up_pre * sig * (1.0 + gate_pre * (1.0 - sig))).astype(bf)
-                grad_up = (grad_hid * silu).astype(bf)
-                shared = (low * share).astype(bf)
-                hid_s[:, part] = shared
-                gate_s[:, part] = grad_gate
-                up_s[:, part] = grad_up
-                acc[0, part, :] += tn(grad_gate, x)
-                acc[1, part, :] += tn(grad_up, x)
-                acc[2, part, :] += tn(shared, c)
-                return dots
-
-            dots = lax.fori_loop(0, hidden // block, hidden_block, jnp.zeros((tile, 1), f32))
-            both = dots * pick
-            for r in range(per_tile):
-                turned = jnp.transpose(both[r * shard : (r + 1) * shard, :])[: gst.shape[1], :]
-                spot_now = t * per_tile + r
-                gst[spot_now] = gst[spot_now] + turned if number else turned
-
-            def column_block(n, inner):
-                k = t * cuts + n
-                place_now = lax.rem(k, 2)
-                columns = pl.ds(pl.multiple_of(n * cut, cut), cut)
-
-                @pl.when(k >= 2)
-                def _():
-                    for copy in outgoing(k - 2, place_now):
-                        copy.wait()
-
-                out = nn(hid_s[...], wv[2, :, columns])
-                back = nn(gate_s[...], wv[0, :, columns]) + nn(up_s[...], wv[1, :, columns])
-                if number:
-                    @pl.when(k + 1 < steps)
-                    def _():
-                        for copy in earlier(k + 1, 1 - place_now):
-                            copy.start()
-
-                    for copy in earlier(k, place_now):
-                        copy.wait()
-                    out = out + prev[place_now, 0].astype(f32)
-                    back = back + prev[place_now, 1].astype(f32)
-                ostage[place_now, 0] = out.astype(bf)
-                ostage[place_now, 1] = back.astype(bf)
-                for copy in outgoing(k, place_now):
-                    copy.start()
-                return inner
-
-            lax.fori_loop(0, cuts, column_block, 0)
-            return carry
-
-        lax.fori_loop(0, tiles, one_tile, 0)
-        for k in (steps - 2, steps - 1):
-            for copy in outgoing(k, k % 2):
-                copy.wait()
-        chunk = stage.shape[1]
-        per_half = half // chunk
-        spots = [(i, h, r) for i in range(3) for h in range(2) for r in range(per_half)]
-
-        def flush(k, number=number):
-            i, h, r = spots[k]
-            return pltpu.make_async_copy(
-                stage.at[k % 2], grads[number][h].at[i, pl.ds(r * chunk, chunk)], dsem.at[k % 2]
-            )
-
-        for k, (i, h, r) in enumerate(spots):
-            if k >= 2:
-                flush(k - 2).wait()
-            first = h * half + r * chunk
-            stage[k % 2] = acc[i, first : first + chunk, :].astype(bf)
-            flush(k).start()
-        for k in (len(spots) - 2, len(spots) - 1):
-            flush(k).wait()
-    last = pltpu.make_async_copy(gst, gs, gsem)
-    last.start()
-    last.wait()
-
-
-def expert_pass(x_all, c_all, s_all, weights, gs_rows):
-    blocks, shard, width = x_all.shape
+        k = jnp.where(mid, t - 2, t - 1)
+        pl.when(k >= 0)(lambda: pump(farthest(k), False))
+        return carry
+
+    lax.fori_loop(0, tiles, second_pass, 0)
+    pl.when(mid)(lambda: pump(items[1], False))
+    flush(1)
+    pump(z, True)
+    for k in range(4):
+        for copy in y_copies(items[k]):
+            copy.wait_send()
+        if k:
+            z_go(items[k], lambda copy: copy.wait_send())
+    gather_sent()
+    x_copy().wait()
+
+
+def expert_pass(x_own, s_own, c_all, weights, gs_rows, cid):
+    blocks, shard, width = c_all.shape
     rows = blocks * shard
     half = weights[0][0][0].shape[0]
     hidden = 2 * half
@@ -1019,15 +1191,22 @@
     anys = pl.BlockSpec(memory_space=pl.ANY)
     sem = pltpu.SemaphoreType.DMA
     flat = [w for one in weights for pair in one for w in pair]
+    shaped = jax.ShapeDtypeStruct
+    half_grads = shaped((3, half, width), bf)
     shapes = [
-        jax.ShapeDtypeStruct((rows, width), bf),
-        jax.ShapeDtypeStruct((rows, width), bf),
-        jax.ShapeDtypeStruct((blocks, gs_rows, shard), f32),
-    ] + [jax.ShapeDtypeStruct((3, half, width), bf)] * 4
+        shaped((blocks, shard, width), bf),
+        shaped((blocks,) + s_own.shape, f32),
+        shaped((rows, width), bf),
+        shaped((rows, width), bf),
+        shaped((shard, width), bf),
+        shaped((gs_rows, shard), f32),
+        shaped((4, shard, width), bf),
+        shaped((5, shard, width), bf),
+    ] + [half_grads] * 5
     return pl.pallas_call(
-        functools.partial(expert_body, rows, width, half, tile, block, cut),
+        functools.partial(expert_body, shard, width, half, block, cut),
         in_specs=[anys] * (3 + len(flat)),
-        out_specs=[anys] * 7,
+        out_specs=[anys] * len(shapes),
         out_shape=shapes,
         scratch_shapes=[
             pltpu.VMEM((2, tile, width), bf),
@@ -1039,19 +1218,231 @@
             pltpu.VMEM((tile, hidden), bf),
             pltpu.VMEM((tile, hidden), bf),
             pltpu.VMEM((blocks, gs_rows, shard), f32),
+            pltpu.VMEM((4, gs_rows, shard), f32),
+            pltpu.VMEM((5, gs_rows, shard), f32),
             pltpu.VMEM((2, 2, tile, cut), bf),
             pltpu.VMEM((2, 2, tile, cut), bf),
-            pltpu.VMEM((2, 64, width), bf),
+            sem((3, 4, 2)),
+            sem((3, 4, 2)),
+            sem((2,)),
+            sem((2, 5, 2)),
+            sem((2, 5, 2)),
+            sem((2, 8)),
+            sem((2,)),
+            sem,
+            sem,
             sem((3, 2)),
             sem((3, 2, 2)),
             sem((2, 2)),
             sem((2, 2)),
-            sem((2,)),
-            sem,
+            sem((8,)),
+            sem((8,)),
+            sem((3, 2)),
         ],
-        compiler_params=pltpu.CompilerParams(vmem_limit_bytes=63 * 2**20),
+        compiler_params=pltpu.CompilerParams(
+            vmem_limit_bytes=63 * 2**20, collective_id=cid, has_side_effects=True
+        ),
         name="expert_pass",
-    )(x_all, c_all, s_all, *flat)
+    )(x_own, s_own, c_all, *flat)
+def attend_body(scale, q_ref, k_ref, v_ref, bias_ref, out_ref, lse_ref, top_ref):
+    head = pl.program_id(0)
+    scores = nt(q_ref[...], k_ref[...]) * scale + bias_ref[...]
+    top = jnp.max(scores, axis=1, keepdims=True)
+    parts = jnp.exp(scores - top)
+    total = jnp.sum(parts, axis=1, keepdims=True)
+    probs = (parts * (1.0 / total)).astype(bf)
+    out_ref[...] = nn(probs, v_ref[...]).astype(bf)
+    lane = lax.broadcasted_iota(jnp.int32, lse_ref.shape, 1)
+
+    @pl.when(head == 0)
+    def _():
+        lse_ref[...] = jnp.zeros_like(lse_ref)
+        top_ref[...] = jnp.zeros_like(top_ref)
+
+    lse_ref[...] = jnp.where(lane == head, top + jnp.log(total), lse_ref[...])
+    row = lax.broadcasted_iota(jnp.int32, top_ref.shape, 1)
+    top_ref[...] = jnp.where(row == head, jnp.max(top), top_ref[...])
+
+
+def attend(queries, keys_values, bias, heads, scale):
+    rows, width = queries.shape
+    keys = keys_values.shape[0]
+    size = width // heads
+    return pl.pallas_call(
+        functools.partial(attend_body, scale),
+        grid=(heads,),
+        in_specs=[
+            pl.BlockSpec((rows, size), lambda h: (0, h)),
+            pl.BlockSpec((keys, size), lambda h: (0, h)),
+            pl.BlockSpec((keys, size), lambda h: (0, heads + h)),
+            pl.BlockSpec((rows, keys), lambda h: (0, 0)),
+        ],
+        out_specs=[
+            pl.BlockSpec((rows, size), lambda h: (0, h)),
+            pl.BlockSpec((rows, 128), lambda h: (0, 0)),
+            pl.BlockSpec((8, 128), lambda h: (0, 0)),
+        ],
+        out_shape=[
+            jax.ShapeDtypeStruct((rows, width), bf),
+            jax.ShapeDtypeStruct((rows, 128), f32),
+            jax.ShapeDtypeStruct((8, 128), f32),
+        ],
+        compiler_params=pltpu.CompilerParams(vmem_limit_bytes=48 * 2**20),
+        name="attend",
+    )(queries, keys_values, keys_values, bias)
+
+
+def attend_back_body(scale, q_ref, k_ref, v_ref, g_ref, bias_ref, lse_ref, dq_ref, dk_ref, dv_ref):
+    head = pl.program_id(0)
+    lane = lax.broadcasted_iota(jnp.int32, lse_ref.shape, 1)
+    lse = jnp.sum(jnp.where(lane == head, lse_ref[...], 0.0), axis=1, keepdims=True)
+    queries, keys, grads = q_ref[...], k_ref[...], g_ref[...]
+    probs = jnp.exp(nt(queries, keys) * scale + bias_ref[...] - lse)
+    low = probs.astype(bf)
+    dv_ref[...] = tn(low, grads).astype(bf)
+    grad_probs = nt(grads, v_ref[...])
+    shift = jnp.sum(probs * grad_probs, axis=1, keepdims=True)
+    grad_scores = (probs * (grad_probs - shift)).astype(bf)
+    dq_ref[...] = (nn(grad_scores, keys) * scale).astype(bf)
+    dk_ref[...] = (tn(grad_scores, queries) * scale).astype(bf)
+
+
+def attend_back(queries, keys_values, grads, bias, lse, heads, scale):
+    rows, width = queries.shape
+    keys = keys_values.shape[0]
+    size = width // heads
+    own = pl.BlockSpec((rows, size), lambda h: (0, h))
+    seen = pl.BlockSpec((keys, size), lambda h: (0, h))
+    return pl.pallas_call(
+        functools.partial(attend_back_body, scale),
+        grid=(heads,),
+        in_specs=[
+            own,
+            seen,
+            pl.BlockSpec((keys, size), lambda h: (0, heads + h)),
+            own,
+            pl.BlockSpec((rows, keys), lambda h: (0, 0)),
+            pl.BlockSpec((rows, 128), lambda h: (0, 0)),
+        ],
+        out_specs=[own, seen, seen],
+        out_shape=[
+            jax.ShapeDtypeStruct((rows, width), bf),
+            jax.ShapeDtypeStruct((keys, width), bf),
+            jax.ShapeDtypeStruct((keys, width), bf),
+        ],
+        compiler_params=pltpu.CompilerParams(vmem_limit_bytes=48 * 2**20),
+        name="attend_back",
+    )(queries, keys_values, keys_values, grads, bias, lse)
+
+
+def chain(z, y, x, core, per_seq):
+    chip = (z * 2 + y) * 2 + x
+    at = lax.rem(chip, per_seq)
+    before, after = at > 0, at < per_seq - 1
+    previous = (chip - jnp.where(before, 1, 0)) * 2 + core
+    following = (chip + jnp.where(after, 1, 0)) * 2 + core
+    return previous, following, before, after
+
+
+def return_body(per_seq, *refs):
+    parts, out = refs[:2], refs[2]
+    far, own, adj, mine, lands, ssem, rsem, lsem = refs[3:]
+    z, y, x, core = place()
+    c_dev = index_of(z, y, x, 1 - core)
+    previous, following, before, after = chain(z, y, x, core, per_seq)
+    greet([c_dev, previous, following], [None, before, after])
+    rows = own.shape[1]
+    far_slot, plain_slot = 4 * (1 - core), 4 * core
+    adds = jnp.where(core == 0, after, before)
+    gives = jnp.where(core == 0, before, after)
+
+    def to_core(kind, a):
+        slot = jnp.where(kind == 0, 1 + 2 * core, 3 - 2 * core)
+        land = adj.at[a] if kind == 0 else mine.at[a]
+        return remote(parts[a].at[slot], land, ssem.at[kind, a], rsem.at[kind, a], c_dev)
+
+    def plain(kind, a, device, sem):
+        return remote(parts[a].at[plain_slot], lands.at[1 if kind == 2 else 0, a], ssem.at[sem, a], rsem.at[kind, a], device)
+
+    def summed(kind, a, device, sem):
+        return remote(far.at[a], lands.at[1 if kind == 2 else 0, a], ssem.at[sem, a], rsem.at[kind, a], device)
+
+    loads = []
+    for a in range(2):
+        pl.when(gives)(lambda a=a: to_core(0, a).start())
+        to_core(1, a).start()
+        loads.append(pltpu.make_async_copy(parts[a].at[far_slot], far.at[a], lsem.at[0, a]))
+        loads.append(pltpu.make_async_copy(parts[a].at[2], own.at[a], lsem.at[1, a]))
+    for copy in loads:
+        copy.start()
+    for a in range(2):
+        pl.when((core == 0) & before)(lambda a=a: plain(2, a, previous, 2).start())
+        pl.when((core == 1) & after)(lambda a=a: plain(3, a, following, 2).start())
+    for a in range(2):
+        @pl.when(adds)
+        def _(a=a):
+            to_core(0, a).wait_recv()
+        loads[2 * a].wait()
+
+        @pl.when(adds)
+        def _(a=a):
+            add_into(far.at[a], adj.at[a])
+            pl.when(core == 0)(lambda: summed(3, a, following, 3).start())
+            pl.when(core == 1)(lambda: summed(2, a, previous, 3).start())
+
+    width = own.shape[2]
+    for a in range(2):
+        loads[2 * a + 1].wait()
+        to_core(1, a).wait_recv()
+        add_into(own.at[a], mine.at[a])
+    for a in range(2):
+        @pl.when(before)
+        def _(a=a):
+            plain(3, a, previous, 2).wait_recv()
+            add_into(own.at[a], lands.at[0, a])
+
+        @pl.when(after)
+        def _(a=a):
+            plain(2, a, previous, 2).wait_recv()
+            add_into(own.at[a], lands.at[1, a])
+
+        out[:, a * width : (a + 1) * width] = own[a]
+    for a in range(2):
+        pl.when(gives)(lambda a=a: to_core(0, a).wait_send())
+        to_core(1, a).wait_send()
+        pl.when((core == 0) & before)(lambda a=a: plain(2, a, previous, 2).wait_send())
+        pl.when((core == 1) & after)(lambda a=a: plain(3, a, following, 2).wait_send())
+        pl.when((core == 0) & after)(lambda a=a: summed(3, a, following, 3).wait_send())
+        pl.when((core == 1) & before)(lambda a=a: summed(2, a, previous, 3).wait_send())
+
+
+def return_near(parts, per_seq, cid):
+    slots, rows, width = parts[0].shape
+    anys = pl.BlockSpec(memory_space=pl.ANY)
+    sem = pltpu.SemaphoreType.DMA
+    block = pltpu.VMEM((2, rows, width), bf)
+    return pl.pallas_call(
+        functools.partial(return_body, per_seq),
+        in_specs=[anys, anys],
+        out_specs=pl.BlockSpec(memory_space=pltpu.VMEM),
+        out_shape=jax.ShapeDtypeStruct((rows, 2 * width), bf),
+        scratch_shapes=[
+            block,
+            block,
+            block,
+            block,
+            pltpu.VMEM((2, 2, rows, width), bf),
+            sem((4, 2)),
+            sem((4, 2)),
+            sem((2, 2)),
+        ],
+        compiler_params=pltpu.CompilerParams(
+            collective_id=cid, has_side_effects=True, vmem_limit_bytes=40 * 2**20
+        ),
+        name="return_near",
+    )(*parts)
+
+
 def dense_layer(
     tokens,
     w_query,
@@ -1085,7 +1476,8 @@
         ((0, 0), (0, 128 - experts - 2)),
     )
     wide_own = jnp.concatenate((w_query, w_key, w_value, extra), axis=1)
-    wide_full, out_full = full_gather([wide_own, w_out], 2)
+    per_seq = devices // (2 * doc_lengths.shape[0])
+    wide_full, out_full, near_tokens = full_gather([wide_own, w_out], tokens, per_seq, 2)
     wide_full = wide_full.reshape(model_width, wide_width + 128)
     out_full = out_full.reshape(model_width, model_width)
     later = lax.optimization_barrier((out_full, cotangent, w_gate, w_up, w_down))
@@ -1098,8 +1490,8 @@
     core_weights = [swapped(w, "fsdp", 0) for w in (gate_own, up_own, down_own)]
     corner_weights = [swapped(w, "fsdp", 0) for w in x_weights]
     expert_weights = [
+        list(zip(x_weights, corner_weights)),
         list(zip((gate_own, up_own, down_own), core_weights)),
-        list(zip(x_weights, corner_weights)),
     ]
     router_full = wide_full[:, wide_width : wide_width + experts]
     gain_one = wide_full[:, wide_width + experts]
@@ -1107,49 +1499,30 @@
     token_values = tokens.astype(f32)
     scale_one = rms_scale(token_values)
     attn_gain = gain_one.astype(f32)
-    normed_attn = (token_values * scale_one * attn_gain).astype(bf)
-    qkv = jnp.dot(normed_attn, wide_full, preferred_element_type=f32).astype(bf)
-    queries = qkv[:, :model_width]
-    kv_own = qkv[:, model_width:wide_width]
     reach_count = (HALF - 2) // tok_rows + 1
-    offsets = list(range(reach_count, 0, -1)) + list(range(-1, -reach_count - 1, -1))
-    arrived = [passed_along(kv_own, "fsdp", offset) for offset in offsets]
-    kv_rows = jnp.concatenate(arrived[:reach_count] + [kv_own] + arrived[reach_count:], axis=0)
-    ordered = offsets[:reach_count] + [0] + offsets[reach_count:]
+    slots = 2 * reach_count + 1
+    key_count = slots * tok_rows
     row_index = jnp.arange(tok_rows, dtype=jnp.int32)
     query_places = device * tok_rows + row_index
-    key_places = jnp.concatenate([(device - offset) * tok_rows + row_index for offset in ordered])
+    key_places = (device - reach_count) * tok_rows + jnp.arange(key_count, dtype=jnp.int32)
     query_docs = document_of(query_places, doc_lengths, seq_len)
     key_docs = document_of(key_places, doc_lengths, seq_len)
+    near_by = (key_docs >= 0) & (key_places // seq_len == query_places[0] // seq_len)
     visible = (
         (query_docs[:, None] == key_docs[None, :])
-        & (key_docs[None, :] >= 0)
+        & near_by[None, :]
         & (jnp.abs(query_places[:, None] - key_places[None, :]) < HALF)
     )
-    key_count = kv_rows.shape[0]
-    query_heads = queries.reshape(tok_rows, head_count, head_size)
-    key_heads = kv_rows[:, :model_width].reshape(key_count, head_count, head_size)
-    value_heads = kv_rows[:, model_width:].reshape(key_count, head_count, head_size)
-
-    def scores_of():
-        raw_scores = (
-            jnp.einsum("qhd,khd->hqk", query_heads, key_heads, preferred_element_type=f32)
-            * score_scale
-        )
-        return jnp.where(visible[None], raw_scores, masked)
-
-    scores = scores_of()
-    head_top = jnp.max(scores, axis=2, keepdims=True)
-    exponents = jnp.exp(scores - head_top)
-    totals = jnp.sum(exponents, axis=2, keepdims=True)
-    log_total = head_top + jnp.log(totals)
-    probs_low = (exponents / totals).astype(bf)
-    own_top = jnp.max(head_top, axis=(1, 2))
-    context = (
-        jnp.einsum("hqk,khd->qhd", probs_low, value_heads, preferred_element_type=f32)
-        .reshape(tok_rows, model_width)
-        .astype(bf)
-    )
+    bias = jnp.where(visible, 0.0, masked)
+    near_values = jnp.where(near_by[:, None], near_tokens.reshape(key_count, model_width).astype(f32), 0.0)
+    near_normed = (near_values * rms_scale(near_values) * attn_gain).astype(bf)
+    own_first = reach_count * tok_rows
+    normed_attn = near_normed[own_first : own_first + tok_rows]
+    queries = jnp.dot(normed_attn, wide_full[:, :model_width], preferred_element_type=f32).astype(bf)
+    keys_values = jnp.dot(
+        near_normed, wide_full[:, model_width:wide_width], preferred_element_type=f32
+    ).astype(bf)
+    context, log_total, own_top = attend(queries, keys_values, bias, head_count, score_scale)
     attended = token_values + jnp.dot(context, out_full, preferred_element_type=f32)
     scale_two = rms_scale(attended)
     moe_gain = gain_two.astype(f32)
@@ -1162,11 +1535,13 @@
     share_rows = jnp.concatenate(
         (
             jnp.pad(gate_share, ((0, 0), (0, 128 - experts))),
-            jnp.pad(own_top[None, :], ((0, 7), (0, 128 - head_count))),
+            own_top,
         ),
         axis=0,
     )
-    x_all, s_all = plane_gather([normed_moe, share_rows], 0)
+    expert_results = expert_pass(normed_moe, share_rows, c_all, expert_weights, experts, 0)
+    s_all, mix_part, grad_from_experts, grad_share = [expert_results[i] for i in (1, 2, 4, 5)]
+    x_terms, own_sum = expert_results[12], expert_results[11]
     head_max = jnp.max(s_all[:, tok_rows, :head_count], axis=0)
     head_max = jnp.maximum(head_max, swapped(head_max, "fsdp", 0))
     head_max = jnp.maximum(head_max, swapped(head_max, "fsdp", 1))
@@ -1174,21 +1549,8 @@
     columns = jnp.repeat(jnp.sqrt(factor), head_size)
     clipped_query = (w_query.astype(f32) * columns[None, :]).astype(bf)
     clipped_key = (w_key.astype(f32) * columns[None, :]).astype(bf)
-    mix_part, gx_part, gs_part, own_grads, core_grads, x_grads, corner_grads = expert_pass(
-        x_all, c_all, s_all, expert_weights, experts
-    )
-    plane_shape = x_all.shape
-    grad_from_experts, grad_share, mixture = plane_reduce(
-        [gx_part.reshape(plane_shape), gs_part, mix_part.reshape(plane_shape)], 1
-    )
-    mixed = (attended + mixture.astype(f32)).astype(bf)
+    mixture = lax.psum_scatter(mix_part, "fsdp", axis_index_groups=planes, tiled=True)
     grad_share = jnp.transpose(grad_share)
-    core_terms, corner_terms = swapped((core_grads, corner_grads), "fsdp", 0)
-    own_sum = own_grads.astype(f32) + core_terms.astype(f32)
-    x_sum = (x_grads.astype(f32) + corner_terms.astype(f32)).astype(bf)
-    x_terms = swapped(x_sum, "fsdp", 1)
-    expert_grads = own_sum + x_terms.astype(f32)
-    grad_gate, grad_up, grad_down = expert_grads[0], expert_grads[1], expert_grads[2]
     grad_mixed = cotangent.astype(f32)
     grad_logits = gate_share * (grad_share - jnp.sum(gate_share * grad_share, axis=1, keepdims=True))
     grad_router_part = jnp.dot(normed_moe.astype(f32).T, grad_logits, precision=highest)
@@ -1199,44 +1561,18 @@
     grad_attended = grad_mixed + grad_from_norm
     grad_attended_low = grad_attended.astype(bf)
     grad_out_part = contract(context, grad_attended_low, 0, 0).astype(bf)
-    grad_context = (
-        contract(grad_attended_low, out_full, 1, 1)
-        .astype(bf)
-        .reshape(tok_rows, head_count, head_size)
-    )
-    probs = jnp.exp(scores_of() - log_total)
-    probs_back = probs.astype(bf)
-    grad_values = jnp.einsum("hqk,qhd->khd", probs_back, grad_context, preferred_element_type=f32)
-    grad_probs = jnp.einsum("qhd,khd->hqk", grad_context, value_heads, preferred_element_type=f32)
-    grad_scores = (
-        probs * (grad_probs - jnp.sum(probs * grad_probs, axis=2, keepdims=True))
-    ).astype(bf)
-    grad_queries = (
-        (
-            jnp.einsum("hqk,khd->qhd", grad_scores, key_heads, preferred_element_type=f32)
-            * score_scale
-        )
-        .reshape(tok_rows, model_width)
-        .astype(bf)
-    )
-    grad_keys = (
-        jnp.einsum("hqk,qhd->khd", grad_scores, query_heads, preferred_element_type=f32)
-        * score_scale
-    )
-    grad_kv = jnp.concatenate(
-        (grad_keys.reshape(key_count, model_width), grad_values.reshape(key_count, model_width)),
-        axis=1,
-    )
-    grad_blocks = [
-        grad_kv[position * tok_rows : (position + 1) * tok_rows] for position in range(len(ordered))
-    ]
-    own_block = grad_blocks[reach_count]
-    remote_blocks = grad_blocks[:reach_count] + grad_blocks[reach_count + 1 :]
-    returned = [
-        passed_along(grad_block.astype(bf), "fsdp", -offset).astype(grad_block.dtype)
-        for grad_block, offset in zip(remote_blocks, offsets)
-    ]
-    grad_kv_low = reduce(jnp.add, returned, own_block).astype(bf)
+    out_sum = lax.psum_scatter(grad_out_part, "fsdp", scatter_dimension=0, tiled=True)
+    grad_context = contract(grad_attended_low, out_full, 1, 1).astype(bf)
+    grad_queries, near_keys, near_values_grad = attend_back(
+        queries, keys_values, grad_context, bias, log_total, head_count, score_scale
+    )
+    near_shape = (slots, tok_rows, model_width)
+    grad_kv_low = return_near(
+        [near_keys.reshape(near_shape), near_values_grad.reshape(near_shape)], per_seq, 1
+    )
+    grad_kv_low, own_sum, x_terms = lax.optimization_barrier((grad_kv_low, own_sum, x_terms))
+    expert_grads = own_sum.astype(f32) + x_terms.astype(f32)
+    grad_gate, grad_up, grad_down = expert_grads[0], expert_grads[1], expert_grads[2]
     grad_qkv = jnp.concatenate((grad_queries, grad_kv_low), axis=1)
     grad_qkv_part = contract(normed_attn, grad_qkv, 0, 0).astype(bf)
     grad_normed_attn = contract(jnp.pad(grad_qkv, ((0, 0), (0, 128))), wide_full, 1, 1)
@@ -1247,21 +1583,22 @@
         ((0, 0), (0, 128 - experts - 2)),
     )
     owners = (devices // 2, 2, weight_rows)
-    qkv_sum, out_sum, extra_sum = full_reduce(
+    qkv_sum, extra_sum = full_reduce(
         [
             grad_qkv_part.reshape(owners + (wide_width,)),
-            grad_out_part.reshape(owners + (model_width,)),
             extra_part.reshape(owners + (128,)),
         ],
         3,
     )
+    mixture, out_sum, qkv_sum = lax.optimization_barrier((mixture, out_sum, qkv_sum))
+    mixed = (attended + mixture.astype(f32)).astype(bf)
     return (
         mixed,
         grad_tokens,
         qkv_sum[:, :model_width],
         qkv_sum[:, model_width : 2 * model_width],
         qkv_sum[:, 2 * model_width :],
-        out_sum,
+        out_sum.astype(f32),
         extra_sum[:, :experts],
         extra_sum[:, experts],
         extra_sum[:, experts + 1],

time: 1510 us -> 1130 us (0.75)
  waiting for transfers between devices: 244 us -> 66.8 us
  local copies, waits for them, and re-layouts: 75.1 us -> 26.5 us
  starting transfers between devices: 51.9 us -> 6.55 us
  other arithmetic: 81.3 us -> 38.2 us
  Pallas kernels: 920 us -> 881 us
  matrix products: 116 us -> 83.8 us
    ppermute x8 -> x0, waiting for transfers between devices: 227 us -> none  [passed_along(): return lax.ppermute(x, axis, pairs)]
    pallas_call x1, Pallas kernels: 246 us -> 194 us  [full_reduce(): pl.pallas_call(body, in_specs=[anys] * count, out_specs=[pl.BlockSpec(mem...]
    ppermute x14 -> x11, waiting for transfers between devices: 16.4 us -> 66.1 us  [swapped(): return lax.ppermute(block, axis, route)]
    dot_general x7 -> x2, matrix products: 67.1 us -> 34.8 us  [the longest x1 27.1 us: dense_layer(): jnp.dot(near_normed, wide_full[:, model_width:wide_width], preferred_elem...]
    ppermute x8 -> x0, starting transfers between devices: 27.3 us -> none  [passed_along(): return lax.ppermute(x, axis, pairs)]
    unnamed x84 -> x63, local copies, waits for them, and re-layouts: 34 us -> 8.97 us
    convert_element_type x3, other arithmetic: 30.4 us -> 6.73 us  [the longest x1 4.6 us: dense_layer(): near_normed = (near_values * rms_scale(near_values) * attn_gain).astype(bf)]
    ppermute x14 -> x11, starting transfers between devices: 24.6 us -> 6.43 us  [swapped(): return lax.ppermute(block, axis, route)]
  transfers between devices with their start and end apart: 23 -> 14, of which waited for: 11 -> 4; matrix products, arithmetic and copies ran while one was open for 12% -> 11% of each run, Pallas kernels for 23% -> 34%
where the time goes in v2:
time: 1130 us; the launch traced here: 1120 us
  Pallas kernels  881 us (78%)
  matrix products  83.8 us (7%)
  waiting for transfers between devices  66.8 us (6%)
  other arithmetic  38.2 us (3%)
  local copies, waits for them, and re-layouts  26.5 us (2%)
  between operations  17.4 us (2%)
    pallas_call x1, Pallas kernels, expert_pass(): pl.pallas_call(functools.partial(expert_body, shard, width, half, block,...  314 us
    pallas_call x1, Pallas kernels, full_reduce(): pl.pallas_call(body, in_specs=[anys] * count, out_specs=[pl.BlockSpec(mem...  194 us
    pallas_call x1, Pallas kernels, full_gather(): pl.pallas_call(body, in_specs=[anys] * (count + 1), out_specs=[anys] * (c...  190 us
    pallas_call x1, Pallas kernels, return_near(): pl.pallas_call(functools.partial(return_body, per_seq), in_specs=[anys, a...  139 us
    ppermute x11, waiting for transfers between devices, swapped(): return lax.ppermute(block, axis, route)  66.1 us
    dot_general x4, matrix products, contract(): lax.dot_general(left, right, (((left_dim,), (right_dim,)), ((), ())), pre...  39.2 us
    dot_general x1, matrix products, dense_layer(): jnp.dot(near_normed, wide_full[:, model_width:wide_width], preferred_elem...  27.1 us
    pallas_call x1, Pallas kernels, attend_back(): pl.pallas_call(functools.partial(attend_back_body, scale), grid=(heads,),...  23.5 us
  transfers between devices with their start and end apart: 14, of which 4 were waited for; matrix products, arithmetic and copies ran while one was open for 11% of the time, Pallas kernels for 34%

profile of v2, /device:TPU:16, one launch (start us, length us, event | category | flops | bytes accessed | tf_op | source)
XLA Modules:
  0.0 1119.8 jit_solution(4682682191743360197)
XLA Ops:
  10.1 190.4 %full_gather.1 = (bf16[32,64,6272]{2,1,0:T(8,128)(2,1)}, bf16[32,64,2048]{2,1,0:T(8,128)(2,1)}, bf16[5,256,2048]{2,1,0:T(8,128)(2,1)}) custom-call(bf16[64,6272]{1,0:T(8,128)(2,1)} %fusion.33.refs_0_, bf16[64,2048]{1,0:T(8,128)(2,1)} %refs_1_.1, bf16[256,2048]{1,0:T(8,128)(2,1)} %refs_2_.1), custom_call_target="tpu_custom_call" | custom-call | tf_op jit(solution)/shard_map/full_gather/pallas_call | solution.py:571
  207.5 4.5 multiply_reduce_fusion
  215.5 4.6 fusion.7
  220.1 7.7 fusion.15.q_ref
  227.9 27.1 %fusion.2.k_ref.v_ref = bf16[1280,4096]{1,0:T(8,128)(2,1)} fusion(bf16[1280,2048]{1,0:T(8,128)(2,1)S(1)} %fusion.7, bf16[2048,6272]{1,0:T(8,128)(2,1)} %bitcast.61), kind=kOutput, calls=%fused_computation.3 | convolution fusion | flops 21480079360 | bytes 32505856 | tf_op jit(solution)/shard_map/dot_general | solution.py:1522
  255.0 19.5 %attend.1 = (bf16[256,2048]{1,0:T(8,128)(2,1)S(1)}, f32[256,128]{1,0:T(8,128)S(1)}, f32[8,128]{1,0:T(8,128)S(1)}) custom-call(bf16[256,2048]{1,0:T(8,128)(2,1)S(1)} %fusion.15.q_ref, bf16[1280,4096]{1,0:T(8,128)(2,1)} %fusion.2.k_ref.v_ref, bf16[1280,4096]{1,0:T(8,128)(2,1)} %fusion.2.k_ref.v_ref, f32[256,1280]{1,0:T(8,128)S(1)} %fusion.27.bias_ref), custom_call_target="tpu_custom_call" | custom-call | tf_op jit(solution)/shard_map/attend/pallas_call | solution.py:1271
  274.7 19.7 %collective-permute-done.2.refs_5_ = bf16[512,2048]{1,0:T(8,128)(2,1)} collective-permute-done((bf16[512,2048]{1,0:T(8,128)(2,1)}, bf16[512,2048]{1,0:T(8,128)(2,1)}, u32[]{:S(2)}, u32[]{:S(2)}) %collective-permute-start.2) | collective-permute-done | bytes 2097184 | tf_op jit(solution)/shard_map/ppermute | solution.py:32
  294.4 44.4 %collective-permute-done.4.refs_7_ = bf16[512,2048]{1,0:T(8,128)(2,1)} collective-permute-done((bf16[512,2048]{1,0:T(8,128)(2,1)}, bf16[512,2048]{1,0:T(8,128)(2,1)}, u32[]{:S(2)}, u32[]{:S(2)}) %collective-permute-start.4) | collective-permute-done | bytes 2097184 | tf_op jit(solution)/shard_map/ppermute | solution.py:32
  346.3 314.3 %expert_pass.1 = (bf16[8,256,2048]{2,1,0:T(8,128)(2,1)}, f32[8,264,128]{2,1,0:T(8,128)}, bf16[2048,2048]{1,0:T(8,128)(2,1)}, bf16[2048,2048]{1,0:T(8,128)(2,1)},...) custom-call(bf16[256,2048]{1,0:T(8,128)(2,1)} %copy-done.12, ...), custom_call_target="tpu_custom_call" | custom-call | tf_op jit(solution)/shard_map/expert_pass/pallas_call | solution.py:1206
  661.5 3.8 multiply_reduce_fusion.1
  666.6 5.7 convolution_convert_fusion.1
  675.5 5.9 convolution_convert_fusion.2.g_ref
  681.4 23.5 %attend_back.1 = (bf16[256,2048]{1,0:T(8,128)(2,1)S(1)}, bf16[1280,2048]{1,0:T(8,128)(2,1)}, bf16[1280,2048]{1,0:T(8,128)(2,1)}) custom-call(bf16[256,2048]{1,0:T(8,128)(2,1)S(1)} %copy-done.5, bf16[1280,4096]{1,0:T(8,128)(2,1)} %fusion.2.k_ref.v_ref, bf16[1280,4096]{1,0:T(8,128)(2,1)} %fusion.2.k_ref.v_ref, ...), custom_call_target="tpu_custom_call" | custom-call | tf_op jit(solution)/shard_map/attend_back/pallas_call | solution.py:1316
  704.9 2.5 copy-done.2
  707.4 2.5 copy-done.3
  709.9 139.1 %return_near.1 = bf16[256,4096]{1,0:T(8,128)(2,1)S(1)} custom-call(bf16[5,256,2048]{2,1,0:T(8,128)(2,1)S(1)} %bitcast.53, bf16[5,256,2048]{2,1,0:T(8,128)(2,1)S(1)} %bitcast.54), custom_call_target="tpu_custom_call" | custom-call | tf_op jit(solution)/shard_map/return_near/pallas_call | solution.py:1424
  852.7 14.0 %fusion.20 = (f32[256]{0:T(256)S(1)}, f32[2048]{0:T(1024)S(1)}, f32[256,2048]{1,0:T(8,128)}) fusion(bf16[256,2048]{1,0:T(8,128)(2,1)S(1)} %copy-done.15, f32[2048]{0:T(1024)S(1)} %bitcast.69, f32[256]{0:T(256)S(1)} %add_rsqrt_fusion.1, bf16[2048,6272]{1,0:T(8,128)(2,1)} %bitcast.64, bf16[256,6144]{1,0:T(8,128)(2,1)} %constant_dynamic-update-slice_fusion), kind=kOutput, calls=%fused_computation.29 | convolution fusion | flops 6580336640 | bytes 32000000 | tf_op jit(solution)/shard_map/dot_general | solution.py:65
  868.2 13.5 %convolution_convert_fusion = bf16[2048,6144]{1,0:T(8,128)(2,1)} fusion(bf16[256,6144]{1,0:T(8,128)(2,1)} %constant_dynamic-update-slice_fusion, bf16[1280,2048]{1,0:T(8,128)(2,1)} %copy-done.16), kind=kOutput, calls=%fused_computation | convolution fusion | flops 6455033856 | bytes 29360128 | tf_op jit(solution)/shard_map/dot_general | solution.py:65
  881.8 193.9 %full_reduce.1 = (f32[64,6144]{1,0:T(8,128)}, f32[64,128]{1,0:T(8,128)}) custom-call(bf16[16,2,64,6144]{3,2,1,0:T(8,128)(2,1)} %bitcast.55, f32[16,2,64,128]{3,2,1,0:T(8,128)} %bitcast.57), custom_call_target="tpu_custom_call" | custom-call | tf_op jit(solution)/shard_map/full_reduce/pallas_call | solution.py:704
  1075.7 4.2 fusion.23
  1079.8 12.2 %convert_add_fusion = f32[3,512,2048]{2,1,0:T(8,128)} fusion(bf16[3,512,2048]{2,1,0:T(8,128)(2,1)} %get-tuple-element.68, bf16[3,512,2048]{2,1,0:T(8,128)(2,1)} %get-tuple-element.67), kind=kLoop, calls=%fused_computation.4 | loop fusion | flops 9437184 | bytes 25165824 | tf_op jit(solution)/shard_map/add | solution.py:1574
  1092.1 9.9 slice_bitcast_fusion
  1102.7 2.8 collective-permute-start.10
  1108.0 2.6 fusion.67
  (139 shorter events, 34.1 us)
Async XLA Ops:
  7.2 339.1 %all-gather.3.cloned.1.call-start = ((), (), s32[]{:S(2)}) async-start(), calls=%async_computation.4 | async-start | bytes 9437184 | tf_op jit(solution)/shard_map/all_gather | solution.py:1488
  8.1 198.5 %copy-start.25 = (s32[2,4]{1,0:T(2,128)S(1)}, s32[2,4]{1,0:T(2,128)}, u32[]{:S(2)}) copy-start(s32[2,4]{1,0:T(2,128)} %param.27) | copy-start | bytes 100
  200.6 907.4 %reduce-scatter.5.cloned.1.call-start = ((), (), s32[]{:S(2)}) async-start(), calls=%async_computation.3 | async-start | bytes 8650752 | tf_op jit(solution)/shard_map/reduce_scatter | solution.py:1564
  200.6 73.9 %collective-permute-start = (bf16[512,2048]{1,0:T(8,128)(2,1)}, bf16[512,2048]{1,0:T(8,128)(2,1)}, u32[]{:S(2)}, u32[]{:S(2)}) collective-permute-start(bf16[512,2048]{1,0:T(8,128)(2,1)} %refs_9_), channel_id=1, source_target_pairs={{0,2},{2,0},{1,3},{3,1},{4,6},{6,4},{5,7},{7,5},{8,10},{10,8},{9,1... | collective-permute-start | bytes 6291464 | tf_op jit(solution)/shard_map/ppermute | solution.py:32
  201.2 137.6 %collective-permute-start.6 = (bf16[512,2048]{1,0:T(8,128)(2,1)}, bf16[512,2048]{1,0:T(8,128)(2,1)}, u32[]{:S(2)}, u32[]{:S(2)}) collective-permute-start(bf16[512,2048]{1,0:T(8,128)(2,1)} %refs_9_), channel_id=1, source_target_pairs={{0,1},{1,0},{2,3},{3,2},{4,5},{5,4},{6,7},{7,6},{8,9},{9,8},{10,11... | collective-permute-start | bytes 6291464 | tf_op jit(solution)/shard_map/ppermute | solution.py:32
  201.3 93.1 %collective-permute-start.2 = (bf16[512,2048]{1,0:T(8,128)(2,1)}, bf16[512,2048]{1,0:T(8,128)(2,1)}, u32[]{:S(2)}, u32[]{:S(2)}) collective-permute-start(bf16[512,2048]{1,0:T(8,128)(2,1)} %refs_11_), channel_id=1, source_target_pairs={{0,2},{2,0},{1,3},{3,1},{4,6},{6,4},{5,7},{7,5},{8,10},{10,8},{9,1... | collective-permute-start | bytes 6291464 | tf_op jit(solution)/shard_map/ppermute | solution.py:32
  202.8 142.3 %collective-permute-start.7 = (bf16[512,2048]{1,0:T(8,128)(2,1)}, bf16[512,2048]{1,0:T(8,128)(2,1)}, u32[]{:S(2)}, u32[]{:S(2)}) collective-permute-start(bf16[512,2048]{1,0:T(8,128)(2,1)} %refs_11_), channel_id=1, source_target_pairs={{0,1},{1,0},{2,3},{3,2},{4,5},{5,4},{6,7},{7,6},{8,9},{9,8},{10,11... | collective-permute-start | bytes 6291464 | tf_op jit(solution)/shard_map/ppermute | solution.py:32
  203.0 135.8 %collective-permute-start.4 = (bf16[512,2048]{1,0:T(8,128)(2,1)}, bf16[512,2048]{1,0:T(8,128)(2,1)}, u32[]{:S(2)}, u32[]{:S(2)}) collective-permute-start(bf16[512,2048]{1,0:T(8,128)(2,1)} %refs_13_), channel_id=1, source_target_pairs={{0,2},{2,0},{1,3},{3,1},{4,6},{6,4},{5,7},{7,5},{8,10},{10,8},{9,1... | collective-permute-start | bytes 6291464 | tf_op jit(solution)/shard_map/ppermute | solution.py:32
  215.5 39.5 %copy-start = (f32[256,1280]{1,0:T(8,128)}, f32[256,1280]{1,0:T(8,128)S(1)}, u32[]{:S(2)}) copy-start(f32[256,1280]{1,0:T(8,128)S(1)} %fusion.27.bias_ref) | copy-start | bytes 3932164
  220.1 119.2 %slice-start = ((s8[8388608]{0:T(1024)(128)(4,1)}), s8[4194304]{0:T(1024)(128)(4,1)S(1)}, s32[]{:S(2)}) async-start(s8[8388608]{0:T(1024)(128)(4,1)} %bitcast.76), calls=%async_computation.5 | async-start | bytes 8388608
  227.9 27.1 %copy-start.4 = (bf16[256,2048]{1,0:T(8,128)(2,1)}, bf16[256,2048]{1,0:T(8,128)(2,1)S(1)}, u32[]{:S(2)}) copy-start(bf16[256,2048]{1,0:T(8,128)(2,1)S(1)} %fusion.15.q_ref) | copy-start | bytes 3145732
  227.9 111.4 %slice-start.1 = ((s8[8388608]{0:T(1024)(128)(4,1)}), s8[4194304]{0:T(1024)(128)(4,1)S(1)}, s32[]{:S(2)}) async-start(s8[8388608]{0:T(1024)(128)(4,1)} %bitcast.76), calls=%async_computation.6 | async-start | bytes 8388608
  255.0 84.3 %copy-start.14 = (bf16[256,2048]{1,0:T(8,128)(2,1)S(1)}, bf16[256,2048]{1,0:T(8,128)(2,1)}, u32[]{:S(2)}) copy-start(bf16[256,2048]{1,0:T(8,128)(2,1)} %refs_2_.1) | copy-start | bytes 3145732
  274.5 67.3 %copy-start.6 = (bf16[256,2048]{1,0:T(8,128)(2,1)}, bf16[256,2048]{1,0:T(8,128)(2,1)S(1)}, u32[]{:S(2)}) copy-start(bf16[256,2048]{1,0:T(8,128)(2,1)S(1)} %get-tuple-element.44) | copy-start | bytes 3145732
  274.5 70.6 %collective-permute-start.8 = (bf16[512,2048]{1,0:T(8,128)(2,1)}, bf16[512,2048]{1,0:T(8,128)(2,1)}, u32[]{:S(2)}, u32[]{:S(2)}) collective-permute-start(bf16[512,2048]{1,0:T(8,128)(2,1)} %refs_13_), channel_id=1, source_target_pairs={{0,1},{1,0},{2,3},{3,2},{4,5},{5,4},{6,7},{7,6},{8,9},{9,8},{10,11... | collective-permute-start | bytes 6291464 | tf_op jit(solution)/shard_map/ppermute | solution.py:32
  294.4 50.8 %collective-permute-start.1 = (bf16[512,2048]{1,0:T(8,128)(2,1)}, bf16[512,2048]{1,0:T(8,128)(2,1)}, u32[]{:S(2)}, u32[]{:S(2)}) collective-permute-start(bf16[512,2048]{1,0:T(8,128)(2,1)} %collective-permute-done.refs_3_), channel_id=1, source_target_pairs={{0,1},{1,0},{2,3},{3,2},{4,5},{5,4},{6,7},{7,6},{8,9},{9,8},{10,11... | collective-permute-start | bytes 6291464 | tf_op jit(solution)/shard_map/ppermute | solution.py:32
  338.8 6.4 collective-permute-start.3
  338.8 7.5 collective-permute-start.5
  672.3 435.7 %reduce-scatter.3.cloned.1.call-start = ((), (), s32[]{:S(2)}) async-start(), calls=%async_computation.2 | async-start | bytes 9437184 | tf_op jit(solution)/shard_map/reduce_scatter | solution.py:1552
  675.4 427.3 %collective-permute-start.9 = (f32[16]{0:T(128)S(1)}, f32[16]{0:T(128)S(1)}, u32[]{:S(2)}, u32[]{:S(2)}) collective-permute-start(f32[16]{0:T(128)S(1)} %slice_reduce_fusion.2), channel_id=1, source_target_pairs={{0,1},{1,0},{2,3},{3,2},{4,5},{5,4},{6,7},{7,6},{8,9},{9,8},{10,11... | collective-permute-start | bytes 200 | tf_op jit(solution)/shard_map/ppermute | solution.py:32
  1092.1 14.9 %copy-start.26 = (f32[16]{0:T(128)S(1)}, f32[16]{0:T(128)}, u32[]{:S(2)}) copy-start(f32[16]{0:T(128)} %param.28) | copy-start | bytes 196
  1092.1 15.0 %copy-start.19 = (bf16[64,2048]{1,0:T(8,128)(2,1)S(1)}, bf16[64,2048]{1,0:T(8,128)(2,1)}, u32[]{:S(2)}) copy-start(bf16[64,2048]{1,0:T(8,128)(2,1)} %param.17) | copy-start | bytes 786436
  1092.1 15.0 %copy-start.20 = (bf16[64,2048]{1,0:T(8,128)(2,1)S(1)}, bf16[64,2048]{1,0:T(8,128)(2,1)}, u32[]{:S(2)}) copy-start(bf16[64,2048]{1,0:T(8,128)(2,1)} %param.16) | copy-start | bytes 786436
  1102.7 4.3 collective-permute-start.10
  (19 other events, 74.4 us)
Sparse Core Ops, SparseCore 0:
  200.7 123.5 all-gather.2
  672.4 196.3 reduce-scatter.4
  872.5 208.9 reduce-scatter.2

commit v3 on v2

--- a/solution.py
+++ b/solution.py
@@ -449,7 +449,92 @@
     near = z + 1 - 2 * lax.rem(z, 2)
     return [z, near, jnp.where(low, 2, 1), jnp.where(low, 3, 0)]
 
-def gather_all(per_seq, ins, near_in, outs, near_out, ssem, rsem, lsem, nsend, nrecv):
+def chain(z, y, x, core, per_seq):
+    chip = (z * 2 + y) * 2 + x
+    at = lax.rem(chip, per_seq)
+    before, after = at > 0, at < per_seq - 1
+    previous = (chip - jnp.where(before, 1, 0)) * 2 + core
+    following = (chip + jnp.where(after, 1, 0)) * 2 + core
+    return previous, following, before, after
+
+
+class Near:
+    def __init__(self, per_seq, ins, outs, blanks, holds, nsend, nrecv, lsem):
+        z, y, x, core = place()
+        self.core, self.ins, self.outs, self.blanks, self.holds = core, ins, outs, blanks, holds
+        self.nsend, self.nrecv, self.lsem = nsend, nrecv, lsem
+        self.c_dev = index_of(z, y, x, 1 - core)
+        self.previous, self.following, self.before, self.after = chain(z, y, x, core, per_seq)
+        self.passes = jnp.where(core == 0, self.after, self.before)
+        self.gets = jnp.where(core == 0, self.before, self.after)
+
+    def one(self, kind, a):
+        src, slot, device = (
+            (self.ins[a], 0, self.following),
+            (self.ins[a], 4, self.previous),
+            (self.ins[a], 1 + 2 * self.core, self.c_dev),
+            (self.outs[a].at[4 * (1 - self.core)], 3 - 2 * self.core, self.c_dev),
+        )[kind]
+        return remote(src, self.outs[a].at[slot], self.nsend.at[kind, a], self.nrecv.at[kind, a], device)
+
+    def own(self, a, store):
+        if store:
+            return pltpu.make_async_copy(self.holds[a], self.outs[a].at[2], self.lsem.at[0, a])
+        return pltpu.make_async_copy(self.ins[a], self.holds[a], self.lsem.at[0, a])
+
+    def fills(self, act):
+        missing = (
+            (jnp.logical_not(self.before), 0),
+            (jnp.logical_not(self.before) & (self.core == 0), 1),
+            (jnp.logical_not(self.after) & (self.core == 1), 3),
+            (jnp.logical_not(self.after), 4),
+        )
+        for n, (condition, slot) in enumerate(missing):
+            @pl.when(condition)
+            def _(n=n, slot=slot):
+                for a in range(len(self.ins)):
+                    act(pltpu.make_async_copy(self.blanks[a], self.outs[a].at[slot], self.lsem.at[n + 1, a]))
+
+    def start(self):
+        for a in range(len(self.ins)):
+            pl.when(self.after)(lambda a=a: self.one(0, a).start())
+            pl.when(self.before)(lambda a=a: self.one(1, a).start())
+            self.one(2, a).start()
+            self.own(a, False).start()
+            self.blanks[a][...] = jnp.zeros_like(self.blanks[a])
+        self.fills(lambda copy: copy.start())
+        for a in range(len(self.ins)):
+            self.own(a, False).wait()
+            self.own(a, True).start()
+
+    def finish(self):
+        for a in range(len(self.ins)):
+            pl.when(self.before)(lambda a=a: self.one(0, a).wait_recv())
+            pl.when(self.after)(lambda a=a: self.one(1, a).wait_recv())
+            pl.when(self.passes)(lambda a=a: self.one(3, a).start())
+        for a in range(len(self.ins)):
+            self.one(2, a).wait_recv()
+            pl.when(self.gets)(lambda a=a: self.one(3, a).wait_recv())
+            pl.when(self.after)(lambda a=a: self.one(0, a).wait_send())
+            pl.when(self.before)(lambda a=a: self.one(1, a).wait_send())
+            self.one(2, a).wait_send()
+            pl.when(self.passes)(lambda a=a: self.one(3, a).wait_send())
+            self.own(a, True).wait()
+        self.fills(lambda copy: copy.wait())
+
+
+def near_scratch(arrays):
+    sem = pltpu.SemaphoreType.DMA
+    count = len(arrays)
+    buffers = [pltpu.VMEM(a.shape, a.dtype) for a in arrays]
+    return buffers + buffers + [sem((4, count)), sem((4, count)), sem((5, count))]
+
+
+def near_shapes(arrays):
+    return [jax.ShapeDtypeStruct((5,) + a.shape, a.dtype) for a in arrays]
+
+
+def gather_all(near, ins, outs, ssem, rsem, lsem):
     count = len(ins)
     z, y, x, core = place()
     mid = (z == 1) | (z == 2)
@@ -459,27 +544,14 @@
     c_dev = index_of(z, y, x, 1 - core)
     up_dev = index_of(jnp.minimum(z + 1, 3), y, x, core)
     down_dev = index_of(jnp.maximum(z - 1, 0), y, x, core)
-    previous, following, before, after = chain(z, y, x, core, per_seq)
-    greet([x_dev, y_dev, c_dev, up_dev, down_dev, previous, following], [None, None, None, up, down, before, after])
+    greet(
+        [x_dev, y_dev, c_dev, up_dev, down_dev, near.previous, near.following],
+        [None, None, None, up, down, near.before, near.after],
+    )
     own = [pltpu.make_async_copy(ins[a], outs[a].at[index_of(z, y, x, core)], lsem.at[a]) for a in range(count)]
-    own.append(pltpu.make_async_copy(near_in, near_out.at[2], lsem.at[count]))
     for copy in own:
         copy.start()
-    passes = jnp.where(core == 0, after, before)
-    pass_slot = 4 * (1 - core)
-
-    def near(kind):
-        src, slot, device = (
-            (near_in, 0, following),
-            (near_in, 4, previous),
-            (near_in, 1 + 2 * core, c_dev),
-            (near_out.at[pass_slot], 3 - 2 * core, c_dev),
-        )[kind]
-        return remote(src, near_out.at[slot], nsend.at[kind], nrecv.at[kind], device)
-
-    pl.when(after)(lambda: near(0).start())
-    pl.when(before)(lambda: near(1).start())
-    near(2).start()
+    near.start()
     pending = []
 
     def go(kind, a, o, src, dst, device, condition=None):
@@ -538,15 +610,7 @@
             go(9, a, o, corner, corner, c_dev)
 
     first(0); first(1); second(0); first(2); second(1); third(0); first(3); second(2); third(1); second(3); third(2); third(3)
-    pl.when(before)(lambda: near(0).wait_recv())
-    pl.when(after)(lambda: near(1).wait_recv())
-    pl.when(passes)(lambda: near(3).start())
-    near(2).wait_recv()
-    pl.when(jnp.where(core == 0, before, after))(lambda: near(3).wait_recv())
-    pl.when(after)(lambda: near(0).wait_send())
-    pl.when(before)(lambda: near(1).wait_send())
-    near(2).wait_send()
-    pl.when(passes)(lambda: near(3).wait_send())
+    near.finish()
     for i in range(4):
         o = items[i]
         for a in range(count):
@@ -564,15 +628,17 @@
     count = len(arrays)
     anys = pl.BlockSpec(memory_space=pl.ANY)
     def body(*refs):
-        ins, near_in = refs[:count], refs[count]
-        outs, near_out = refs[count + 1:2 * count + 1], refs[2 * count + 1]
-        gather_all(per_seq, ins, near_in, outs, near_out, *refs[2 * count + 2:])
+        it = iter(refs)
+        take = lambda n: [next(it) for _ in range(n)]
+        ins, near_in, outs, near_out = take(count), take(1), take(count), take(1)
+        ssem, rsem, lsem = take(3)
+        near = Near(per_seq, near_in, near_out, take(1), take(1), *take(3))
+        gather_all(near, ins, outs, ssem, rsem, lsem)
     sem = pltpu.SemaphoreType.DMA
     return pl.pallas_call(
         body, in_specs=[anys] * (count + 1), out_specs=[anys] * (count + 1),
-        out_shape=[jax.ShapeDtypeStruct((32,) + a.shape, a.dtype) for a in arrays]
-        + [jax.ShapeDtypeStruct((5,) + near_rows.shape, near_rows.dtype)],
-        scratch_shapes=[sem((10, 4, count)), sem((10, 4, count)), sem((count + 1,)), sem((4,)), sem((4,))],
+        out_shape=[jax.ShapeDtypeStruct((32,) + a.shape, a.dtype) for a in arrays] + near_shapes([near_rows]),
+        scratch_shapes=[sem((10, 4, count)), sem((10, 4, count)), sem((count,))] + near_scratch([near_rows]),
         compiler_params=pltpu.CompilerParams(collective_id=cid, has_side_effects=True),
         name="full_gather")(*arrays, near_rows)
 
@@ -588,8 +654,10 @@
         return carry
     lax.fori_loop(0, total // step, one, 0)
 
-def reduce_all(parts, outs, accs, crecvs, dxs, dys, xrecvs, yrecvs, zrecvs, ssem, rsem, lsem, osem):
-    count = len(parts)
+def reduce_all(ins, extra, outs, held, accs, dxs, dys, xrecvs, yrecvs, zrecvs, ssem, rsem, lsem, csend, crecv):
+    left, wide, narrow = ins
+    left_v, right_v, extra_land = held
+    count = 2
     z, y, x, core = place()
     mid = (z == 1) | (z == 2)
     up, down = z < 3, z > 0
@@ -602,6 +670,10 @@
     items = line_items(z)[::-1]
     mine, xp, yp, dp = y * 2 + x, y * 2 + 1 - x, (1 - y) * 2 + x, (1 - y) * 2 + 1 - x
     pending = []
+    rows = left_v.shape[0] // 2
+    wide_width, narrow_width = wide.shape[1], narrow.shape[1]
+    features = left_v.shape[1] // 2
+    own_part, other_part = pl.ds(0, rows), pl.ds(rows, rows)
 
     def go(make, condition=None):
         if condition is None:
@@ -613,36 +685,67 @@
     def arrived(kind, a, o, land):
         remote(land, land, ssem.at[kind, 0, a], rsem.at[kind, o, a], c_dev).wait_recv()
 
-    loads = {}
-    for i, o in enumerate(items):
-        for a in range(count):
-            go(lambda o=o, a=a: remote(parts[a].at[pl.ds(o * 4, 4), 1 - core], crecvs[a].at[o],
-                                       ssem.at[0, o, a], rsem.at[0, o, a], c_dev))
-            loads[i, a] = pltpu.make_async_copy(parts[a].at[pl.ds(o * 4, 4), core], accs[a].at[o], lsem.at[o, a])
-            loads[i, a].start()
+    crossing = (
+        (left.at[1 - core], left_v.at[other_part]),
+        (wide, right_v.at[other_part, pl.ds(0, wide_width)]),
+        (narrow, right_v.at[other_part, pl.ds(wide_width, narrow_width)]),
+        (extra.at[:, 1 - core], extra_land),
+    )
+    staying = (
+        (left.at[core], left_v.at[own_part]),
+        (wide, right_v.at[own_part, pl.ds(0, wide_width)]),
+        (narrow, right_v.at[own_part, pl.ds(wide_width, narrow_width)]),
+    )
+
+    def cross(n):
+        return remote(crossing[n][0], crossing[n][1], csend.at[n], crecv.at[n], c_dev)
+
+    for n in range(4):
+        cross(n).start()
+    loads = [pltpu.make_async_copy(src, dst, lsem.at[n]) for n, (src, dst) in enumerate(staying)]
+    loads += [
+        pltpu.make_async_copy(extra.at[pl.ds(o * 4, 4), core], accs[1].at[o], lsem.at[3 + o]) for o in range(4)
+    ]
+    for copy in loads:
+        copy.start()
+    for copy in loads:
+        copy.wait()
+    for n in range(4):
+        cross(n).wait_recv()
+
+    chunk = 1024
 
     def first(i):
         o = items[i]
+        for at, begin, total in ((0, 0, wide_width), (features, wide_width, narrow_width)):
+            lines = pl.ds(pl.multiple_of(at + o * (features // 4), features // 4), features // 4)
+
+            def some(n, carry):
+                columns = pl.ds(pl.multiple_of(begin + n * chunk, chunk), chunk)
+                product = lax.dot_general(
+                    left_v[:, lines], right_v[:, columns], (((0,), (0,)), ((), ())), preferred_element_type=f32
+                )
+                accs[0][o, :, :, columns] = product.astype(bf).reshape(4, features // 16, chunk)
+                return carry
+
+            lax.fori_loop(0, total // chunk, some, 0)
+        for p in range(4):
+            accs[1][o, p] = accs[1][o, p] + extra_land[o * 4 + p]
         for a in range(count):
-            half = parts[a].shape[2] // 2
-            arrived(0, a, o, crecvs[a].at[o])
-            loads[i, a].wait()
-            for p in (dp, xp, yp, mine):
-                add_into(accs[a].at[o, p], crecvs[a].at[o, p])
-                if p is dp:
-                    go(lambda a=a, half=half: remote(accs[a].at[o, dp, pl.ds(0, half)], dxs[a].at[o], ssem.at[1, o, a], rsem.at[1, o, a], x_dev))
-                    go(lambda a=a, half=half: remote(accs[a].at[o, dp, pl.ds(half, half)], dys[a].at[o], ssem.at[2, o, a], rsem.at[2, o, a], y_dev))
+            half = accs[a].shape[2] // 2
+            go(lambda a=a, half=half: remote(accs[a].at[o, dp, pl.ds(0, half)], dxs[a].at[o], ssem.at[1, o, a], rsem.at[1, o, a], x_dev))
+            go(lambda a=a, half=half: remote(accs[a].at[o, dp, pl.ds(half, half)], dys[a].at[o], ssem.at[2, o, a], rsem.at[2, o, a], y_dev))
 
     def second(i):
         o = items[i]
         for a in range(count):
-            half = parts[a].shape[2] // 2
+            half = accs[a].shape[2] // 2
             arrived(1, a, o, dxs[a].at[o])
             add_into(accs[a].at[o, yp, pl.ds(0, half)], dxs[a].at[o])
-            go(lambda a=a, half=half: remote(accs[a].at[o, yp], yrecvs[a].at[o], ssem.at[4, o, a], rsem.at[4, o, a], y_dev))
+            go(lambda a=a: remote(accs[a].at[o, yp], yrecvs[a].at[o], ssem.at[4, o, a], rsem.at[4, o, a], y_dev))
             arrived(2, a, o, dys[a].at[o])
             add_into(accs[a].at[o, xp, pl.ds(half, half)], dys[a].at[o])
-            go(lambda a=a, half=half: remote(accs[a].at[o, xp], xrecvs[a].at[o], ssem.at[3, o, a], rsem.at[3, o, a], x_dev))
+            go(lambda a=a: remote(accs[a].at[o, xp], xrecvs[a].at[o], ssem.at[3, o, a], rsem.at[3, o, a], x_dev))
 
     def third(i):
         o = items[i]
@@ -684,29 +787,41 @@
                         lax.fori_loop(0, rows // step, one, 0)
 
     first(0); first(1); second(0); first(2); second(1); third(0); first(3); second(2); third(1); second(3); third(2); third(3)
+    for n in range(4):
+        cross(n).wait_send()
     for make, condition in pending:
         if condition is None:
             make().wait_send()
         else:
             pl.when(condition)(lambda make=make: make().wait_send())
 
-def full_reduce(parts, cid):
-    count = len(parts)
+def full_reduce(left, wide, narrow, extra, cid):
+    rows = extra.shape[2]
+    columns = wide.shape[1] + narrow.shape[1]
+    widths = ((columns, bf), (128, f32))
     anys = pl.BlockSpec(memory_space=pl.ANY)
+
     def body(*refs):
         it = iter(refs)
         take = lambda n: [next(it) for _ in range(n)]
-        reduce_all(*[take(count) for _ in range(9)], *it)
+        ins, extra_in, outs, held = take(3), next(it), take(2), take(3)
+        reduce_all(ins, extra_in, outs, held, *[take(2) for _ in range(6)], *it)
+
     sem = pltpu.SemaphoreType.DMA
-    scratch = []
-    for lead, cut in (((4, 4), 1), ((4, 4), 1), ((4,), 2), ((4,), 2), ((4,), 1), ((4,), 1), ((5,), 1)):
-        scratch += [pltpu.VMEM(lead + (p.shape[2] // cut, p.shape[3]), p.dtype) for p in parts]
+    tokens = left.shape[1]
+    scratch = [
+        pltpu.VMEM((2 * tokens, left.shape[2]), bf),
+        pltpu.VMEM((2 * tokens, columns), bf),
+        pltpu.VMEM((16, rows, 128), f32),
+    ]
+    for lead, cut in (((4, 4), 1), ((4,), 2), ((4,), 2), ((4,), 1), ((4,), 1), ((5,), 1)):
+        scratch += [pltpu.VMEM(lead + (rows // cut, width), dtype) for width, dtype in widths]
     return pl.pallas_call(
-        body, in_specs=[anys] * count, out_specs=[pl.BlockSpec(memory_space=pltpu.VMEM)] * count,
-        out_shape=[jax.ShapeDtypeStruct(p.shape[2:], f32) for p in parts],
-        scratch_shapes=scratch + [sem((6, 5, count)), sem((6, 5, count)), sem((4, count)), sem((count,))],
-        compiler_params=pltpu.CompilerParams(collective_id=cid, has_side_effects=True, vmem_limit_bytes=62 * 2**20),
-        name="full_reduce")(*parts)
+        body, in_specs=[anys] * 4, out_specs=[pl.BlockSpec(memory_space=pltpu.VMEM)] * 2,
+        out_shape=[jax.ShapeDtypeStruct((rows, width), f32) for width, dtype in widths],
+        scratch_shapes=scratch + [sem((6, 5, 2)), sem((6, 5, 2)), sem((7,)), sem((4,)), sem((4,))],
+        compiler_params=pltpu.CompilerParams(collective_id=cid, has_side_effects=True, vmem_limit_bytes=60 * 2**20),
+        name="full_reduce")(left, wide, narrow, extra)
 def nt(left, right):
     return lax.dot_general(left, right, (((1,), (1,)), ((), ())), preferred_element_type=f32)
 
@@ -722,15 +837,17 @@
 def expert_body(shard, width, half, block, cut, *refs):
     it = iter(refs)
     take = lambda n: [next(it) for _ in range(n)]
-    x_own, s_own, c_all = take(3)
-    weights = [[take(2) for _ in range(3)] for _ in range(2)]
-    x_all, s_all, mix, gx, gx_sum, gs_sum, y_land, z_land = take(8)
+    own, side, near, beyond = [take(1) for _ in range(4)]
+    c_all = next(it)
+    x_weights, corner_weights, own_weights = take(3), take(3), take(3)
+    x_all, mix, gx, gx_sum, gs_sum, y_land, z_land = take(7)
     core_land = take(2)
     grad_sum = take(2)
     x_land = next(it)
+    core_weights = take(3)
     xv, cv, sv, wv, acc, hid_s, gate_s, up_s, gst, gs_y, gs_z, ostage, prev = take(13)
     gsend, grecv, lsem, rsend, rrecv, csend, crecv, xsend, xrecv = take(9)
-    wsem, insem, osem, psem, dsem, hsem, tsem = take(7)
+    wsem, insem, osem, psem, dsem, hsem, tsem, wsend, wrecv = take(9)
     hidden = 2 * half
     tile = 2 * shard
     cuts = width // cut
@@ -754,58 +871,80 @@
     def farthest(k):
         return nearest(3 - k)
 
-    sources, landings = (x_own, s_own), (x_all, s_all)
-    own_rows = xv.at[0, pl.ds(pl.multiple_of(y * shard, shard), shard)]
-    own_in = [
-        pltpu.make_async_copy(x_own, own_rows, lsem.at[0]),
-        pltpu.make_async_copy(s_own, s_all.at[z * 2 + y], lsem.at[1]),
-    ]
-    own_out = pltpu.make_async_copy(own_rows, x_all.at[z * 2 + y], lsem.at[0])
+    landings = (x_all,)
+    marks = pl.ds(width, 128)
+    ends = jnp.logical_not(mid)
+
+    def part_of(r):
+        return pl.ds(pl.multiple_of(r * shard, shard), shard)
 
     def hop(kind, a, o, src, device):
         return remote(src, landings[a].at[o * 2 + y], gsend.at[kind, o, a], grecv.at[kind, o, a], device)
 
-    def gather_first():
-        for copy in own_in:
-            copy.start()
-        for a in range(2):
-            hop(2, a, z, sources[a], y_dev).start()
-            pl.when(up)(lambda a=a: hop(0, a, z, sources[a], up_dev).start())
-            pl.when(down)(lambda a=a: hop(1, a, z, sources[a], down_dev).start())
-
-    def gather_next(k):
-        o = nearest(k)
-        from_below = o < z
-        for a in range(2):
+    def column(k, a):
+        return (own[a], near[a])[k] if k < 2 else landings[a].at[items[k] * 2 + y]
+
+    def outwards(k, act):
+        for a in range(1):
+            src = beyond[a] if k == 2 else column(k, a)
+            pl.when(z == 1)(lambda a=a, src=src: act(hop(1, a, items[k], src, down_dev)))
+            pl.when(z == 2)(lambda a=a, src=src: act(hop(0, a, items[k], src, up_dev)))
+
+    def over(act):
+        for a in range(1):
+            pl.when(z == 1)(lambda a=a: act(hop(0, a, items[1], near[a], up_dev)))
+            pl.when(z == 2)(lambda a=a: act(hop(1, a, items[1], near[a], down_dev)))
+
+    def sideways(k, act):
+        for a in range(1):
+            if k == 2:
+                pl.when(mid)(lambda a=a: act(hop(2, a, items[k], beyond[a], y_dev)))
+                pl.when(ends)(lambda a=a: act(hop(2, a, items[k], column(k, a), y_dev)))
+            else:
+                act(hop(2, a, items[k], column(k, a), y_dev))
+
+    def column_landed(k, condition):
+        o = items[k]
+        for a in range(1):
             land = landings[a].at[o * 2 + y]
-
-            @pl.when(from_below)
-            def _():
-                hop(0, a, o, land, up_dev).wait_recv()
-                pl.when(mid)(lambda: hop(0, a, o, land, up_dev).start())
-
-            @pl.when(jnp.logical_not(from_below))
-            def _():
-                hop(1, a, o, land, down_dev).wait_recv()
-                pl.when(mid)(lambda: hop(1, a, o, land, down_dev).start())
-
-            hop(2, a, o, land, y_dev).start()
+            pl.when(condition & (o < z))(lambda a=a, land=land: hop(0, a, o, land, y_dev).wait_recv())
+            pl.when(condition & (o > z))(lambda a=a, land=land: hop(1, a, o, land, y_dev).wait_recv())
+
+    shares_over = [
+        (
+            pltpu.make_async_copy(
+                block[0].at[pl.ds(0, 16), marks], x_all.at[slot, pl.ds(0, 16), marks], lsem.at[n]
+            ),
+            condition,
+        )
+        for n, (block, slot, condition) in enumerate(
+            (
+                (own, z * 2 + y, None),
+                (side, z * 2 + 1 - y, None),
+                (near, items[1] * 2 + y, None),
+                (beyond, items[2] * 2 + y, mid),
+            )
+        )
+    ]
+
+    def shares(act):
+        for copy, condition in shares_over:
+            if condition is None:
+                act(copy)
+            else:
+                pl.when(condition)(lambda copy=copy: act(copy))
 
     def gather_landed(o):
-        for a in range(2):
+        for a in range(1):
             land = landings[a].at[o * 2 + 1 - y]
             remote(land, land, gsend.at[2, o, a], grecv.at[2, o, a], y_dev).wait_recv()
 
     def gather_sent():
-        for a in range(2):
-            pl.when(up)(lambda a=a: hop(0, a, z, sources[a], up_dev).wait_send())
-            pl.when(down)(lambda a=a: hop(1, a, z, sources[a], down_dev).wait_send())
-            for k in range(4):
-                hop(2, a, items[k], sources[a], y_dev).wait_send()
-            for k in range(1, 4):
-                o = items[k]
-                pl.when(mid & (o < z))(lambda a=a, o=o: hop(0, a, o, sources[a], up_dev).wait_send())
-                pl.when(mid & (o > z))(lambda a=a, o=o: hop(1, a, o, sources[a], down_dev).wait_send())
+        over(lambda copy: copy.wait_send())
+        for k in (2, 3):
+            outwards(k, lambda copy: copy.wait_send())
+        for k in (1, 2, 3):
+            sideways(k, lambda copy: copy.wait_send())
 
     def lines(block_index):
         return pl.ds(pl.multiple_of(block_index * shard, shard), shard)
@@ -1007,15 +1146,34 @@
             for r in range(2)
         ]
 
-    def x_loads(o, slot):
-        copies = []
-        for r in range(2):
-            part = pl.ds(r * shard, shard)
-            copies += [
-                pltpu.make_async_copy(x_all.at[o * 2 + r], xv.at[slot, part], insem.at[0, r, slot]),
-                pltpu.make_async_copy(s_all.at[o * 2 + r, pl.ds(0, shard)], sv.at[slot, part], insem.at[2, r, slot]),
-            ]
-        return copies
+    def x_load(k, slot, act):
+        for n in range(4):
+            o = items[n]
+
+            def bring(column, other):
+                for r, src in ((y, column[0]), (1 - y, other[0])):
+                    for which, target, part in ((0, xv, pl.ds(0, width)), (2, sv, marks)):
+                        act(
+                            pltpu.make_async_copy(
+                                src.at[:, part], target.at[slot, part_of(r)], insem.at[which, r, slot]
+                            )
+                        )
+
+            landed = [ref.at[o * 2 + y] for ref in landings]
+            other = side if n == 0 else [ref.at[o * 2 + 1 - y] for ref in landings]
+            if n < 2:
+                pl.when(k == n)(lambda n=n, other=other: bring((own, near)[n], other))
+            elif n == 2:
+                pl.when((k == n) & mid)(lambda other=other: bring(beyond, other))
+                pl.when((k == n) & ends)(lambda landed=landed, other=other: bring(landed, other))
+            else:
+                pl.when(k == n)(lambda landed=landed, other=other: bring(landed, other))
+
+    def start(copy):
+        copy.start()
+
+    def wait(copy):
+        copy.wait()
 
     def spot(o, n):
         return pl.ds(pl.multiple_of(o * tile, tile), tile), pl.ds(pl.multiple_of(n * cut, cut), cut)
@@ -1035,18 +1193,23 @@
         ]
 
     def weight_loads(number):
+        sources = list(zip(*((x_weights, corner_weights), (own_weights, core_weights))[number]))
         return [
-            pltpu.make_async_copy(weights[number][i][h], wv.at[i, pl.ds(h * half, half)], wsem.at[i, h])
-            for i in range(3)
-            for h in range(2)
+            pltpu.make_async_copy(src, wv.at[i, pl.ds(h * half, half)], wsem.at[i, h])
+            for i, pair in enumerate(sources)
+            for h, src in enumerate(pair)
         ]
+
+    def weights_across():
+        return [remote(own_weights[i], core_weights[i], wsend.at[i], wrecv.at[i], c_dev) for i in range(3)]
 
     def run_tile(number, o, slot):
         if number:
             for copy in earlier(o, 0, 0):
                 copy.start()
         pick = (lane == experts[number]).astype(f32)
-        share = jnp.sum(sv[slot] * pick, axis=1, keepdims=True)
+        halves_of = pick + (lane == experts[number] + gst.shape[1]).astype(f32)
+        share = jnp.sum(sv[slot].astype(f32) * halves_of, axis=1, keepdims=True)
 
         def hidden_block(j, dots):
             part = pl.ds(pl.multiple_of(j * block, block), block)
@@ -1109,42 +1272,61 @@
                 copy.wait()
 
     greet([x_dev, y_dev, c_dev, up_dev, down_dev], [None, None, None, up, down])
-    gather_first()
+    across = weights_across()
+    outwards(2, start)
+    over(start)
+    sideways(1, start)
     loads = weight_loads(0) + c_loads(items[0], 0)
     for copy in loads:
         copy.start()
+    x_load(0, 0, start)
+    shares(start)
     acc[...] = jnp.zeros_like(acc)
-    own_in[0].wait()
-    own_out.start()
-    for copy in loads[:-2]:
+    for copy in loads[:6]:
         copy.wait()
-    own_out.wait()
-    own_in[1].wait()
+    for copy in across:
+        copy.start()
 
     def first_pass(t, carry):
         slot = lax.rem(t, 2)
         o = nearest(t)
 
+        @pl.when(t == 1)
+        def _():
+            column_landed(3, mid)
+            outwards(3, start)
+            column_landed(2, ends)
+            sideways(2, start)
+
+        @pl.when(t == 2)
+        def _():
+            column_landed(3, ends)
+            sideways(3, start)
+
         @pl.when(t + 1 < tiles)
         def _():
-            gather_next(t + 1)
             for copy in c_loads(nearest(t + 1), 1 - slot):
                 copy.start()
 
-        gather_landed(o)
-        now = x_loads(o, slot)
-        for copy in now:
-            copy.start()
-        for copy in now + c_loads(o, slot):
+        @pl.when(t > 0)
+        def _():
+            gather_landed(o)
+            x_load(t, slot, start)
+
+        x_load(t, slot, wait)
+        for copy in c_loads(o, slot):
             copy.wait()
         run_tile(0, o, slot)
         return carry
 
     lax.fori_loop(0, tiles, first_pass, 0)
+    for copy in across:
+        copy.wait()
     loads = weight_loads(1)
-    begin = c_loads(items[3], 0) + x_loads(items[3], 0)
-    for copy in loads + begin:
+    for copy in loads + c_loads(items[3], 0):
         copy.start()
+    x_load(3, 0, start)
+    shares(wait)
     flush(0)
     x_copy().start()
     acc[...] = jnp.zeros_like(acc)
@@ -1157,11 +1339,13 @@
 
         @pl.when(t + 1 < tiles)
         def _():
-            for copy in c_loads(farthest(t + 1), 1 - slot) + x_loads(farthest(t + 1), 1 - slot):
+            for copy in c_loads(farthest(t + 1), 1 - slot):
                 copy.start()
-
-        for copy in c_loads(o, slot) + x_loads(o, slot):
+            x_load(2 - t, 1 - slot, start)
+
+        for copy in c_loads(o, slot):
             copy.wait()
+        x_load(3 - t, slot, wait)
         run_tile(1, o, slot)
         for copy in y_copies(o):
             copy.start()
@@ -1182,36 +1366,35 @@
     x_copy().wait()
 
 
-def expert_pass(x_own, s_own, c_all, weights, gs_rows, cid):
+def expert_pass(rows_in, c_all, x_weights, corner_weights, own_weights, gs_rows, cid):
     blocks, shard, width = c_all.shape
     rows = blocks * shard
-    half = weights[0][0][0].shape[0]
+    half = own_weights[0].shape[0]
     hidden = 2 * half
     tile, block, cut = 2 * shard, half, 512
     anys = pl.BlockSpec(memory_space=pl.ANY)
     sem = pltpu.SemaphoreType.DMA
-    flat = [w for one in weights for pair in one for w in pair]
+    flat = list(x_weights) + list(corner_weights) + list(own_weights)
     shaped = jax.ShapeDtypeStruct
     half_grads = shaped((3, half, width), bf)
     shapes = [
-        shaped((blocks, shard, width), bf),
-        shaped((blocks,) + s_own.shape, f32),
+        shaped((blocks, shard, width + 128), bf),
         shaped((rows, width), bf),
         shaped((rows, width), bf),
         shaped((shard, width), bf),
         shaped((gs_rows, shard), f32),
         shaped((4, shard, width), bf),
         shaped((5, shard, width), bf),
-    ] + [half_grads] * 5
+    ] + [half_grads] * 5 + [shaped((half, width), bf)] * 3
     return pl.pallas_call(
         functools.partial(expert_body, shard, width, half, block, cut),
-        in_specs=[anys] * (3 + len(flat)),
+        in_specs=[anys] * (5 + len(flat)),
         out_specs=[anys] * len(shapes),
         out_shape=shapes,
         scratch_shapes=[
             pltpu.VMEM((2, tile, width), bf),
             pltpu.VMEM((2, tile, width), bf),
-            pltpu.VMEM((2, tile, 128), f32),
+            pltpu.VMEM((2, tile, 128), bf),
             pltpu.VMEM((3, hidden, width), bf),
             pltpu.VMEM((3, hidden, width), f32),
             pltpu.VMEM((tile, hidden), bf),
@@ -1224,7 +1407,7 @@
             pltpu.VMEM((2, 2, tile, cut), bf),
             sem((3, 4, 2)),
             sem((3, 4, 2)),
-            sem((2,)),
+            sem((8,)),
             sem((2, 5, 2)),
             sem((2, 5, 2)),
             sem((2, 8)),
@@ -1238,12 +1421,14 @@
             sem((8,)),
             sem((8,)),
             sem((3, 2)),
+            sem((3,)),
+            sem((3,)),
         ],
         compiler_params=pltpu.CompilerParams(
             vmem_limit_bytes=63 * 2**20, collective_id=cid, has_side_effects=True
         ),
         name="expert_pass",
-    )(x_own, s_own, c_all, *flat)
+    )(*rows_in, c_all, *flat)
 def attend_body(scale, q_ref, k_ref, v_ref, bias_ref, out_ref, lse_ref, top_ref):
     head = pl.program_id(0)
     scores = nt(q_ref[...], k_ref[...]) * scale + bias_ref[...]
@@ -1264,17 +1449,17 @@
     top_ref[...] = jnp.where(row == head, jnp.max(top), top_ref[...])
 
 
-def attend(queries, keys_values, bias, heads, scale):
-    rows, width = queries.shape
-    keys = keys_values.shape[0]
+def attend(near_qkv, bias, heads, width, scale):
+    rows, keys = bias.shape
     size = width // heads
+    middle = keys // rows // 2
     return pl.pallas_call(
         functools.partial(attend_body, scale),
         grid=(heads,),
         in_specs=[
-            pl.BlockSpec((rows, size), lambda h: (0, h)),
-            pl.BlockSpec((keys, size), lambda h: (0, h)),
+            pl.BlockSpec((rows, size), lambda h: (middle, h)),
             pl.BlockSpec((keys, size), lambda h: (0, heads + h)),
+            pl.BlockSpec((keys, size), lambda h: (0, 2 * heads + h)),
             pl.BlockSpec((rows, keys), lambda h: (0, 0)),
         ],
         out_specs=[
@@ -1289,158 +1474,140 @@
         ],
         compiler_params=pltpu.CompilerParams(vmem_limit_bytes=48 * 2**20),
         name="attend",
-    )(queries, keys_values, keys_values, bias)
-
-
-def attend_back_body(scale, q_ref, k_ref, v_ref, g_ref, bias_ref, lse_ref, dq_ref, dk_ref, dv_ref):
+    )(near_qkv, near_qkv, near_qkv, bias)
+
+
+def attend_queries_body(scale, per_seq, heads, *refs):
+    it = iter(refs)
+    take = lambda n: [next(it) for _ in range(n)]
+    q_ref, k_ref, v_ref, g_ref, bias_ref, lse_ref = take(6)
+    sent, dq_ref, landed = take(2), next(it), take(2)
+    near = Near(per_seq, sent, landed, take(2), take(2), *take(3))
     head = pl.program_id(0)
+
+    @pl.when(head == 0)
+    def _():
+        greet([near.c_dev, near.previous, near.following], [None, near.before, near.after])
+        near.start()
+
     lane = lax.broadcasted_iota(jnp.int32, lse_ref.shape, 1)
     lse = jnp.sum(jnp.where(lane == head, lse_ref[...], 0.0), axis=1, keepdims=True)
-    queries, keys, grads = q_ref[...], k_ref[...], g_ref[...]
-    probs = jnp.exp(nt(queries, keys) * scale + bias_ref[...] - lse)
-    low = probs.astype(bf)
-    dv_ref[...] = tn(low, grads).astype(bf)
-    grad_probs = nt(grads, v_ref[...])
+    keys = k_ref[...]
+    probs = jnp.exp(nt(q_ref[...], keys) * scale + bias_ref[...] - lse)
+    grad_probs = nt(g_ref[...], v_ref[...])
     shift = jnp.sum(probs * grad_probs, axis=1, keepdims=True)
     grad_scores = (probs * (grad_probs - shift)).astype(bf)
     dq_ref[...] = (nn(grad_scores, keys) * scale).astype(bf)
-    dk_ref[...] = (tn(grad_scores, queries) * scale).astype(bf)
-
-
-def attend_back(queries, keys_values, grads, bias, lse, heads, scale):
-    rows, width = queries.shape
-    keys = keys_values.shape[0]
+    pl.when(head == heads - 1)(near.finish)
+
+
+def attend_queries(near_qkv, grads, bias, lse, stats, heads, scale, per_seq, cid):
+    rows, keys = bias.shape
+    width = grads.shape[1]
     size = width // heads
+    middle = keys // rows // 2
     own = pl.BlockSpec((rows, size), lambda h: (0, h))
-    seen = pl.BlockSpec((keys, size), lambda h: (0, h))
+    anys = pl.BlockSpec(memory_space=pl.ANY)
     return pl.pallas_call(
-        functools.partial(attend_back_body, scale),
+        functools.partial(attend_queries_body, scale, per_seq, heads),
         grid=(heads,),
         in_specs=[
-            own,
-            seen,
+            pl.BlockSpec((rows, size), lambda h: (middle, h)),
             pl.BlockSpec((keys, size), lambda h: (0, heads + h)),
+            pl.BlockSpec((keys, size), lambda h: (0, 2 * heads + h)),
             own,
             pl.BlockSpec((rows, keys), lambda h: (0, 0)),
             pl.BlockSpec((rows, 128), lambda h: (0, 0)),
+            anys,
+            anys,
         ],
-        out_specs=[own, seen, seen],
-        out_shape=[
-            jax.ShapeDtypeStruct((rows, width), bf),
-            jax.ShapeDtypeStruct((keys, width), bf),
-            jax.ShapeDtypeStruct((keys, width), bf),
+        out_specs=[own, anys, anys],
+        out_shape=[jax.ShapeDtypeStruct((rows, width), bf)] + near_shapes([grads, stats]),
+        scratch_shapes=near_scratch([grads, stats]),
+        compiler_params=pltpu.CompilerParams(
+            vmem_limit_bytes=48 * 2**20, collective_id=cid, has_side_effects=True
+        ),
+        name="attend_queries",
+    )(near_qkv, near_qkv, near_qkv, grads, bias, lse, grads, stats)
+
+
+def attend_keys_body(scale, q_ref, k_ref, v_ref, g_ref, bias_ref, stats_ref, dk_ref, dv_ref):
+    head = pl.program_id(0)
+    heads = stats_ref.shape[1] // 2
+    row = lax.broadcasted_iota(jnp.int32, stats_ref.shape[1:], 0)
+
+    def line(at):
+        parts = [
+            jnp.sum(jnp.where(row == at, stats_ref[j], 0.0), axis=0, keepdims=True)
+            for j in range(stats_ref.shape[0])
+        ]
+        return jnp.concatenate(parts, axis=1)
+
+    queries, grads = q_ref[...], g_ref[...]
+    probs = jnp.exp(nt(k_ref[...], queries) * scale + bias_ref[...] - line(head))
+    dv_ref[...] = nn(probs.astype(bf), grads).astype(bf)
+    grad_probs = nt(v_ref[...], grads)
+    grad_scores = (probs * (grad_probs - line(heads + head))).astype(bf)
+    dk_ref[...] = (nn(grad_scores, queries) * scale).astype(bf)
+
+
+def attend_keys(near_qkv, near_grads, bias, near_stats, heads, scale):
+    rows, keys = bias.shape
+    width = near_grads.shape[1]
+    size = width // heads
+    middle = keys // rows // 2
+    own = pl.BlockSpec((rows, size), lambda h: (0, h))
+    return pl.pallas_call(
+        functools.partial(attend_keys_body, scale),
+        grid=(heads,),
+        in_specs=[
+            pl.BlockSpec((keys, size), lambda h: (0, h)),
+            pl.BlockSpec((rows, size), lambda h: (middle, heads + h)),
+            pl.BlockSpec((rows, size), lambda h: (middle, 2 * heads + h)),
+            pl.BlockSpec((keys, size), lambda h: (0, h)),
+            pl.BlockSpec((rows, keys), lambda h: (0, 0)),
+            pl.BlockSpec(near_stats.shape, lambda h: (0, 0, 0)),
         ],
+        out_specs=[own, own],
+        out_shape=[jax.ShapeDtypeStruct((rows, width), bf)] * 2,
         compiler_params=pltpu.CompilerParams(vmem_limit_bytes=48 * 2**20),
-        name="attend_back",
-    )(queries, keys_values, keys_values, grads, bias, lse)
-
-
-def chain(z, y, x, core, per_seq):
-    chip = (z * 2 + y) * 2 + x
-    at = lax.rem(chip, per_seq)
-    before, after = at > 0, at < per_seq - 1
-    previous = (chip - jnp.where(before, 1, 0)) * 2 + core
-    following = (chip + jnp.where(after, 1, 0)) * 2 + core
-    return previous, following, before, after
-
-
-def return_body(per_seq, *refs):
-    parts, out = refs[:2], refs[2]
-    far, own, adj, mine, lands, ssem, rsem, lsem = refs[3:]
+        name="attend_keys",
+    )(near_qkv, near_qkv, near_qkv, near_grads, bias, near_stats)
+
+
+def rows_body(own, side, near, beyond, ssem, rsem):
     z, y, x, core = place()
-    c_dev = index_of(z, y, x, 1 - core)
-    previous, following, before, after = chain(z, y, x, core, per_seq)
-    greet([c_dev, previous, following], [None, before, after])
-    rows = own.shape[1]
-    far_slot, plain_slot = 4 * (1 - core), 4 * core
-    adds = jnp.where(core == 0, after, before)
-    gives = jnp.where(core == 0, before, after)
-
-    def to_core(kind, a):
-        slot = jnp.where(kind == 0, 1 + 2 * core, 3 - 2 * core)
-        land = adj.at[a] if kind == 0 else mine.at[a]
-        return remote(parts[a].at[slot], land, ssem.at[kind, a], rsem.at[kind, a], c_dev)
-
-    def plain(kind, a, device, sem):
-        return remote(parts[a].at[plain_slot], lands.at[1 if kind == 2 else 0, a], ssem.at[sem, a], rsem.at[kind, a], device)
-
-    def summed(kind, a, device, sem):
-        return remote(far.at[a], lands.at[1 if kind == 2 else 0, a], ssem.at[sem, a], rsem.at[kind, a], device)
-
-    loads = []
-    for a in range(2):
-        pl.when(gives)(lambda a=a: to_core(0, a).start())
-        to_core(1, a).start()
-        loads.append(pltpu.make_async_copy(parts[a].at[far_slot], far.at[a], lsem.at[0, a]))
-        loads.append(pltpu.make_async_copy(parts[a].at[2], own.at[a], lsem.at[1, a]))
-    for copy in loads:
-        copy.start()
-    for a in range(2):
-        pl.when((core == 0) & before)(lambda a=a: plain(2, a, previous, 2).start())
-        pl.when((core == 1) & after)(lambda a=a: plain(3, a, following, 2).start())
-    for a in range(2):
-        @pl.when(adds)
-        def _(a=a):
-            to_core(0, a).wait_recv()
-        loads[2 * a].wait()
-
-        @pl.when(adds)
-        def _(a=a):
-            add_into(far.at[a], adj.at[a])
-            pl.when(core == 0)(lambda: summed(3, a, following, 3).start())
-            pl.when(core == 1)(lambda: summed(2, a, previous, 3).start())
-
-    width = own.shape[2]
-    for a in range(2):
-        loads[2 * a + 1].wait()
-        to_core(1, a).wait_recv()
-        add_into(own.at[a], mine.at[a])
-    for a in range(2):
-        @pl.when(before)
-        def _(a=a):
-            plain(3, a, previous, 2).wait_recv()
-            add_into(own.at[a], lands.at[0, a])
-
-        @pl.when(after)
-        def _(a=a):
-            plain(2, a, previous, 2).wait_recv()
-            add_into(own.at[a], lands.at[1, a])
-
-        out[:, a * width : (a + 1) * width] = own[a]
-    for a in range(2):
-        pl.when(gives)(lambda a=a: to_core(0, a).wait_send())
-        to_core(1, a).wait_send()
-        pl.when((core == 0) & before)(lambda a=a: plain(2, a, previous, 2).wait_send())
-        pl.when((core == 1) & after)(lambda a=a: plain(3, a, following, 2).wait_send())
-        pl.when((core == 0) & after)(lambda a=a: summed(3, a, following, 3).wait_send())
-        pl.when((core == 1) & before)(lambda a=a: summed(2, a, previous, 3).wait_send())
-
-
-def return_near(parts, per_seq, cid):
-    slots, rows, width = parts[0].shape
+    mid = (z == 1) | (z == 2)
+    y_dev = index_of(z, 1 - y, x, core)
+    near_dev = index_of(z + 1 - 2 * lax.rem(z, 2), y, x, core)
+    beyond_dev = index_of(jnp.where(mid, 3 - z, z), y, x, core)
+    greet([y_dev, near_dev, beyond_dev], [None, None, mid])
+    copies = [
+        (remote(own, target, ssem.at[n], rsem.at[n], device), condition)
+        for n, (target, device, condition) in enumerate(
+            ((beyond, beyond_dev, mid), (side, y_dev, None), (near, near_dev, None))
+        )
+    ]
+    for act in (lambda copy: copy.start(), lambda copy: copy.wait()):
+        for copy, condition in copies:
+            if condition is None:
+                act(copy)
+            else:
+                pl.when(condition)(lambda copy=copy, act=act: act(copy))
+
+
+def rows_around(own, cid):
     anys = pl.BlockSpec(memory_space=pl.ANY)
-    sem = pltpu.SemaphoreType.DMA
-    block = pltpu.VMEM((2, rows, width), bf)
+    sem = pltpu.SemaphoreType.DMA((3,))
     return pl.pallas_call(
-        functools.partial(return_body, per_seq),
-        in_specs=[anys, anys],
-        out_specs=pl.BlockSpec(memory_space=pltpu.VMEM),
-        out_shape=jax.ShapeDtypeStruct((rows, 2 * width), bf),
-        scratch_shapes=[
-            block,
-            block,
-            block,
-            block,
-            pltpu.VMEM((2, 2, rows, width), bf),
-            sem((4, 2)),
-            sem((4, 2)),
-            sem((2, 2)),
-        ],
-        compiler_params=pltpu.CompilerParams(
-            collective_id=cid, has_side_effects=True, vmem_limit_bytes=40 * 2**20
-        ),
-        name="return_near",
-    )(*parts)
+        rows_body,
+        in_specs=[anys],
+        out_specs=[anys] * 3,
+        out_shape=[jax.ShapeDtypeStruct(own.shape, own.dtype)] * 3,
+        scratch_shapes=[sem, sem],
+        compiler_params=pltpu.CompilerParams(collective_id=cid, has_side_effects=True),
+        name="rows_around",
+    )(own)
 
 
 def dense_layer(
@@ -1487,12 +1654,6 @@
     ]
     c_all = lax.all_gather(cot_own, "fsdp", axis_index_groups=planes)
     x_weights = [swapped(w, "fsdp", 1) for w in (gate_own, up_own, down_own)]
-    core_weights = [swapped(w, "fsdp", 0) for w in (gate_own, up_own, down_own)]
-    corner_weights = [swapped(w, "fsdp", 0) for w in x_weights]
-    expert_weights = [
-        list(zip(x_weights, corner_weights)),
-        list(zip((gate_own, up_own, down_own), core_weights)),
-    ]
     router_full = wide_full[:, wide_width : wide_width + experts]
     gain_one = wide_full[:, wide_width + experts]
     gain_two = wide_full[:, wide_width + experts + 1]
@@ -1514,15 +1675,13 @@
         & (jnp.abs(query_places[:, None] - key_places[None, :]) < HALF)
     )
     bias = jnp.where(visible, 0.0, masked)
-    near_values = jnp.where(near_by[:, None], near_tokens.reshape(key_count, model_width).astype(f32), 0.0)
+    near_values = near_tokens.reshape(key_count, model_width).astype(f32)
     near_normed = (near_values * rms_scale(near_values) * attn_gain).astype(bf)
-    own_first = reach_count * tok_rows
-    normed_attn = near_normed[own_first : own_first + tok_rows]
-    queries = jnp.dot(normed_attn, wide_full[:, :model_width], preferred_element_type=f32).astype(bf)
-    keys_values = jnp.dot(
-        near_normed, wide_full[:, model_width:wide_width], preferred_element_type=f32
-    ).astype(bf)
-    context, log_total, own_top = attend(queries, keys_values, bias, head_count, score_scale)
+    normed_attn = (token_values * scale_one * attn_gain).astype(bf)
+    near_qkv = jnp.dot(near_normed, wide_full, preferred_element_type=f32).astype(bf)
+    context, log_total, own_top = attend(near_qkv, bias, head_count, model_width, score_scale)
+    both_left = jnp.stack((normed_attn, context)).reshape(2, tok_rows, devices // 2, 2, weight_rows)
+    by_core = jnp.transpose(both_left, (3, 1, 0, 2, 4)).reshape(2, tok_rows, 2 * model_width // 2)
     attended = token_values + jnp.dot(context, out_full, preferred_element_type=f32)
     scale_two = rms_scale(attended)
     moe_gain = gain_two.astype(f32)
@@ -1532,17 +1691,24 @@
     chosen = jnp.where(named, logits, masked)
     lifted = jnp.where(named, jnp.exp(logits - jnp.max(chosen, axis=1, keepdims=True)), 0.0)
     gate_share = lifted / jnp.sum(lifted, axis=1, keepdims=True)
-    share_rows = jnp.concatenate(
-        (
-            jnp.pad(gate_share, ((0, 0), (0, 128 - experts))),
-            own_top,
-        ),
-        axis=0,
-    )
-    expert_results = expert_pass(normed_moe, share_rows, c_all, expert_weights, experts, 0)
-    s_all, mix_part, grad_from_experts, grad_share = [expert_results[i] for i in (1, 2, 4, 5)]
-    x_terms, own_sum = expert_results[12], expert_results[11]
-    head_max = jnp.max(s_all[:, tok_rows, :head_count], axis=0)
+    lanes = []
+    for values in (gate_share, jnp.broadcast_to(own_top[:1, :head_count], (tok_rows, head_count))):
+        most = lax.reduce_precision(values, 8, 7)
+        lanes += [most.astype(bf), (values - most).astype(bf)]
+    lanes = jnp.concatenate(lanes, axis=1)
+    lane_count = lanes.shape[1]
+    own_rows = jnp.concatenate((normed_moe, jnp.pad(lanes, ((0, 0), (0, 128 - lane_count)))), axis=1)
+    rows_in = [own_rows, *rows_around(own_rows, 4)]
+    x_weights = [lax.optimization_barrier((w, rows_in[1]))[0] for w in x_weights]
+    corner_weights = [swapped(w, "fsdp", 0) for w in x_weights]
+    expert_results = expert_pass(
+        rows_in, c_all, x_weights, corner_weights, (gate_own, up_own, down_own), experts, 0
+    )
+    x_all, mix_part, grad_from_experts, grad_share = [expert_results[i] for i in (0, 1, 3, 4)]
+    x_terms, own_sum = expert_results[11], expert_results[10]
+    first_lane = model_width + 2 * experts
+    tops = x_all[:, 0, first_lane : first_lane + 2 * head_count].astype(f32)
+    head_max = jnp.max(tops[:, :head_count] + tops[:, head_count:], axis=0)
     head_max = jnp.maximum(head_max, swapped(head_max, "fsdp", 0))
     head_max = jnp.maximum(head_max, swapped(head_max, "fsdp", 1))
     factor = clip_limit / jnp.maximum(head_max, clip_limit)
@@ -1560,21 +1726,17 @@
     grad_from_norm, grad_gain_two = norm_back(grad_normed_moe, attended, scale_two, moe_gain)
     grad_attended = grad_mixed + grad_from_norm
     grad_attended_low = grad_attended.astype(bf)
-    grad_out_part = contract(context, grad_attended_low, 0, 0).astype(bf)
-    out_sum = lax.psum_scatter(grad_out_part, "fsdp", scatter_dimension=0, tiled=True)
     grad_context = contract(grad_attended_low, out_full, 1, 1).astype(bf)
-    grad_queries, near_keys, near_values_grad = attend_back(
-        queries, keys_values, grad_context, bias, log_total, head_count, score_scale
-    )
-    near_shape = (slots, tok_rows, model_width)
-    grad_kv_low = return_near(
-        [near_keys.reshape(near_shape), near_values_grad.reshape(near_shape)], per_seq, 1
-    )
-    grad_kv_low, own_sum, x_terms = lax.optimization_barrier((grad_kv_low, own_sum, x_terms))
-    expert_grads = own_sum.astype(f32) + x_terms.astype(f32)
-    grad_gate, grad_up, grad_down = expert_grads[0], expert_grads[1], expert_grads[2]
-    grad_qkv = jnp.concatenate((grad_queries, grad_kv_low), axis=1)
-    grad_qkv_part = contract(normed_attn, grad_qkv, 0, 0).astype(bf)
+    by_head = grad_context.astype(f32) * context.astype(f32)
+    shifts = jnp.sum(by_head.reshape(tok_rows, head_count, head_size), axis=2)
+    stats = jnp.transpose(jnp.concatenate((log_total[:, :head_count], shifts), axis=1))
+    grad_queries, near_grads, near_stats = attend_queries(
+        near_qkv, grad_context, bias, log_total, stats, head_count, score_scale, per_seq, 1
+    )
+    grad_keys, grad_values = attend_keys(
+        near_qkv, near_grads.reshape(key_count, model_width), bias, near_stats, head_count, score_scale
+    )
+    grad_qkv = jnp.concatenate((grad_queries, grad_keys, grad_values), axis=1)
     grad_normed_attn = contract(jnp.pad(grad_qkv, ((0, 0), (0, 128))), wide_full, 1, 1)
     grad_from_first, grad_gain_one = norm_back(grad_normed_attn, token_values, scale_one, attn_gain)
     grad_tokens = grad_attended + grad_from_first
@@ -1583,22 +1745,21 @@
         ((0, 0), (0, 128 - experts - 2)),
     )
     owners = (devices // 2, 2, weight_rows)
-    qkv_sum, extra_sum = full_reduce(
-        [
-            grad_qkv_part.reshape(owners + (wide_width,)),
-            extra_part.reshape(owners + (128,)),
-        ],
-        3,
-    )
-    mixture, out_sum, qkv_sum = lax.optimization_barrier((mixture, out_sum, qkv_sum))
+    grads_sum, extra_sum = full_reduce(
+        by_core, grad_qkv, grad_attended_low, extra_part.reshape(owners + (128,)), 3
+    )
+    mixture, own_sum, x_terms, grads_sum = lax.optimization_barrier(
+        (mixture, own_sum, x_terms, grads_sum)
+    )
+    grad_gate, grad_up, grad_down = [own_sum[i].astype(f32) + x_terms[i].astype(f32) for i in range(3)]
     mixed = (attended + mixture.astype(f32)).astype(bf)
     return (
         mixed,
         grad_tokens,
-        qkv_sum[:, :model_width],
-        qkv_sum[:, model_width : 2 * model_width],
-        qkv_sum[:, 2 * model_width :],
-        out_sum.astype(f32),
+        grads_sum[:, :model_width],
+        grads_sum[:, model_width : 2 * model_width],
+        grads_sum[:, 2 * model_width : wide_width],
+        grads_sum[:, wide_width:],
         extra_sum[:, :experts],
         extra_sum[:, experts],
         extra_sum[:, experts + 1],

time: 1130 us -> 965 us (0.85)
  Pallas kernels: 881 us -> 795 us
  waiting for transfers between devices: 66.8 us -> 12 us
  matrix products: 83.8 us -> 69.4 us
    ppermute x11 -> x8, waiting for transfers between devices: 66.1 us -> 11.9 us  [swapped(): return lax.ppermute(block, axis, route)]
    pallas_call x1, Pallas kernels: 314 us -> 267 us  [expert_pass(): pl.pallas_call(functools.partial(expert_body, shard, width, half, block,...]
    pallas_call x3 -> x4, Pallas kernels: 356 us -> 319 us  [the longest x1 188 us: full_reduce(): pl.pallas_call(body, in_specs=[anys] * 4, out_specs=[pl.BlockSpec(memory_...]
    dot_general x4 -> x2, matrix products: 39.2 us -> 20.5 us  [contract(): lax.dot_general(left, right, (((left_dim,), (right_dim,)), ((), ())), pre...]
    dot_general x2 -> x1, matrix products: 34.8 us -> 39.6 us  [dense_layer(): jnp.dot(near_normed, wide_full, preferred_element_type=f32).astype(bf)]
  transfers between devices with their start and end apart: 14 -> 10, of which waited for: 4 -> 4; matrix products, arithmetic and copies ran while one was open for 11% -> 12% of each run, Pallas kernels for 34% -> 35%
where the time goes in v3:
time: 965 us; the launch traced here: 959 us
  Pallas kernels  795 us (82%)
  matrix products  69.4 us (7%)
  other arithmetic  37.9 us (4%)
  local copies, waits for them, and re-layouts  23.3 us (2%)
  between operations  17.5 us (2%)
  waiting for transfers between devices  12 us (1%)
    pallas_call x1, Pallas kernels, expert_pass(): pl.pallas_call(functools.partial(expert_body, shard, width, half, block,...  267 us
    pallas_call x1, Pallas kernels, full_gather(): pl.pallas_call(body, in_specs=[anys] * (count + 1), out_specs=[anys] * (c...  190 us
    pallas_call x1, Pallas kernels, full_reduce(): pl.pallas_call(body, in_specs=[anys] * 4, out_specs=[pl.BlockSpec(memory_...  188 us
    pallas_call x1, Pallas kernels, rows_around(): pl.pallas_call(rows_body, in_specs=[anys], out_specs=[anys] * 3, out_shap...  59.7 us
    pallas_call x1, Pallas kernels, attend_queries(): pl.pallas_call(functools.partial(attend_queries_body, scale, per_seq, hea...  53 us
    dot_general x1, matrix products, dense_layer(): jnp.dot(near_normed, wide_full, preferred_element_type=f32).astype(bf)  39.6 us
    dot_general x2, matrix products, contract(): lax.dot_general(left, right, (((left_dim,), (right_dim,)), ((), ())), pre...  20.5 us
  transfers between devices with their start and end apart: 10, of which 4 were waited for; matrix products, arithmetic and copies ran while one was open for 12% of the time, Pallas kernels for 35%

profile of v3, /device:TPU:16, one launch (start us, length us, event | category | flops | bytes accessed | tf_op | source)
XLA Modules:
  0.0 958.7 jit_solution(6261574174198635517)
XLA Ops:
  10.1 190.4 %full_gather.1 = (bf16[32,64,6272]{2,1,0:T(8,128)(2,1)}, bf16[32,64,2048]{2,1,0:T(8,128)(2,1)}, bf16[5,256,2048]{2,1,0:T(8,128)(2,1)}) custom-call(bf16[64,6272]{1,0:T(8,128)(2,1)} %fusion.25.refs_0_, bf16[64,2048]{1,0:T(8,128)(2,1)} %refs_1_.1, bf16[256,2048]{1,0:T(8,128)(2,1)} %refs_2_.1), custom_call_target="tpu_custom_call" | custom-call | tf_op jit(solution)/shard_map/full_gather/pallas_call | solution.py:638
  209.5 4.0 fusion
  214.6 4.3 fusion.2
  218.9 39.6 %convolution_convert_fusion.q_ref.k_ref.v_ref.refs_0_.refs_1_.refs_2_ = bf16[1280,6272]{1,0:T(8,128)(2,1)} fusion(bf16[1280,2048]{1,0:T(8,128)(2,1)S(1)} %bitcast.62, bf16[2048,6272]{1,0:T(8,128)(2,1)} %bitcast.68), kind=kOutput, calls=%fused_computation | convolution fusion | flops 32891371520 | bytes 46989312 | tf_op jit(solution)/shard_map/dot_general | solution.py:1681
  258.5 19.3 %attend.1 = (bf16[256,2048]{1,0:T(8,128)(2,1)S(1)}, f32[256,128]{1,0:T(8,128)S(1)}, f32[8,128]{1,0:T(8,128)S(1)}) custom-call(bf16[1280,6272]{1,0:T(8,128)(2,1)} %convolution_convert_fusion.q_ref.k_ref.v_ref.refs_0_.refs_1_.refs_2_, bf16[1280,6272]{1,0:T(8,128)(2,1)} %convolution_convert_fusion.q_ref.k_ref.v_ref.refs_0_.refs_1_.refs_2_, ...), custom_call_target="tpu_custom_call" | custom-call | tf_op jit(solution)/shard_map/attend/pallas_call | solution.py:1456
  277.8 2.5 multiply_reduce_fusion.2
  284.0 2.3 fusion.21.own.refs_0_
  286.3 59.7 %rows_around.1 = (bf16[256,2176]{1,0:T(8,128)(2,1)}, bf16[256,2176]{1,0:T(8,128)(2,1)}, bf16[256,2176]{1,0:T(8,128)(2,1)}) custom-call(bf16[256,2176]{1,0:T(8,128)(2,1)} %fusion.21.own.refs_0_), custom_call_target="tpu_custom_call" | custom-call | tf_op jit(solution)/shard_map/rows_around/pallas_call | solution.py:1602
  346.7 3.9 collective-permute-done.5.refs_10_
  350.6 3.0 collective-permute-done.4.refs_9_
  353.6 3.0 collective-permute-done.3.refs_8_
  356.6 266.9 %expert_pass.1 = (bf16[8,256,2176]{2,1,0:T(8,128)(2,1)}, bf16[2048,2048]{1,0:T(8,128)(2,1)}, bf16[2048,2048]{1,0:T(8,128)(2,1)}, bf16[256,2048]{1,0:T(8,128)(2,1...) custom-call(bf16[256,2176]{1,0:T(8,128)(2,1)} %fusion.21.own.refs_0_, ...), custom_call_target="tpu_custom_call" | custom-call | tf_op jit(solution)/shard_map/expert_pass/pallas_call | solution.py:1389
  627.7 3.8 multiply_reduce_fusion
  633.7 6.1 convolution_convert_fusion.1.refs_3_.refs_6_
  641.9 2.3 reduce_sum.116
  644.3 53.0 %attend_queries.1 = (bf16[256,2048]{1,0:T(8,128)(2,1)S(1)}, bf16[5,256,2048]{2,1,0:T(8,128)(2,1)}, f32[5,32,256]{2,1,0:T(8,128)S(1)}) custom-call(bf16[1280,6272]{1,0:T(8,128)(2,1)} %convolution_convert_fusion.q_ref.k_ref.v_ref.refs_0_.refs_1_.refs_2_, bf16[1280,6272]{1,0:T(8,128)(2,1)} %convolution_convert_fusion.q_ref.k_ref.v_ref.refs_0_.refs_1_.refs_2_, ...), custom_call_target="tpu_custom_call" | custom-call | tf_op jit(solution)/shard_map/attend_queries/pallas_call | solution.py:1511
  697.3 18.0 %attend_keys.1 = (bf16[256,2048]{1,0:T(8,128)(2,1)S(1)}, bf16[256,2048]{1,0:T(8,128)(2,1)S(1)}) custom-call(bf16[1280,6272]{1,0:T(8,128)(2,1)} %convolution_convert_fusion.q_ref.k_ref.v_ref.refs_0_.refs_1_.refs_2_, bf16[1280,6272]{1,0:T(8,128)(2,1)} %convolution_convert_fusion.q_ref.k_ref.v_ref.refs_0_.refs_1_.refs_2_, ...), custom_call_target="tpu_custom_call" | custom-call | tf_op jit(solution)/shard_map/attend_keys/pallas_call | solution.py:1560
  718.0 14.4 %fusion.13 = (f32[256]{0:T(256)S(1)}, f32[2048]{0:T(1024)S(1)}, f32[256,2048]{1,0:T(8,128)}) fusion(bf16[256,2048]{1,0:T(8,128)(2,1)S(1)} %copy-done.11, f32[2048]{0:T(1024)S(1)} %bitcast.76, f32[256]{0:T(256)S(1)} %add_rsqrt_fusion.1, bf16[2048,6272]{1,0:T(8,128)(2,1)} %bitcast.71, bf16[256,6144]{1,0:T(8,128)(2,1)} %copy-done.13), kind=kOutput, calls=%fused_computation.25 | convolution fusion | flops 6580336640 | bytes 32000000 | tf_op jit(solution)/shard_map/dot_general | solution.py:65
  733.8 2.3 pad.19.clone
  736.1 4.0 fusion.16
  742.0 2.4 copy.83.refs_0_
  744.3 188.0 %full_reduce.1 = (f32[64,8192]{1,0:T(8,128)}, f32[64,128]{1,0:T(8,128)}) custom-call(bf16[2,256,2048]{2,1,0:T(8,128)(2,1)} %copy.83.refs_0_, bf16[256,6144]{1,0:T(8,128)(2,1)} %copy-done.13, bf16[256,2048]{1,0:T(8,128)(2,1)} %copy-done.14, f32[16,2,64,128]{3,2,1,0:T(8,128)} %bitcast.63), custom_call_target="tpu_custom_call" | custom-call | tf_op jit(solution)/shard_map/full_reduce/pallas_call | solution.py:819
  938.4 3.0 fusion.55
  942.7 9.0 add_bitcast_fusion
  (145 shorter events, 36.2 us)
Async XLA Ops:
  7.2 349.4 %all-gather.3.cloned.1.call-start = ((), (), s32[]{:S(2)}) async-start(), calls=%async_computation.2 | async-start | bytes 9437184 | tf_op jit(solution)/shard_map/all_gather | solution.py:1655
  8.1 198.4 %copy-start.26 = (s32[2,4]{1,0:T(2,128)S(1)}, s32[2,4]{1,0:T(2,128)}, u32[]{:S(2)}) copy-start(s32[2,4]{1,0:T(2,128)} %param.27) | copy-start | bytes 100
  200.6 145.4 %collective-permute-start.2 = (bf16[512,2048]{1,0:T(8,128)(2,1)}, bf16[512,2048]{1,0:T(8,128)(2,1)}, u32[]{:S(2)}, u32[]{:S(2)}) collective-permute-start(bf16[512,2048]{1,0:T(8,128)(2,1)} %refs_13_), channel_id=1, source_target_pairs={{0,2},{2,0},{1,3},{3,1},{4,6},{6,4},{5,7},{7,5},{8,10},{10,8},{9,1... | collective-permute-start | bytes 6291464 | tf_op jit(solution)/shard_map/ppermute | solution.py:32
  201.2 144.9 %collective-permute-start.1 = (bf16[512,2048]{1,0:T(8,128)(2,1)}, bf16[512,2048]{1,0:T(8,128)(2,1)}, u32[]{:S(2)}, u32[]{:S(2)}) collective-permute-start(bf16[512,2048]{1,0:T(8,128)(2,1)} %refs_12_), channel_id=1, source_target_pairs={{0,2},{2,0},{1,3},{3,1},{4,6},{6,4},{5,7},{7,5},{8,10},{10,8},{9,1... | collective-permute-start | bytes 6291464 | tf_op jit(solution)/shard_map/ppermute | solution.py:32
  202.7 143.9 %collective-permute-start = (bf16[512,2048]{1,0:T(8,128)(2,1)}, bf16[512,2048]{1,0:T(8,128)(2,1)}, u32[]{:S(2)}, u32[]{:S(2)}) collective-permute-start(bf16[512,2048]{1,0:T(8,128)(2,1)} %refs_11_), channel_id=1, source_target_pairs={{0,2},{2,0},{1,3},{3,1},{4,6},{6,4},{5,7},{7,5},{8,10},{10,8},{9,1... | collective-permute-start | bytes 6291464 | tf_op jit(solution)/shard_map/ppermute | solution.py:32
  203.2 735.2 %reduce-scatter.2.cloned.1.call-start = ((), (), s32[]{:S(2)}) async-start(), calls=%async_computation.1 | async-start | bytes 9437184 | tf_op jit(solution)/shard_map/reduce_scatter | solution.py:1718
  209.5 5.1 copy-start.22
  209.5 4.3 copy-start.25
  214.6 43.9 %copy-start = (f32[256,1280]{1,0:T(8,128)}, f32[256,1280]{1,0:T(8,128)S(1)}, u32[]{:S(2)}) copy-start(f32[256,1280]{1,0:T(8,128)S(1)} %fusion.20.bias_ref.refs_4_) | copy-start | bytes 3932164
  214.6 63.1 %slice-start.1 = ((s8[8388608]{0:T(1024)(128)(4,1)}), s8[4194304]{0:T(1024)(128)(4,1)S(1)}, s32[]{:S(2)}) async-start(s8[8388608]{0:T(1024)(128)(4,1)} %bitcast.84), calls=%async_computation.4 | async-start | bytes 8388608
  218.9 58.9 %slice-start.2 = ((s8[8388608]{0:T(1024)(128)(4,1)}), s8[4194304]{0:T(1024)(128)(4,1)S(1)}, s32[]{:S(2)}) async-start(s8[8388608]{0:T(1024)(128)(4,1)} %bitcast.84), calls=%async_computation.5 | async-start | bytes 8388608
  258.5 19.3 %copy-start.9 = (bf16[256,2048]{1,0:T(8,128)(2,1)S(1)}, bf16[256,2048]{1,0:T(8,128)(2,1)}, u32[]{:S(2)}) copy-start(bf16[256,2048]{1,0:T(8,128)(2,1)} %refs_2_.1) | copy-start | bytes 3145732
  346.0 4.6 collective-permute-start.5
  346.1 7.5 collective-permute-start.4
  346.6 10.0 %collective-permute-start.3 = (bf16[512,2048]{1,0:T(8,128)(2,1)}, bf16[512,2048]{1,0:T(8,128)(2,1)}, u32[]{:S(2)}, u32[]{:S(2)}) collective-permute-start(bf16[512,2048]{1,0:T(8,128)(2,1)} %collective-permute-done.refs_5_), channel_id=1, source_target_pairs={{0,1},{1,0},{2,3},{3,2},{4,5},{5,4},{6,7},{7,6},{8,9},{9,8},{10,11... | collective-permute-start | bytes 6291464 | tf_op jit(solution)/shard_map/ppermute | solution.py:32
  626.2 5.3 copy-start.21
  627.4 306.4 %collective-permute-start.6 = (f32[16]{0:T(128)S(1)}, f32[16]{0:T(128)S(1)}, u32[]{:S(2)}, u32[]{:S(2)}) collective-permute-start(f32[16]{0:T(128)S(1)} %add_reduce_fusion), channel_id=1, source_target_pairs={{0,1},{1,0},{2,3},{3,2},{4,5},{5,4},{6,7},{7,6},{8,9},{9,8},{10,11... | collective-permute-start | bytes 200 | tf_op jit(solution)/shard_map/ppermute | solution.py:32
  627.7 3.9 copy-start.5
  627.7 3.9 copy-start.15
  633.7 6.1 copy-start.14
  744.3 193.1 %copy-start.27 = (f32[16]{0:T(128)S(1)}, f32[16]{0:T(128)}, u32[]{:S(2)}) copy-start(f32[16]{0:T(128)} %param.28) | copy-start | bytes 196
  744.3 193.2 %copy-start.18 = (bf16[64,2048]{1,0:T(8,128)(2,1)S(1)}, bf16[64,2048]{1,0:T(8,128)(2,1)}, u32[]{:S(2)}) copy-start(bf16[64,2048]{1,0:T(8,128)(2,1)} %param.17) | copy-start | bytes 786436
  744.3 193.2 %copy-start.19 = (bf16[64,2048]{1,0:T(8,128)(2,1)S(1)}, bf16[64,2048]{1,0:T(8,128)(2,1)}, u32[]{:S(2)}) copy-start(bf16[64,2048]{1,0:T(8,128)(2,1)} %param.16) | copy-start | bytes 786436
  933.9 3.5 collective-permute-start.7
  (17 other events, 40.6 us)
Sparse Core Ops, SparseCore 0:
  203.3 145.8 all-gather.2
  623.6 171.5 reduce-scatter.1

commit v4 on v3

--- a/solution.py
+++ b/solution.py
@@ -1531,7 +1531,11 @@
     )(near_qkv, near_qkv, near_qkv, grads, bias, lse, grads, stats)
 
 
-def attend_keys_body(scale, q_ref, k_ref, v_ref, g_ref, bias_ref, stats_ref, dk_ref, dv_ref):
+def attend_keys_body(
+    scale, q_ref, k_ref, v_ref, g_ref, bias_ref, stats_ref, sums_ref, terms_ref, dk_ref, dv_ref, *total_refs
+):
+    for n, total_ref in enumerate(total_refs):
+        total_ref[...] = sums_ref[n].astype(f32) + terms_ref[n].astype(f32)
     head = pl.program_id(0)
     heads = stats_ref.shape[1] // 2
     row = lax.broadcasted_iota(jnp.int32, stats_ref.shape[1:], 0)
@@ -1551,7 +1555,11 @@
     dk_ref[...] = (nn(grad_scores, queries) * scale).astype(bf)
 
 
-def attend_keys(near_qkv, near_grads, bias, near_stats, heads, scale):
+def attend_keys(near_qkv, near_grads, bias, near_stats, sums, terms, heads, scale):
+    count, units = sums.shape[:2]
+    slice_rows = units // heads
+    part = pl.BlockSpec((count, slice_rows, sums.shape[2]), lambda h: (0, h, 0))
+    total = pl.BlockSpec((slice_rows, sums.shape[2]), lambda h: (h, 0))
     rows, keys = bias.shape
     width = near_grads.shape[1]
     size = width // heads
@@ -1567,12 +1575,15 @@
             pl.BlockSpec((keys, size), lambda h: (0, h)),
             pl.BlockSpec((rows, keys), lambda h: (0, 0)),
             pl.BlockSpec(near_stats.shape, lambda h: (0, 0, 0)),
+            part,
+            part,
         ],
-        out_specs=[own, own],
-        out_shape=[jax.ShapeDtypeStruct((rows, width), bf)] * 2,
+        out_specs=[own, own] + [total] * count,
+        out_shape=[jax.ShapeDtypeStruct((rows, width), bf)] * 2
+        + [jax.ShapeDtypeStruct(sums.shape[1:], f32)] * count,
         compiler_params=pltpu.CompilerParams(vmem_limit_bytes=48 * 2**20),
         name="attend_keys",
-    )(near_qkv, near_qkv, near_qkv, near_grads, bias, near_stats)
+    )(near_qkv, near_qkv, near_qkv, near_grads, bias, near_stats, sums, terms)
 
 
 def rows_body(own, side, near, beyond, ssem, rsem):
@@ -1733,8 +1744,15 @@
     grad_queries, near_grads, near_stats = attend_queries(
         near_qkv, grad_context, bias, log_total, stats, head_count, score_scale, per_seq, 1
     )
-    grad_keys, grad_values = attend_keys(
-        near_qkv, near_grads.reshape(key_count, model_width), bias, near_stats, head_count, score_scale
+    grad_keys, grad_values, grad_gate, grad_up, grad_down = attend_keys(
+        near_qkv,
+        near_grads.reshape(key_count, model_width),
+        bias,
+        near_stats,
+        own_sum,
+        x_terms,
+        head_count,
+        score_scale,
     )
     grad_qkv = jnp.concatenate((grad_queries, grad_keys, grad_values), axis=1)
     grad_normed_attn = contract(jnp.pad(grad_qkv, ((0, 0), (0, 128))), wide_full, 1, 1)
@@ -1748,10 +1766,7 @@
     grads_sum, extra_sum = full_reduce(
         by_core, grad_qkv, grad_attended_low, extra_part.reshape(owners + (128,)), 3
     )
-    mixture, own_sum, x_terms, grads_sum = lax.optimization_barrier(
-        (mixture, own_sum, x_terms, grads_sum)
-    )
-    grad_gate, grad_up, grad_down = [own_sum[i].astype(f32) + x_terms[i].astype(f32) for i in range(3)]
+    mixture, grads_sum = lax.optimization_barrier((mixture, grads_sum))
     mixed = (attended + mixture.astype(f32)).astype(bf)
     return (
         mixed,

time: 965 us -> 964 us (level)
  transfers between devices with their start and end apart: 10 -> 10, of which waited for: 4 -> 4; matrix products, arithmetic and copies ran while one was open for 12% -> 12% of each run, Pallas kernels for 35% -> 36%
where the time goes in v4:
time: 964 us; the launch traced here: 957 us
  Pallas kernels  801 us (83%)
  matrix products  71.3 us (7%)
  other arithmetic  30.1 us (3%)
  local copies, waits for them, and re-layouts  22.2 us (2%)
  between operations  17.5 us (2%)
  waiting for transfers between devices  11.7 us (1%)
    pallas_call x1, Pallas kernels, expert_pass(): pl.pallas_call(functools.partial(expert_body, shard, width, half, block,...  267 us
    pallas_call x1, Pallas kernels, full_gather(): pl.pallas_call(body, in_specs=[anys] * (count + 1), out_specs=[anys] * (c...  190 us
    pallas_call x1, Pallas kernels, full_reduce(): pl.pallas_call(body, in_specs=[anys] * 4, out_specs=[pl.BlockSpec(memory_...  188 us
    pallas_call x1, Pallas kernels, rows_around(): pl.pallas_call(rows_body, in_specs=[anys], out_specs=[anys] * 3, out_shap...  59.6 us
    pallas_call x1, Pallas kernels, attend_queries(): pl.pallas_call(functools.partial(attend_queries_body, scale, per_seq, hea...  52.9 us
    dot_general x1, matrix products, dense_layer(): jnp.dot(near_normed, wide_full, preferred_element_type=f32).astype(bf)  39.5 us
    pallas_call x1, Pallas kernels, attend_keys(): pl.pallas_call(functools.partial(attend_keys_body, scale), grid=(heads,),...  23.9 us
    dot_general x2, matrix products, contract(): lax.dot_general(left, right, (((left_dim,), (right_dim,)), ((), ())), pre...  20.8 us
  transfers between devices with their start and end apart: 10, of which 4 were waited for; matrix products, arithmetic and copies ran while one was open for 12% of the time, Pallas kernels for 36%

profile of v4, /device:TPU:16, one launch (start us, length us, event | category | flops | bytes accessed | tf_op | source)
XLA Modules:
  0.0 957.1 jit_solution(10095456100844824733)
XLA Ops:
  10.1 190.4 %full_gather.1 = (bf16[32,64,6272]{2,1,0:T(8,128)(2,1)}, bf16[32,64,2048]{2,1,0:T(8,128)(2,1)}, bf16[5,256,2048]{2,1,0:T(8,128)(2,1)}) custom-call(bf16[64,6272]{1,0:T(8,128)(2,1)} %fusion.25.refs_0_, bf16[64,2048]{1,0:T(8,128)(2,1)} %refs_1_.1, bf16[256,2048]{1,0:T(8,128)(2,1)} %refs_2_.1), custom_call_target="tpu_custom_call" | custom-call | tf_op jit(solution)/shard_map/full_gather/pallas_call | solution.py:638
  209.6 4.0 fusion
  214.7 4.2 fusion.2
  218.9 39.5 %convolution_convert_fusion.q_ref.k_ref.v_ref.refs_0_.refs_1_.refs_2_ = bf16[1280,6272]{1,0:T(8,128)(2,1)} fusion(bf16[1280,2048]{1,0:T(8,128)(2,1)S(1)} %bitcast.56, bf16[2048,6272]{1,0:T(8,128)(2,1)} %bitcast.62), kind=kOutput, calls=%fused_computation | convolution fusion | flops 32891371520 | bytes 46989312 | tf_op jit(solution)/shard_map/dot_general | solution.py:1692
  258.5 18.6 %attend.1 = (bf16[256,2048]{1,0:T(8,128)(2,1)S(1)}, f32[256,128]{1,0:T(8,128)S(1)}, f32[8,128]{1,0:T(8,128)S(1)}) custom-call(bf16[1280,6272]{1,0:T(8,128)(2,1)} %convolution_convert_fusion.q_ref.k_ref.v_ref.refs_0_.refs_1_.refs_2_, bf16[1280,6272]{1,0:T(8,128)(2,1)} %convolution_convert_fusion.q_ref.k_ref.v_ref.refs_0_.refs_1_.refs_2_, ...), custom_call_target="tpu_custom_call" | custom-call | tf_op jit(solution)/shard_map/attend/pallas_call | solution.py:1456
  277.1 2.5 multiply_reduce_fusion.2
  283.6 2.3 fusion.21.own.refs_0_
  285.9 59.6 %rows_around.1 = (bf16[256,2176]{1,0:T(8,128)(2,1)}, bf16[256,2176]{1,0:T(8,128)(2,1)}, bf16[256,2176]{1,0:T(8,128)(2,1)}) custom-call(bf16[256,2176]{1,0:T(8,128)(2,1)} %fusion.21.own.refs_0_), custom_call_target="tpu_custom_call" | custom-call | tf_op jit(solution)/shard_map/rows_around/pallas_call | solution.py:1613
  346.2 3.9 collective-permute-done.5.refs_10_
  350.1 3.0 collective-permute-done.4.refs_9_
  353.1 3.0 collective-permute-done.3.refs_8_
  356.1 266.9 %expert_pass.1 = (bf16[8,256,2176]{2,1,0:T(8,128)(2,1)}, bf16[2048,2048]{1,0:T(8,128)(2,1)}, bf16[2048,2048]{1,0:T(8,128)(2,1)}, bf16[256,2048]{1,0:T(8,128)(2,1...) custom-call(bf16[256,2176]{1,0:T(8,128)(2,1)} %fusion.21.own.refs_0_, ...), custom_call_target="tpu_custom_call" | custom-call | tf_op jit(solution)/shard_map/expert_pass/pallas_call | solution.py:1389
  627.3 3.8 multiply_reduce_fusion
  631.2 2.1 fusion.53
  633.3 6.1 convolution_convert_fusion.1.refs_3_.refs_6_
  641.5 2.3 reduce_sum.116
  643.9 52.9 %attend_queries.1 = (bf16[256,2048]{1,0:T(8,128)(2,1)S(1)}, bf16[5,256,2048]{2,1,0:T(8,128)(2,1)}, f32[5,32,256]{2,1,0:T(8,128)S(1)}) custom-call(bf16[1280,6272]{1,0:T(8,128)(2,1)} %convolution_convert_fusion.q_ref.k_ref.v_ref.refs_0_.refs_1_.refs_2_, bf16[1280,6272]{1,0:T(8,128)(2,1)} %convolution_convert_fusion.q_ref.k_ref.v_ref.refs_0_.refs_1_.refs_2_, ...), custom_call_target="tpu_custom_call" | custom-call | tf_op jit(solution)/shard_map/attend_queries/pallas_call | solution.py:1511
  696.9 23.9 %attend_keys.1 = (bf16[256,2048]{1,0:T(8,128)(2,1)S(1)}, bf16[256,2048]{1,0:T(8,128)(2,1)S(1)}, f32[512,2048]{1,0:T(8,128)}, f32[512,2048]{1,0:T(8,128)}, f32[512,2048]{1,0:T(8,128)}) custom-call(bf16[1280,6272]{1,0:T(8,128)(2,1)} %convolution_convert_fusion.q_ref.k_ref.v_ref.refs_0_.refs_1_.refs_2_, ...), custom_call_target="tpu_custom_call" | custom-call | tf_op jit(solution)/shard_map/attend_keys/pallas_call | solution.py:1568
  724.7 14.7 %fusion.13 = (f32[256]{0:T(256)S(1)}, f32[2048]{0:T(1024)S(1)}, f32[256,2048]{1,0:T(8,128)}) fusion(bf16[256,2048]{1,0:T(8,128)(2,1)S(1)} %copy-done.9, f32[2048]{0:T(1024)S(1)} %bitcast.70, f32[256]{0:T(256)S(1)} %add_rsqrt_fusion.1, bf16[2048,6272]{1,0:T(8,128)(2,1)} %bitcast.65, bf16[256,6144]{1,0:T(8,128)(2,1)} %copy-done.11), kind=kOutput, calls=%fused_computation.22 | convolution fusion | flops 6580336640 | bytes 32000000 | tf_op jit(solution)/shard_map/dot_general | solution.py:65
  740.7 2.3 pad.19.clone
  743.0 4.0 fusion.16
  748.9 2.5 copy.83.refs_0_
  751.4 188.2 %full_reduce.1 = (f32[64,8192]{1,0:T(8,128)}, f32[64,128]{1,0:T(8,128)}) custom-call(bf16[2,256,2048]{2,1,0:T(8,128)(2,1)} %copy.83.refs_0_, bf16[256,6144]{1,0:T(8,128)(2,1)} %copy-done.11, bf16[256,2048]{1,0:T(8,128)(2,1)} %copy-done.12, f32[16,2,64,128]{3,2,1,0:T(8,128)} %bitcast.57), custom_call_target="tpu_custom_call" | custom-call | tf_op jit(solution)/shard_map/full_reduce/pallas_call | solution.py:819
  945.7 3.0 fusion.55
  (140 shorter events, 35.7 us)
Async XLA Ops:
  7.2 348.9 %all-gather.3.cloned.1.call-start = ((), (), s32[]{:S(2)}) async-start(), calls=%async_computation.2 | async-start | bytes 9437184 | tf_op jit(solution)/shard_map/all_gather | solution.py:1666
  8.1 198.4 %copy-start.24 = (s32[2,4]{1,0:T(2,128)S(1)}, s32[2,4]{1,0:T(2,128)}, u32[]{:S(2)}) copy-start(s32[2,4]{1,0:T(2,128)} %param.27) | copy-start | bytes 100
  200.6 144.9 %collective-permute-start.2 = (bf16[512,2048]{1,0:T(8,128)(2,1)}, bf16[512,2048]{1,0:T(8,128)(2,1)}, u32[]{:S(2)}, u32[]{:S(2)}) collective-permute-start(bf16[512,2048]{1,0:T(8,128)(2,1)} %refs_13_), channel_id=1, source_target_pairs={{0,2},{2,0},{1,3},{3,1},{4,6},{6,4},{5,7},{7,5},{8,10},{10,8},{9,1... | collective-permute-start | bytes 6291464 | tf_op jit(solution)/shard_map/ppermute | solution.py:32
  201.2 144.5 %collective-permute-start.1 = (bf16[512,2048]{1,0:T(8,128)(2,1)}, bf16[512,2048]{1,0:T(8,128)(2,1)}, u32[]{:S(2)}, u32[]{:S(2)}) collective-permute-start(bf16[512,2048]{1,0:T(8,128)(2,1)} %refs_12_), channel_id=1, source_target_pairs={{0,2},{2,0},{1,3},{3,1},{4,6},{6,4},{5,7},{7,5},{8,10},{10,8},{9,1... | collective-permute-start | bytes 6291464 | tf_op jit(solution)/shard_map/ppermute | solution.py:32
  202.7 143.4 %collective-permute-start = (bf16[512,2048]{1,0:T(8,128)(2,1)}, bf16[512,2048]{1,0:T(8,128)(2,1)}, u32[]{:S(2)}, u32[]{:S(2)}) collective-permute-start(bf16[512,2048]{1,0:T(8,128)(2,1)} %refs_11_), channel_id=1, source_target_pairs={{0,2},{2,0},{1,3},{3,1},{4,6},{6,4},{5,7},{7,5},{8,10},{10,8},{9,1... | collective-permute-start | bytes 6291464 | tf_op jit(solution)/shard_map/ppermute | solution.py:32
  203.2 742.5 %reduce-scatter.2.cloned.1.call-start = ((), (), s32[]{:S(2)}) async-start(), calls=%async_computation.1 | async-start | bytes 9437184 | tf_op jit(solution)/shard_map/reduce_scatter | solution.py:1729
  209.6 5.1 copy-start.20
  209.6 4.3 copy-start.23
  214.6 43.8 %copy-start = (f32[256,1280]{1,0:T(8,128)}, f32[256,1280]{1,0:T(8,128)S(1)}, u32[]{:S(2)}) copy-start(f32[256,1280]{1,0:T(8,128)S(1)} %fusion.20.bias_ref.refs_4_) | copy-start | bytes 3932164
  214.7 62.4 %slice-start.1 = ((s8[8388608]{0:T(1024)(128)(4,1)}), s8[4194304]{0:T(1024)(128)(4,1)S(1)}, s32[]{:S(2)}) async-start(s8[8388608]{0:T(1024)(128)(4,1)} %bitcast.78), calls=%async_computation.4 | async-start | bytes 8388608
  218.9 58.2 %slice-start.2 = ((s8[8388608]{0:T(1024)(128)(4,1)}), s8[4194304]{0:T(1024)(128)(4,1)S(1)}, s32[]{:S(2)}) async-start(s8[8388608]{0:T(1024)(128)(4,1)} %bitcast.78), calls=%async_computation.5 | async-start | bytes 8388608
  258.5 18.7 %copy-start.7 = (bf16[256,2048]{1,0:T(8,128)(2,1)S(1)}, bf16[256,2048]{1,0:T(8,128)(2,1)}, u32[]{:S(2)}) copy-start(bf16[256,2048]{1,0:T(8,128)(2,1)} %refs_2_.1) | copy-start | bytes 3145732
  345.5 4.6 collective-permute-start.5
  345.6 7.5 collective-permute-start.4
  346.1 10.0 %collective-permute-start.3 = (bf16[512,2048]{1,0:T(8,128)(2,1)}, bf16[512,2048]{1,0:T(8,128)(2,1)}, u32[]{:S(2)}, u32[]{:S(2)}) collective-permute-start(bf16[512,2048]{1,0:T(8,128)(2,1)} %collective-permute-done.refs_5_), channel_id=1, source_target_pairs={{0,1},{1,0},{2,3},{3,2},{4,5},{5,4},{6,7},{7,6},{8,9},{9,8},{10,11... | collective-permute-start | bytes 6291464 | tf_op jit(solution)/shard_map/ppermute | solution.py:32
  625.8 5.3 copy-start.19
  627.0 314.1 %collective-permute-start.6 = (f32[16]{0:T(128)S(1)}, f32[16]{0:T(128)S(1)}, u32[]{:S(2)}, u32[]{:S(2)}) collective-permute-start(f32[16]{0:T(128)S(1)} %add_reduce_fusion), channel_id=1, source_target_pairs={{0,1},{1,0},{2,3},{3,2},{4,5},{5,4},{6,7},{7,6},{8,9},{9,8},{10,11... | collective-permute-start | bytes 200 | tf_op jit(solution)/shard_map/ppermute | solution.py:32
  627.3 3.9 copy-start.5
  627.3 3.9 copy-start.13
  633.3 6.1 copy-start.12
  751.4 193.3 %copy-start.25 = (f32[16]{0:T(128)S(1)}, f32[16]{0:T(128)}, u32[]{:S(2)}) copy-start(f32[16]{0:T(128)} %param.28) | copy-start | bytes 196
  751.4 193.4 %copy-start.16 = (bf16[64,2048]{1,0:T(8,128)(2,1)S(1)}, bf16[64,2048]{1,0:T(8,128)(2,1)}, u32[]{:S(2)}) copy-start(bf16[64,2048]{1,0:T(8,128)(2,1)} %param.17) | copy-start | bytes 786436
  751.4 193.4 %copy-start.17 = (bf16[64,2048]{1,0:T(8,128)(2,1)S(1)}, bf16[64,2048]{1,0:T(8,128)(2,1)}, u32[]{:S(2)}) copy-start(bf16[64,2048]{1,0:T(8,128)(2,1)} %param.16) | copy-start | bytes 786436
  941.2 3.5 collective-permute-start.7
  (15 other events, 40.3 us)
Sparse Core Ops, SparseCore 0:
  203.3 145.8 all-gather.2
  623.2 171.4 reduce-scatter.1
